TPU v7x, 512 devices: a whole 4x8x8 slice. The times are simulated.
512 devices in a mesh: lam: 32 (over y, x), dom: 16 (over z, core).
Axes of the slice: x: 4, y: 8, z: 8, core: 2. Of those that a mesh axis runs over, the one named last changes fastest.
Arguments:
- cells: int32 [32, 3, 16384], P('lam', None, 'dom'), may hold values from 0 to 127, as said below
- offsets: float32 [32, 3, 16384], P('lam', None, 'dom'), may hold values from 0 to 1
- velocities: float32 [32, 3, 16384], P('lam', None, 'dom'), may hold values from -6 to 6
- charges: float32 [16384], P('dom'), may hold values from -2.5 to 2.5, as said below
- coupling: float32 [16384], P('dom'), may hold values from 0 to 1
- inverse_mass: float32 [16384], P('dom'), may hold values from 0.1 to 1
- lambdas: float32 [32], P('lam'), may hold values from 0 to 0.9
- tile_lists: int32 [32, 128, 6], P('lam', 'dom'), may hold values from 0 to 15, as said below
- halo_lists: int32 [32, 32, 512], P('lam', 'dom'), may hold values from 0 to 1023, as said below
- accept_flags: int32 [2, 32], P(None, 'lam'), may hold values 0 or 1
Outputs:
- new_cells: int32 [32, 3, 16384], P('lam', None, 'dom')
- new_offsets: float32 [32, 3, 16384], P('lam', None, 'dom')
- new_velocities: float32 [32, 3, 16384], P('lam', None, 'dom')
Inputs may be any that keep to these rules, and one draw needn't show every extreme that they name: `cells`: for atom a of a window, with d = a // 1024 and c = (a % 1024) // 128: its first cell index lies in [d * 8, (d + 1) * 8) and its second in [c * 16, (c + 1) * 16). The third cell indices of all atoms of one window lie among 8 consecutive values, counted modulo 128 (a membrane slab). `charges`: every charge has a magnitude between 1.5 and 2.5, of either sign. `tile_lists`: row d * 8 + c of a window lists, in order: c; three different clusters among c - 2, c - 1, c + 1, c + 2 modulo 8; 8 + c // 2; 12 + c // 2. `halo_lists`: rows 2d and 2d + 1 hold indices within domain d. Entries c * 64 to (c + 1) * 64 - 1 of row 2d are the atoms of cluster c with the lowest first cell index, those of row 2d + 1 the others (ties by atom number); each of the domain's atoms stands once in the two rows.
All inputs are finite; a program needn't handle non-finite values. No bound on the sum of `accept_flags` on one device may be relied on, other than what follows from the above.
Results may differ from a plain program's by a relative error of at most 0.0003.
Values sent between devices are 32-bit elements; how exact they have to be, the bound alone decides.
No kernel may reach another device: no remote copies, remote signals or barrier semaphores. Data moves between devices by JAX's collectives and lax.ppermute only.
A program may use at most 64 MiB of HBM per device.

v0:
```python
import functools
import math

import jax
import jax.numpy as jnp
import ml_dtypes
import numpy as np
from jax import lax
from jax.experimental import pallas as pl
from jax.experimental.pallas import tpu as pltpu
from jax.sharding import PartitionSpec as P

K = 128
CLUSTER = 128
N_DOM = 16
A_DEV = 1024
CLUSTERS = 8
HALO = 512
MODES = 32
SLAB = 24
ROWS = N_DOM * SLAB

EWALD_BETA = 0.5
COULOMB = 20.0
LJ_DEPTH = 1.0
LJ_SIGMA_SQ = 0.49
SOFT_SCALE = 0.5
SOFT_FLOOR = 0.5
STEP_DT = 0.25

F32 = jnp.float32
BF16 = jnp.bfloat16
HIGHEST = lax.Precision.HIGHEST

TURN = 2.0**32
SPAN_SQ = 2.0**-50
SPAN = 2.0**-25

SCREEN = (
    -0.0818439527,
    0.648023047,
    -2.23331568,
    4.38709699,
    -5.37737017,
    4.16223694,
    -1.81397109,
    0.0540053844,
    0.5630337,
    -5.2346482e-05,
    0.282096019,
)


def real_basis(count):
    half = count // 2
    place = np.arange(count)
    rows = []
    for k in range(half + 1):
        scale = math.sqrt((1.0 if k in (0, half) else 2.0) / count)
        rows.append(scale * np.cos(2.0 * np.pi * (k * place % count) / count))
    for k in range(1, half):
        rows.append(math.sqrt(2.0 / count) * np.sin(2.0 * np.pi * (k * place % count) / count))
    return np.stack(rows)


def halves(table):
    high = table.astype(np.float32).astype(ml_dtypes.bfloat16)
    low = (table - high.astype(np.float64)).astype(np.float32).astype(ml_dtypes.bfloat16)
    return high, low


def basis_table():
    basis = real_basis(K)
    high, low = halves(basis)
    return np.concatenate([high, low, high.T, low.T], axis=0)


def slab_basis():
    basis = real_basis(MODES)
    order = [0, MODES // 2]
    for k in range(1, MODES // 2):
        order += [k, MODES // 2 + k]
    return basis[np.array(order)].astype(np.float32)


def spline_modulus(k):
    return (3.0 / (2.0 + np.cos(2.0 * np.pi * k / K))) ** 2


def slab_weights():
    k = np.arange(K // 2 + 1)
    delta = np.arange(-MODES // 2 + 1, MODES // 2 + 1)
    folded = np.where((k == 0) | (k == K // 2), 1.0, 2.0)
    own = folded * np.exp(-np.pi**2 * (k / K) ** 2 / EWALD_BETA**2) * spline_modulus(k)
    rows = []
    for j in range(MODES // 2 + 1):
        window = np.cos(2 * np.pi * k[:, None] * delta / K) * np.cos(2 * np.pi * j * delta / MODES)
        rows.append(own * window.sum(axis=1))
    return np.stack(rows).astype(np.float32)


def plane_gain():
    k = np.concatenate([np.arange(K // 2 + 1), np.arange(1, K // 2)])
    square = (k / K) ** 2
    factor = np.exp(-np.pi**2 * square / EWALD_BETA**2) * spline_modulus(k)
    return square.astype(np.float32), factor.astype(np.float32)


def split(x):
    high = x.astype(BF16)
    return high, (x - high.astype(F32)).astype(BF16)


def dot3(left, right, dims=(((1,), (0,)), ((), ()))):
    lh, ll = left
    rh, rl = right
    dot = functools.partial(lax.dot_general, dimension_numbers=dims, preferred_element_type=F32)
    return dot(lh, rh) + (dot(lh, rl) + dot(ll, rh))


def spline_set(u):
    v = 1.0 - u
    u2 = u * u
    u3 = u2 * u
    weights = (
        v * v * v / 6.0,
        (3.0 * u3 - 6.0 * u2 + 4.0) / 6.0,
        (-3.0 * u3 + 3.0 * u2 + 3.0 * u + 1.0) / 6.0,
        u3 / 6.0,
    )
    slopes = (-0.5 * v * v, 1.5 * u2 - 2.0 * u, -1.5 * u2 + u + 0.5, 0.5 * u2)
    return weights, slopes


def chosen(distance, rows):
    out = jnp.where(distance == 3, rows[3], 0.0)
    for k in (2, 1, 0):
        out = jnp.where(distance == k, rows[k], out)
    return out


def iota_rows(rows, columns):
    return lax.broadcasted_iota(jnp.int32, (rows, columns), 0)


def fixed_turns(x):
    t = x * (1.0 / K)
    f = t - jnp.floor(t + 0.5)
    return jnp.maximum(f, -0.5) * TURN


def pair_terms(own, other, floor_value):
    ax, ay, az, qa, wa = own
    bx, by, bz, qb, wb = other
    dx = (ax - bx).astype(F32)
    dy = (ay - by).astype(F32)
    dz = (az - bz).astype(F32)
    s = (dx * dx + dy * dy + dz * dz) * SPAN_SQ + floor_value
    w = lax.rsqrt(s)
    u = w * w
    screen = jnp.full_like(w, SCREEN[0])
    for c in SCREEN[1:]:
        screen = screen * w + c
    gauss = jnp.exp2(s * (-(EWALD_BETA**2) * math.log2(math.e)))
    a = LJ_SIGMA_SQ * u
    t = a * a * a
    g = u * ((qa * qb) * (gauss * screen) + (wa * wb) * (t * (t - 0.5)))
    return g * dx, g * dy, g * dz


def own_rows(data_ref, turns, start, rows=8):
    def spread(row):
        return jnp.broadcast_to(row, (rows, CLUSTER))

    columns = pl.ds(start, CLUSTER)
    xyz = [spread(turns[i : i + 1, columns].astype(jnp.int32)) for i in range(3)]
    q = spread(data_ref[3:4, columns] * (2.0 * COULOMB))
    w = spread(data_ref[4:5, columns] * (48.0 * LJ_DEPTH))
    return (*xyz, q, w)


def write_halo(data, lists_ref, low_ref, high_ref):
    lane = lax.broadcasted_iota(jnp.int32, (8, CLUSTER), 1)
    for row, out_ref in ((0, low_ref), (1, high_ref)):
        for k in range(HALO // CLUSTER):
            columns = slice(k * CLUSTER, (k + 1) * CLUSTER)
            index = jnp.broadcast_to(lists_ref[0, row : row + 1, columns] & (CLUSTER - 1), (8, CLUSTER))
            first = data[:, 2 * k * CLUSTER : (2 * k + 1) * CLUSTER]
            second = data[:, (2 * k + 1) * CLUSTER : (2 * k + 2) * CLUSTER]
            out_ref[:, columns] = jnp.where(
                lane < CLUSTER // 2,
                jnp.take_along_axis(first, index, axis=1, mode="promise_in_bounds"),
                jnp.take_along_axis(second, index, axis=1, mode="promise_in_bounds"),
            )


def spread_kernel(
    lam_ref, flag_ref, cells_ref, off_ref, vel_ref, charge_ref, coup_ref, mass_ref, lists_ref, slab_ref,
    out_ref, data_ref, move_ref, low_ref, high_ref, mixed_high, mixed_low,
):
    cells = cells_ref[0]
    off = off_ref[0]
    cells_f = cells.astype(F32)
    weight = 1.0 - lam_ref[0] * coup_ref[...]
    charge = charge_ref[...] * weight

    data_ref[0:3, :] = cells_f + off
    data_ref[3:4, :] = charge
    data_ref[4:5, :] = weight
    data_ref[5:6, :] = mass_ref[...]
    data_ref[6:8, :] = jnp.zeros((2, A_DEV), F32)
    write_halo(data_ref[...], lists_ref, low_ref, high_ref)

    move_ref[0:3, :] = off
    move_ref[3:6, :] = cells_f
    move_ref[6:7, :] = jnp.full((1, A_DEV), flag_ref[0, 0].astype(F32))
    move_ref[7:8, :] = jnp.full((1, A_DEV), flag_ref[1, 0].astype(F32))
    move_ref[8:11, :] = vel_ref[0]
    move_ref[11:16, :] = jnp.zeros((5, A_DEV), F32)

    weights, _ = spline_set(off)
    row = iota_rows(16, A_DEV)
    plane = jnp.where(row < 8, row, 8 + (row & 3))
    x_table = chosen(plane - (cells[0:1] & 7), [m[0:1] for m in weights]) * charge
    z_table = chosen((iota_rows(MODES, A_DEV) - cells[2:3]) & (MODES - 1), [m[2:3] for m in weights])
    z_modes = jnp.dot(slab_ref[...], z_table, precision=HIGHEST, preferred_element_type=F32)
    y_table = chosen((iota_rows(K, A_DEV) - cells[1:2]) & (K - 1), [m[1:2] for m in weights])

    near, far = x_table[0:8], x_table[8:16]
    upper = iota_rows(8, A_DEV) < 4
    for i in range(0, N_DOM, 2):
        pieces = []
        for k in (i, i + 1):
            first = jnp.broadcast_to(z_modes[2 * k : 2 * k + 1], (8, A_DEV))
            second = jnp.broadcast_to(z_modes[2 * k + 1 : 2 * k + 2], (8, A_DEV))
            pieces += [near * first, near * second, far * jnp.where(upper, first, second)]
        high, low = split(jnp.concatenate(pieces, axis=0))
        mixed_high[i * SLAB : (i + 2) * SLAB, :] = high
        mixed_low[i * SLAB : (i + 2) * SLAB, :] = low
    out_ref[...] = dot3((mixed_high[...], mixed_low[...]), split(y_table), (((1,), (1,)), ((), ())))


def mesh_kernel(grid_ref, gain_ref, basis_ref, out_ref, block):
    top = iota_rows(8, K) < 4
    for e in range(N_DOM):
        spill = grid_ref[((e - 1) % N_DOM) * SLAB + 16 : ((e - 1) % N_DOM) * SLAB + 24, :]
        turned = pltpu.roll(spill, 4, 0)
        block[8 * e : 8 * e + 8, :] = grid_ref[e * SLAB : e * SLAB + 8, :] + jnp.where(top, spill, 0.0)
        block[K + 8 * e : K + 8 * e + 8, :] = grid_ref[e * SLAB + 8 : e * SLAB + 16, :] + jnp.where(top, turned, 0.0)
    basis = (basis_ref[0:K, :], basis_ref[K : 2 * K, :])
    turned_basis = (basis_ref[2 * K : 3 * K, :], basis_ref[3 * K : 4 * K, :])
    along_y = dot3(split(block[...]), turned_basis)
    for mode in range(2):
        part = split(along_y[mode * K : (mode + 1) * K])
        scaled = dot3(basis, part) * gain_ref[mode]
        block[mode * K : (mode + 1) * K, :] = dot3(turned_basis, split(scaled))
    block[...] = dot3(split(block[...]), basis)
    for e in range(N_DOM):
        following = 8 * ((e + 1) % N_DOM)
        out_ref[e * SLAB : e * SLAB + 8, :] = block[8 * e : 8 * e + 8, :]
        out_ref[e * SLAB + 8 : e * SLAB + 16, :] = block[K + 8 * e : K + 8 * e + 8, :]
        out_ref[e * SLAB + 16 : e * SLAB + 24, :] = jnp.where(
            top,
            block[following : following + 8, :],
            pltpu.roll(block[K + following : K + following + 8, :], 4, 0),
        )


def write_gain(mode_weights_ref, rows_ref, lanes_ref, gain_ref):
    dom = lax.axis_index("dom")
    square_y, factor_y = lanes_ref[0:1, :], lanes_ref[1:2, :]
    scale = COULOMB / (math.pi * K)
    first = dom
    second = jnp.where(dom == 0, MODES // 2, dom)

    def totals(square):
        one = jnp.zeros_like(square)
        two = jnp.zeros_like(square)
        for k in range(K // 2 + 1):
            whole = square + (k / K) ** 2
            inverse = 1.0 / whole if k else jnp.where(whole > 0.0, 1.0 / jnp.where(whole > 0.0, whole, 1.0), 0.0)
            one = one + inverse * mode_weights_ref[first, k]
            two = two + inverse * mode_weights_ref[second, k]
        return one, two

    def block(start):
        rows = pl.ds(start, 8)
        square = jnp.broadcast_to(rows_ref[rows, 0:1], (8, K)) + square_y
        factor = jnp.broadcast_to(rows_ref[rows, 1:2], (8, K)) * factor_y * scale
        one, two = totals(square)
        return one * factor, two * factor

    def step(b, carry):
        start = pl.multiple_of(b * 8, 8)
        one, two = block(start)
        gain_ref[0, pl.ds(start, 8), :] = one
        gain_ref[1, pl.ds(start, 8), :] = two
        gain_ref[0, pl.ds(start + K // 2, 8), :] = one
        gain_ref[1, pl.ds(start + K // 2, 8), :] = two
        return carry

    lax.fori_loop(0, 8, step, 0)
    one, two = block(K // 2)
    gain_ref[0, K // 2 : K // 2 + 1, :] = one[0:1]
    gain_ref[1, K // 2 : K // 2 + 1, :] = two[0:1]


def own_forces(lam_ref, tiles_ref, data_ref, force_ref, turns, columns):
    turns[...] = fixed_turns(data_ref[0:3, :])
    force_ref[...] = jnp.zeros_like(force_ref)

    def prepare(c, carry):
        start = pl.multiple_of(c * CLUSTER, CLUSTER)
        lanes = pl.ds(start, CLUSTER)
        stack = jnp.concatenate([turns[:, lanes], data_ref[3:8, lanes]], axis=0)
        turned = stack.T
        for i in range(5):
            columns[i, lanes, :] = jnp.broadcast_to(turned[:, i : i + 1], (CLUSTER, CLUSTER))
        return carry

    lax.fori_loop(0, CLUSTERS, prepare, 0)
    floor_value = SOFT_FLOOR + SOFT_SCALE * lam_ref[0]

    def one_cluster(c, carry):
        start = pl.multiple_of(c * CLUSTER, CLUSTER)
        own = own_rows(data_ref, turns, start)
        total = [jnp.zeros((8, CLUSTER), F32) for _ in range(3)]
        for slot in range(4):
            base = c if slot == 0 else tiles_ref[c, slot]
            for chunk in range(CLUSTER // 8):
                rows = pl.ds(pl.multiple_of(base * CLUSTER + chunk * 8, 8), 8)
                other = [columns[i, rows, :] for i in range(5)]
                other[:3] = [x.astype(jnp.int32) for x in other[:3]]
                terms = pair_terms(own, other, floor_value)
                total = [a + b for a, b in zip(total, terms)]
        for i in range(3):
            force_ref[i : i + 1, pl.ds(start, CLUSTER)] = SPAN * jnp.sum(total[i], axis=0, keepdims=True)
        return carry

    lax.fori_loop(0, CLUSTERS, one_cluster, 0)


def own_kernel(lam_ref, tiles_ref, data_ref, force_ref, turns, columns):
    own_forces(lam_ref, tiles_ref, data_ref, force_ref, turns, columns)


def own_gain_kernel(
    lam_ref, tiles_ref, weights_ref, data_ref, rows_ref, lanes_ref, force_ref, gain_ref, turns, columns
):
    write_gain(weights_ref, rows_ref, lanes_ref, gain_ref)
    own_forces(lam_ref, tiles_ref, data_ref, force_ref, turns, columns)


def add_halo_forces(lam_ref, data_ref, below_ref, above_ref, partial_ref, force_ref, turns):
    turns[...] = fixed_turns(data_ref[0:3, :])
    floor_value = SOFT_FLOOR + SOFT_SCALE * lam_ref[0]

    def one_pair(k, carry):
        start = pl.multiple_of(k * CLUSTER, CLUSTER)
        starts = [pl.multiple_of(k * (2 * CLUSTER), CLUSTER), pl.multiple_of(k * (2 * CLUSTER) + CLUSTER, CLUSTER)]
        owns = [own_rows(data_ref, turns, s) for s in starts]
        totals = [[jnp.zeros((8, CLUSTER), F32) for _ in range(3)] for _ in range(2)]
        for source in (below_ref, above_ref):
            block = source[:, pl.ds(start, CLUSTER)]
            stack = jnp.where(iota_rows(8, CLUSTER) < 3, fixed_turns(block), block)
            turned = stack.T
            for chunk in range(CLUSTER // 8):
                part = turned[chunk * 8 : chunk * 8 + 8]
                other = [jnp.broadcast_to(part[:, i : i + 1], (8, CLUSTER)) for i in range(5)]
                other[:3] = [x.astype(jnp.int32) for x in other[:3]]
                for j in range(2):
                    terms = pair_terms(owns[j], other, floor_value)
                    totals[j] = [a + b for a, b in zip(totals[j], terms)]
        for j in range(2):
            lanes = pl.ds(starts[j], CLUSTER)
            for i in range(3):
                force_ref[i : i + 1, lanes] = partial_ref[i : i + 1, lanes] + SPAN * jnp.sum(
                    totals[j][i], axis=0, keepdims=True
                )
        return carry

    lax.fori_loop(0, HALO // CLUSTER, one_pair, 0)


def halo_kernel(lam_ref, data_ref, below_ref, above_ref, partial_ref, force_ref, turns):
    force_ref[...] = jnp.zeros_like(force_ref)
    add_halo_forces(lam_ref, data_ref, below_ref, above_ref, partial_ref, force_ref, turns)


def advance(force, kicks, data_ref, move_ref, lists_ref, data_out, move_out, low_ref, high_ref):
    mass = data_ref[5:6, :]
    velocity = move_ref[8:11, :]
    for _ in range(kicks):
        velocity = velocity + 0.5 * STEP_DT * force * mass
    off = move_ref[0:3, :] + STEP_DT * velocity
    move_out[...] = move_ref[...]
    move_out[0:3, :] = off
    move_out[8:11, :] = velocity
    data_out[...] = data_ref[...]
    data_out[0:3, :] = move_ref[3:6, :] + off
    write_halo(data_out[...], lists_ref, low_ref, high_ref)


def gather_kernel(
    pot_ref, data_ref, move_ref, short_ref, lists_ref, slab_ref,
    long_ref, data_out, move_out, low_ref, high_ref, force,
):
    off = move_ref[0:3, :]
    cells = move_ref[3:6, :].astype(jnp.int32)
    charge = data_ref[3:4, :]
    weights, slopes = spline_set(off)
    row = iota_rows(16, A_DEV)
    reach = jnp.where(row < 8, row, 8 + (row & 3)) - (cells[0:1] & 7)
    x_table = chosen(reach, [m[0:1] for m in weights])
    x_slope = chosen(reach, [m[0:1] for m in slopes])
    reach = (iota_rows(MODES, A_DEV) - cells[2:3]) & (MODES - 1)
    z_table = chosen(reach, [m[2:3] for m in weights])
    z_slope = chosen(reach, [m[2:3] for m in slopes])
    z_modes = jnp.dot(slab_ref[...], z_table, precision=HIGHEST, preferred_element_type=F32)
    z_tilts = jnp.dot(slab_ref[...], z_slope, precision=HIGHEST, preferred_element_type=F32)
    potential = split(pot_ref[...])
    upper = iota_rows(8, CLUSTER) < 4
    for c in range(CLUSTERS):
        lanes = slice(c * CLUSTER, (c + 1) * CLUSTER)
        reach = (iota_rows(K, CLUSTER) - cells[1:2, lanes]) & (K - 1)
        y_both = jnp.concatenate(
            [chosen(reach, [m[1:2, lanes] for m in weights]), chosen(reach, [m[1:2, lanes] for m in slopes])], axis=1
        )
        along = dot3(potential, split(y_both))
        value, tilt = along[:, :CLUSTER], along[:, CLUSTER:]
        sums = [[jnp.zeros((8, CLUSTER), F32) for _ in range(2)] for _ in range(3)]
        for i in range(N_DOM):
            pairs = []
            for table in (z_modes, z_tilts):
                first = jnp.broadcast_to(table[2 * i : 2 * i + 1, lanes], (8, CLUSTER))
                second = jnp.broadcast_to(table[2 * i + 1 : 2 * i + 2, lanes], (8, CLUSTER))
                pairs.append((first, second, jnp.where(upper, first, second)))
            for which, (source, table) in enumerate(((value, 0), (tilt, 0), (value, 1))):
                block = source[i * SLAB : (i + 1) * SLAB]
                first, second, mixed = pairs[table]
                sums[which][0] = sums[which][0] + (first * block[0:8] + second * block[8:16])
                sums[which][1] = sums[which][1] + mixed * block[16:24]
        for i in range(3):
            table = x_slope if i == 0 else x_table
            near = table[0:8, lanes] * sums[i][0] + table[8:16, lanes] * sums[i][1]
            force[i : i + 1, lanes] = -charge[:, lanes] * jnp.sum(near, axis=0, keepdims=True)
    long_ref[...] = jnp.zeros_like(long_ref)
    long_ref[0:3, :] = force[0:3, :]
    advance(
        short_ref[0:3, :] + force[0:3, :], 1, data_ref, move_ref, lists_ref, data_out, move_out, low_ref, high_ref
    )


def halo_step_kernel(
    lam_ref, data_ref, below_ref, above_ref, partial_ref, long_ref, move_ref, lists_ref,
    data_out, move_out, low_ref, high_ref, turns, force,
):
    add_halo_forces(lam_ref, data_ref, below_ref, above_ref, partial_ref, force, turns)
    total = force[0:3, :] + long_ref[0:3, :]
    advance(total, 2, data_ref, move_ref, lists_ref, data_out, move_out, low_ref, high_ref)


def halo_last_kernel(
    lam_ref, data_ref, below_ref, above_ref, partial_ref, long_ref, move_ref, move_out, turns, force
):
    add_halo_forces(lam_ref, data_ref, below_ref, above_ref, partial_ref, force, turns)
    total = force[0:3, :] + long_ref[0:3, :]
    move_out[...] = move_ref[...]
    move_out[8:11, :] = move_ref[8:11, :] + 0.5 * STEP_DT * total * data_ref[5:6, :]


def swap_flag(round_index, here_ref, there_ref):
    window = lax.axis_index("lam")
    windows = lax.axis_size("lam")
    row = 6 + round_index
    lower = jnp.logical_and(window % 2 == round_index % 2, window + 1 < windows)
    upper = jnp.logical_and(window % 2 != round_index % 2, window >= 1)
    here = jnp.where(lower, here_ref[row : row + 1, :], 0.0)
    there = jnp.where(upper, there_ref[row : row + 1, :], 0.0)
    return (here + there) == 1.0


def first_swap_kernel(here_ref, there_ref, out_ref):
    take = swap_flag(0, here_ref, there_ref)
    out_ref[0:6, :] = jnp.where(take, there_ref[0:6, :], here_ref[0:6, :])
    out_ref[6:8, :] = here_ref[6:8, :]
    out_ref[8:16, :] = jnp.where(take, there_ref[8:16, :], here_ref[8:16, :])


def last_swap_kernel(here_ref, there_ref, cells_ref, off_ref, vel_ref):
    take = swap_flag(1, here_ref, there_ref)
    state = jnp.where(take, there_ref[...], here_ref[...])
    off_ref[0] = state[0:3]
    cells_ref[0] = state[3:6].astype(jnp.int32)
    vel_ref[0] = state[8:11]


SMEM = pl.BlockSpec(memory_space=pltpu.SMEM)
VMEM = pl.BlockSpec(memory_space=pltpu.VMEM)


def call(kernel, ins, outs, scratch=(), cost=0):
    return pl.pallas_call(
        kernel,
        out_shape=[jax.ShapeDtypeStruct(shape, dtype) for shape, dtype in outs],
        in_specs=[SMEM if place == "s" else VMEM for place, _ in ins],
        out_specs=[VMEM] * len(outs),
        scratch_shapes=list(scratch),
        compiler_params=pltpu.CompilerParams(vmem_limit_bytes=40 * 2**20),
        cost_estimate=pl.CostEstimate(flops=cost, bytes_accessed=200000, transcendentals=0),
    )(*[value for _, value in ins])


def passed_along(value, axis, by):
    size = lax.axis_size(axis)
    return lax.ppermute(value, axis, [(i, (i + by) % size) for i in range(size)])


def traded(value, round_index):
    windows = lax.axis_size("lam")
    pairs = []
    for w in range(round_index % 2, windows - 1, 2):
        pairs += [(w, w + 1), (w + 1, w)]
    return lax.ppermute(value, "lam", pairs)


def exchanged(value):
    return lax.all_to_all(value, "dom", split_axis=0, concat_axis=0, tiled=True)


def body(
    cells, offsets, velocities, charges, coupling, inverse_mass, lambdas, tile_lists, halo_lists, accept_flags
):
    wide = ((8, A_DEV), F32)
    state = ((16, A_DEV), F32)
    border = ((8, HALO), F32)
    turns = pltpu.VMEM((3, A_DEV), F32)
    columns = pltpu.VMEM((5, A_DEV, CLUSTER), F32)
    tiles = tile_lists[0]
    slab = jnp.asarray(slab_basis())
    square, factor = plane_gain()
    gain_rows = np.zeros((K, 8), np.float32)
    gain_rows[:, 0], gain_rows[:, 1] = square, factor
    gain_lanes = np.zeros((8, K), np.float32)
    gain_lanes[0], gain_lanes[1] = square, factor

    grid, data, move, low, high = call(
        spread_kernel,
        [
            ("s", lambdas), ("s", accept_flags), ("v", cells), ("v", offsets), ("v", velocities),
            ("v", charges[None]), ("v", coupling[None]), ("v", inverse_mass[None]), ("v", halo_lists), ("v", slab),
        ],
        [((ROWS, K), F32), wide, state, border, border],
        [pltpu.VMEM((ROWS, A_DEV), BF16), pltpu.VMEM((ROWS, A_DEV), BF16)],
    )
    grid = exchanged(grid)
    below, above = passed_along(high, "dom", 1), passed_along(low, "dom", -1)
    short, gain = call(
        own_gain_kernel,
        [
            ("s", lambdas), ("s", tiles), ("s", jnp.asarray(slab_weights())), ("v", data),
            ("v", jnp.asarray(gain_rows)), ("v", jnp.asarray(gain_lanes)),
        ],
        [wide, ((2, K, K), F32)],
        [turns, columns],
        cost=2 * 10**9,
    )
    (potential,) = call(
        mesh_kernel,
        [("v", grid), ("v", gain), ("v", jnp.asarray(basis_table()))],
        [((ROWS, K), F32)],
        [pltpu.VMEM((2 * K, K), F32)],
    )
    potential = exchanged(potential)
    (short,) = call(
        halo_kernel,
        [("s", lambdas), ("v", data), ("v", below), ("v", above), ("v", short)],
        [wide],
        [turns],
        cost=10**9,
    )
    far, data, move, low, high = call(
        gather_kernel,
        [("v", potential), ("v", data), ("v", move), ("v", short), ("v", halo_lists), ("v", slab)],
        [wide, wide, state, border, border],
        [pltpu.VMEM((8, A_DEV), F32)],
    )

    def own_call(data):
        (partial,) = call(
            own_kernel, [("s", lambdas), ("s", tiles), ("v", data)], [wide], [turns, columns], cost=2 * 10**9
        )
        return partial

    below, above = passed_along(high, "dom", 1), passed_along(low, "dom", -1)
    short = own_call(data)
    data, move, low, high = call(
        halo_step_kernel,
        [
            ("s", lambdas), ("v", data), ("v", below), ("v", above), ("v", short), ("v", far), ("v", move),
            ("v", halo_lists),
        ],
        [wide, state, border, border],
        [turns, pltpu.VMEM((8, A_DEV), F32)],
    )
    below, above = passed_along(high, "dom", 1), passed_along(low, "dom", -1)
    short = own_call(data)
    (move,) = call(
        halo_last_kernel,
        [("s", lambdas), ("v", data), ("v", below), ("v", above), ("v", short), ("v", far), ("v", move)],
        [state],
        [turns, pltpu.VMEM((8, A_DEV), F32)],
    )
    (move,) = call(first_swap_kernel, [("v", move), ("v", traded(move, 0))], [state])
    triple = (1, 3, A_DEV)
    return tuple(
        call(
            last_swap_kernel,
            [("v", move), ("v", traded(move, 1))],
            [(triple, jnp.int32), (triple, F32), (triple, F32)],
        )
    )


def solution(mesh):
    in_specs = (
        P("lam", None, "dom"),
        P("lam", None, "dom"),
        P("lam", None, "dom"),
        P("dom"),
        P("dom"),
        P("dom"),
        P("lam"),
        P("lam", "dom", None),
        P("lam", "dom", None),
        P(None, "lam"),
    )
    out_specs = (P("lam", None, "dom"), P("lam", None, "dom"), P("lam", None, "dom"))
    return jax.shard_map(body, mesh=mesh, in_specs=in_specs, out_specs=out_specs, check_vma=False)
```

profile of v0, /device:TPU:32, one launch (start us, length us, event | category | flops | bytes accessed | tf_op | source)
XLA Modules:
  0.0 90.7 jit_solution(1647213061112975586)
XLA Ops:
  1.3 0.7 copy.19.cells_ref
  2.0 0.7 copy-done.10
  2.8 0.1 copy.18.flag_ref
  2.9 0.6 copy-done.1
  3.5 2.4 %shard_map.166 = (f32[384,128]{1,0:T(8,128)}, f32[8,1024]{1,0:T(8,128)S(1)}, f32[16,1024]{1,0:T(8,128)S(1)}, f32[8,512]{1,0:T(8,128)S(1)}, f32[8,512]{1,0:T(8,128)S(1)}) custom-call(f32[1]{0:T(128)S(6)} %copy.26.lam_ref, s32[2,1]{1,0:T(2,128)S(1)} %copy.18.flag_ref, s32[1,3,1024]{2,1,0:T(4,128)S(1)} %copy.19.cells_ref, f32[1,3,1024]{2,1,0:T(4,128)S(1)} %copy.20.off_ref, ...), custom_call_target="tpu_custom_call" | custom-call | bytes 200000 | tf_op jit(solution)/shard_map/pallas_call | solution.py:503
  5.9 10.6 %all-to-all-start = ((f32[16,24,128]{2,1,0:T(8,128)}), f32[16,24,128]{2,1,0:T(8,128)S(1)}, u32[]{:S(2)}, u32[]{:S(2)}) async-start(f32[16,24,128]{2,1,0:T(8,128)} %bitcast.3), calls=%async_computation | async-start | bytes 393216 | tf_op jit(solution)/shard_map/all_to_all | solution.py:528
  16.4 0.1 copy.22
  16.5 0.6 copy-done.8
  17.1 8.9 %shard_map.167 = (f32[8,1024]{1,0:T(8,128)S(1)}, f32[2,128,128]{2,1,0:T(8,128)S(1)}) custom-call(f32[1]{0:T(128)S(6)} %copy.26.lam_ref, s32[8,6]{1,0:T(8,128)S(1)} %bitcast.10, f32[17,65]{1,0:T(8,128)S(1)} %copy-done.7, f32[8,1024]{1,0:T(8,128)S(1)} %get-tuple-element.20.data_ref, f32[128,8]{1,0:T(8,128)S(1)} %copy-done.6, f32[8,128]{1,0:T(8,128)S(1)} %copy-done.8), custom_call_target="tpu_custom_call" | custom-call | flops 2000000000 | bytes 200000 | tf_op jit(solution)/shard_map/pallas_call | solution.py:503
  26.1 0.3 all-to-all-done
  26.4 1.5 %shard_map.168 = f32[384,128]{1,0:T(8,128)} custom-call(f32[384,128]{1,0:T(8,128)S(1)} %bitcast.9, f32[2,128,128]{2,1,0:T(8,128)S(1)} %get-tuple-element.21.gain_ref, bf16[512,128]{1,0:T(8,128)(2,1)S(1)} %copy-done), custom_call_target="tpu_custom_call" | custom-call | bytes 200000 | tf_op jit(solution)/shard_map/pallas_call | solution.py:503
  27.8 6.9 %all-to-all-start.1 = ((f32[16,24,128]{2,1,0:T(8,128)}), f32[16,24,128]{2,1,0:T(8,128)S(1)}, u32[]{:S(2)}, u32[]{:S(2)}) async-start(f32[16,24,128]{2,1,0:T(8,128)} %bitcast.6), calls=%async_computation.1 | async-start | bytes 393216 | tf_op jit(solution)/shard_map/all_to_all | solution.py:528
  34.8 0.4 collective-permute-start
  35.2 2.6 %collective-permute-start.1 = (f32[8,512]{1,0:T(8,128)S(1)}, f32[8,512]{1,0:T(8,128)S(1)}, u32[]{:S(2)}, u32[]{:S(2)}) collective-permute-start(f32[8,512]{1,0:T(8,128)S(1)} %get-tuple-element.24), channel_id=1, source_target_pairs={{0,15},{1,0},{2,1},{3,2},{4,3},{5,4},{6,5},{7,6},{8,7},{9,8},{10,9... | collective-permute-start | bytes 49160 | tf_op jit(solution)/shard_map/ppermute | solution.py:516
  37.7 4.4 %collective-permute-done.below_ref = f32[8,512]{1,0:T(8,128)S(1)} collective-permute-done((f32[8,512]{1,0:T(8,128)S(1)}, f32[8,512]{1,0:T(8,128)S(1)}, u32[]{:S(2)}, u32[]{:S(2)}) %collective-permute-start) | collective-permute-done | bytes 16416 | tf_op jit(solution)/shard_map/ppermute | solution.py:516
  42.1 2.8 %shard_map.169.short_ref = f32[8,1024]{1,0:T(8,128)S(1)} custom-call(f32[1]{0:T(128)S(6)} %copy.26.lam_ref, f32[8,1024]{1,0:T(8,128)S(1)} %get-tuple-element.20.data_ref, f32[8,512]{1,0:T(8,128)S(1)} %collective-permute-done.below_ref, f32[8,512]{1,0:T(8,128)S(1)} %collective-permute-done.1.above_ref, f32[8,1024]{1,0:T(8,128)S(1)} %get-tuple-element.25.partial_ref), custom_call_target="tpu_custom_call" | custom-call | flops 1000000000 | bytes 200000 | tf_op jit(solution)/shard_map/pallas_call | solution.py:503
  44.9 1.8 %shard_map.170 = (f32[8,1024]{1,0:T(8,128)S(1)}, f32[8,1024]{1,0:T(8,128)S(1)}, f32[16,1024]{1,0:T(8,128)S(1)}, f32[8,512]{1,0:T(8,128)S(1)}, f32[8,512]{1,0:T(8,128)S(1)}) custom-call(f32[384,128]{1,0:T(8,128)S(1)} %bitcast.8, f32[8,1024]{1,0:T(8,128)S(1)} %get-tuple-element.20.data_ref, f32[16,1024]{1,0:T(8,128)S(1)} %get-tuple-element.22.move_ref, ...), custom_call_target="tpu_custom_call" | custom-call | bytes 200000 | tf_op jit(solution)/shard_map/pallas_call | solution.py:503
  46.7 1.0 %collective-permute-start.2 = (f32[8,512]{1,0:T(8,128)S(1)}, f32[8,512]{1,0:T(8,128)S(1)}, u32[]{:S(2)}, u32[]{:S(2)}) collective-permute-start(f32[8,512]{1,0:T(8,128)S(1)} %get-tuple-element.27), channel_id=1, source_target_pairs={{0,1},{1,2},{2,3},{3,4},{4,5},{5,6},{6,7},{7,8},{8,9},{9,10},{10,1... | collective-permute-start | bytes 49160 | tf_op jit(solution)/shard_map/ppermute | solution.py:516
  47.6 2.0 %collective-permute-start.3 = (f32[8,512]{1,0:T(8,128)S(1)}, f32[8,512]{1,0:T(8,128)S(1)}, u32[]{:S(2)}, u32[]{:S(2)}) collective-permute-start(f32[8,512]{1,0:T(8,128)S(1)} %get-tuple-element.28), channel_id=1, source_target_pairs={{0,15},{1,0},{2,1},{3,2},{4,3},{5,4},{6,5},{7,6},{8,7},{9,8},{10,9... | collective-permute-start | bytes 49160 | tf_op jit(solution)/shard_map/ppermute | solution.py:516
  49.6 7.4 %shard_map.171.partial_ref = f32[8,1024]{1,0:T(8,128)S(1)} custom-call(f32[1]{0:T(128)S(6)} %copy.26.lam_ref, s32[8,6]{1,0:T(8,128)S(1)} %bitcast.11, f32[8,1024]{1,0:T(8,128)S(1)} %get-tuple-element.26.data_ref), custom_call_target="tpu_custom_call" | custom-call | flops 2000000000 | bytes 200000 | tf_op jit(solution)/shard_map/pallas_call | solution.py:503
  57.1 2.9 %shard_map.172 = (f32[8,1024]{1,0:T(8,128)S(1)}, f32[16,1024]{1,0:T(8,128)S(1)}, f32[8,512]{1,0:T(8,128)S(1)}, f32[8,512]{1,0:T(8,128)S(1)}) custom-call(f32[1]{0:T(128)S(6)} %copy.26.lam_ref, f32[8,1024]{1,0:T(8,128)S(1)} %get-tuple-element.26.data_ref, f32[8,512]{1,0:T(8,128)S(1)} %collective-permute-done.2.below_ref, ...), custom_call_target="tpu_custom_call" | custom-call | bytes 200000 | tf_op jit(solution)/shard_map/pallas_call | solution.py:503
  59.9 0.0 collective-permute-start.4
  60.0 2.9 %collective-permute-start.5 = (f32[8,512]{1,0:T(8,128)S(1)}, f32[8,512]{1,0:T(8,128)S(1)}, u32[]{:S(2)}, u32[]{:S(2)}) collective-permute-start(f32[8,512]{1,0:T(8,128)S(1)} %get-tuple-element.33), channel_id=1, source_target_pairs={{0,15},{1,0},{2,1},{3,2},{4,3},{5,4},{6,5},{7,6},{8,7},{9,8},{10,9... | collective-permute-start | bytes 49160 | tf_op jit(solution)/shard_map/ppermute | solution.py:516
  62.9 7.4 %shard_map.173.partial_ref = f32[8,1024]{1,0:T(8,128)S(1)} custom-call(f32[1]{0:T(128)S(6)} %copy.26.lam_ref, s32[8,6]{1,0:T(8,128)S(1)} %bitcast.12, f32[8,1024]{1,0:T(8,128)S(1)} %get-tuple-element.31.data_ref), custom_call_target="tpu_custom_call" | custom-call | flops 2000000000 | bytes 200000 | tf_op jit(solution)/shard_map/pallas_call | solution.py:503
  70.3 2.8 %shard_map.174.here_ref = f32[16,1024]{1,0:T(8,128)S(1)} custom-call(f32[1]{0:T(128)S(6)} %copy.26.lam_ref, f32[8,1024]{1,0:T(8,128)S(1)} %get-tuple-element.31.data_ref, f32[8,512]{1,0:T(8,128)S(1)} %collective-permute-done.4.below_ref, f32[8,512]{1,0:T(8,128)S(1)} %collective-permute-done.5.above_ref, f32[8,1024]{1,0:T(8,128)S(1)} %shard_map.173.partial_ref, ...), custom_call_target="tpu_custom_call" | custom-call | bytes 200000 | tf_op jit(solution)/shard_map/pallas_call | solution.py:503
  73.1 3.4 %collective-permute-start.6 = (f32[16,1024]{1,0:T(8,128)S(1)}, f32[16,1024]{1,0:T(8,128)S(1)}, u32[]{:S(2)}, u32[]{:S(2)}) collective-permute-start(f32[16,1024]{1,0:T(8,128)S(1)} %shard_map.174.here_ref), channel_id=1, source_target_pairs={{0,16},{16,0},{32,48},{48,32},{64,80},{80,64},{96,112},{112,96},{1... | collective-permute-start | bytes 196616 | tf_op jit(solution)/shard_map/ppermute | solution.py:524
  76.5 2.8 %collective-permute-done.6.there_ref = f32[16,1024]{1,0:T(8,128)S(1)} collective-permute-done((f32[16,1024]{1,0:T(8,128)S(1)}, f32[16,1024]{1,0:T(8,128)S(1)}, u32[]{:S(2)}, u32[]{:S(2)}) %collective-permute-start.6) | collective-permute-done | bytes 65568 | tf_op jit(solution)/shard_map/ppermute | solution.py:524
  79.3 4.6 %collective-permute-start.7 = (f32[16,1024]{1,0:T(8,128)S(1)}, f32[16,1024]{1,0:T(8,128)S(1)}, u32[]{:S(2)}, u32[]{:S(2)}) collective-permute-start(f32[16,1024]{1,0:T(8,128)S(1)} %shard_map.175.here_ref), channel_id=1, source_target_pairs={{16,32},{32,16},{48,64},{64,48},{80,96},{96,80},{112,128},{128,112... | collective-permute-start | bytes 196616 | tf_op jit(solution)/shard_map/ppermute | solution.py:524
  83.9 4.9 %collective-permute-done.7.there_ref = f32[16,1024]{1,0:T(8,128)S(1)} collective-permute-done((f32[16,1024]{1,0:T(8,128)S(1)}, f32[16,1024]{1,0:T(8,128)S(1)}, u32[]{:S(2)}, u32[]{:S(2)}) %collective-permute-start.7) | collective-permute-done | bytes 65568 | tf_op jit(solution)/shard_map/ppermute | solution.py:524
  88.8 0.6 copy.23
  89.4 0.6 copy.24
  90.0 0.6 copy.25
  (33 shorter events, 0.1 us)
Async XLA Ops:
  1.3 0.7 copy-start.9
  2.0 0.7 copy-start.10
  2.0 0.7 copy-start.12
  2.7 0.7 copy-start.1
  2.7 0.7 copy-start.3
  2.7 0.7 copy-start.4
  2.7 0.7 copy-start.5
  2.8 0.7 copy-start.2
  5.9 10.6 %copy-start.11 = (s32[1,8,6]{1,0,2:T(1,128)S(1)}, s32[1,8,6]{1,0,2:T(1,128)}, u32[]{:S(2)}) copy-start(s32[1,8,6]{1,0,2:T(1,128)} %param.22) | copy-start | bytes 580
  5.9 10.7 %copy-start.6 = (f32[128,8]{1,0:T(8,128)S(1)}, f32[128,8]{1,0:T(8,128)}, u32[]{:S(2)}) copy-start(f32[128,8]{1,0:T(8,128)} %constant.12.clone.rows_ref) | copy-start | bytes 12292
  5.9 10.7 %copy-start.7 = (f32[17,65]{1,0:T(8,128)S(1)}, f32[17,65]{1,0:T(8,128)}, u32[]{:S(2)}) copy-start(f32[17,65]{1,0:T(8,128)} %constant.11.clone.weights_ref) | copy-start | bytes 13264
  5.9 20.5 %all-to-all-start = ((f32[16,24,128]{2,1,0:T(8,128)}), f32[16,24,128]{2,1,0:T(8,128)S(1)}, u32[]{:S(2)}, u32[]{:S(2)}) async-start(f32[16,24,128]{2,1,0:T(8,128)} %bitcast.3), calls=%async_computation | async-start | bytes 393216 | tf_op jit(solution)/shard_map/all_to_all | solution.py:528
  16.4 0.7 copy-start.8
  17.1 9.3 %copy-start = (bf16[512,128]{1,0:T(8,128)(2,1)S(1)}, bf16[512,128]{1,0:T(8,128)(2,1)}, u32[]{:S(2)}) copy-start(bf16[512,128]{1,0:T(8,128)(2,1)} %constant.14.clone.basis_ref) | copy-start | bytes 393220
  27.8 17.0 %all-to-all-start.1 = ((f32[16,24,128]{2,1,0:T(8,128)}), f32[16,24,128]{2,1,0:T(8,128)S(1)}, u32[]{:S(2)}, u32[]{:S(2)}) async-start(f32[16,24,128]{2,1,0:T(8,128)} %bitcast.6), calls=%async_computation.1 | async-start | bytes 393216 | tf_op jit(solution)/shard_map/all_to_all | solution.py:528
  34.8 7.3 %collective-permute-start = (f32[8,512]{1,0:T(8,128)S(1)}, f32[8,512]{1,0:T(8,128)S(1)}, u32[]{:S(2)}, u32[]{:S(2)}) collective-permute-start(f32[8,512]{1,0:T(8,128)S(1)} %get-tuple-element.23), channel_id=1, source_target_pairs={{0,1},{1,2},{2,3},{3,4},{4,5},{5,6},{6,7},{7,8},{8,9},{9,10},{10,1... | collective-permute-start | bytes 49160 | tf_op jit(solution)/shard_map/ppermute | solution.py:516
  35.2 6.9 %collective-permute-start.1 = (f32[8,512]{1,0:T(8,128)S(1)}, f32[8,512]{1,0:T(8,128)S(1)}, u32[]{:S(2)}, u32[]{:S(2)}) collective-permute-start(f32[8,512]{1,0:T(8,128)S(1)} %get-tuple-element.24), channel_id=1, source_target_pairs={{0,15},{1,0},{2,1},{3,2},{4,3},{5,4},{6,5},{7,6},{8,7},{9,8},{10,9... | collective-permute-start | bytes 49160 | tf_op jit(solution)/shard_map/ppermute | solution.py:516
  46.7 10.4 %collective-permute-start.2 = (f32[8,512]{1,0:T(8,128)S(1)}, f32[8,512]{1,0:T(8,128)S(1)}, u32[]{:S(2)}, u32[]{:S(2)}) collective-permute-start(f32[8,512]{1,0:T(8,128)S(1)} %get-tuple-element.27), channel_id=1, source_target_pairs={{0,1},{1,2},{2,3},{3,4},{4,5},{5,6},{6,7},{7,8},{8,9},{9,10},{10,1... | collective-permute-start | bytes 49160 | tf_op jit(solution)/shard_map/ppermute | solution.py:516
  47.6 9.4 %collective-permute-start.3 = (f32[8,512]{1,0:T(8,128)S(1)}, f32[8,512]{1,0:T(8,128)S(1)}, u32[]{:S(2)}, u32[]{:S(2)}) collective-permute-start(f32[8,512]{1,0:T(8,128)S(1)} %get-tuple-element.28), channel_id=1, source_target_pairs={{0,15},{1,0},{2,1},{3,2},{4,3},{5,4},{6,5},{7,6},{8,7},{9,8},{10,9... | collective-permute-start | bytes 49160 | tf_op jit(solution)/shard_map/ppermute | solution.py:516
  59.9 10.4 %collective-permute-start.4 = (f32[8,512]{1,0:T(8,128)S(1)}, f32[8,512]{1,0:T(8,128)S(1)}, u32[]{:S(2)}, u32[]{:S(2)}) collective-permute-start(f32[8,512]{1,0:T(8,128)S(1)} %get-tuple-element.32), channel_id=1, source_target_pairs={{0,1},{1,2},{2,3},{3,4},{4,5},{5,6},{6,7},{7,8},{8,9},{9,10},{10,1... | collective-permute-start | bytes 49160 | tf_op jit(solution)/shard_map/ppermute | solution.py:516
  60.0 10.4 %collective-permute-start.5 = (f32[8,512]{1,0:T(8,128)S(1)}, f32[8,512]{1,0:T(8,128)S(1)}, u32[]{:S(2)}, u32[]{:S(2)}) collective-permute-start(f32[8,512]{1,0:T(8,128)S(1)} %get-tuple-element.33), channel_id=1, source_target_pairs={{0,15},{1,0},{2,1},{3,2},{4,3},{5,4},{6,5},{7,6},{8,7},{9,8},{10,9... | collective-permute-start | bytes 49160 | tf_op jit(solution)/shard_map/ppermute | solution.py:516
  73.1 6.2 %collective-permute-start.6 = (f32[16,1024]{1,0:T(8,128)S(1)}, f32[16,1024]{1,0:T(8,128)S(1)}, u32[]{:S(2)}, u32[]{:S(2)}) collective-permute-start(f32[16,1024]{1,0:T(8,128)S(1)} %shard_map.174.here_ref), channel_id=1, source_target_pairs={{0,16},{16,0},{32,48},{48,32},{64,80},{80,64},{96,112},{112,96},{1... | collective-permute-start | bytes 196616 | tf_op jit(solution)/shard_map/ppermute | solution.py:524
  79.3 9.5 %collective-permute-start.7 = (f32[16,1024]{1,0:T(8,128)S(1)}, f32[16,1024]{1,0:T(8,128)S(1)}, u32[]{:S(2)}, u32[]{:S(2)}) collective-permute-start(f32[16,1024]{1,0:T(8,128)S(1)} %shard_map.175.here_ref), channel_id=1, source_target_pairs={{16,32},{32,16},{48,64},{64,48},{80,96},{96,80},{112,128},{128,112... | collective-permute-start | bytes 196616 | tf_op jit(solution)/shard_map/ppermute | solution.py:524
where the time goes:
time: 91.3 us; the launch traced here: 90.7 us
  Pallas kernels  37.8 us (41%)
  starting transfers between devices  34.3 us (38%)
  waiting for transfers between devices  12.4 us (14%)
  local copies, waits for them, and re-layouts  4.66 us (5%)
  between operations  1.48 us (2%)
    pallas_call x11, Pallas kernels, call(): pl.pallas_call(kernel, out_shape=[jax.ShapeDtypeStruct(shape, dtype) for...  37.8 us
    all_to_all x2, starting transfers between devices, exchanged(): return lax.all_to_all(value, 'dom', split_axis=0, concat_axis=0, tiled=True)  17.5 us
    ppermute x6, starting transfers between devices, passed_along(): lax.ppermute(value, axis, [(i, (i + by) % size) for i in range(size)])  8.9 us
    ppermute x2, starting transfers between devices, traded(): return lax.ppermute(value, 'lam', pairs)  7.95 us
    ppermute x2, waiting for transfers between devices, traded(): return lax.ppermute(value, 'lam', pairs)  7.67 us
    ppermute x6, waiting for transfers between devices, passed_along(): lax.ppermute(value, axis, [(i, (i + by) % size) for i in range(size)])  4.38 us
    unnamed x31, local copies, waits for them, and re-layouts  2.82 us
    pallas_call x3, local copies, waits for them, and re-layouts, call(): pl.pallas_call(kernel, out_shape=[jax.ShapeDtypeStruct(shape, dtype) for...  1.84 us
  transfers between devices with their start and end apart: 10, of which 4 were waited for; matrix products, arithmetic and copies ran while one was open for 0% of the time, Pallas kernels for 29%

commit v1 on v0

--- a/solution.py
+++ b/solution.py
@@ -179,12 +179,15 @@
     return (*xyz, q, w)
 
 
-def write_halo(data, lists_ref, low_ref, high_ref):
+def write_halo(data, lists_ref, inner_ref, outer_ref):
+    even = lax.axis_index("dom") % 2 == 0
     lane = lax.broadcasted_iota(jnp.int32, (8, CLUSTER), 1)
-    for row, out_ref in ((0, low_ref), (1, high_ref)):
+    for flip, out_ref in ((False, inner_ref), (True, outer_ref)):
         for k in range(HALO // CLUSTER):
             columns = slice(k * CLUSTER, (k + 1) * CLUSTER)
-            index = jnp.broadcast_to(lists_ref[0, row : row + 1, columns] & (CLUSTER - 1), (8, CLUSTER))
+            low, high = lists_ref[0, 0:1, columns], lists_ref[0, 1:2, columns]
+            row = jnp.where(even, low, high) if flip else jnp.where(even, high, low)
+            index = jnp.broadcast_to(row & (CLUSTER - 1), (8, CLUSTER))
             first = data[:, 2 * k * CLUSTER : (2 * k + 1) * CLUSTER]
             second = data[:, (2 * k + 1) * CLUSTER : (2 * k + 2) * CLUSTER]
             out_ref[:, columns] = jnp.where(
@@ -198,33 +201,33 @@
     lam_ref, flag_ref, cells_ref, off_ref, vel_ref, charge_ref, coup_ref, mass_ref, lists_ref, slab_ref,
     out_ref, data_ref, move_ref, low_ref, high_ref, mixed_high, mixed_low,
 ):
-    cells = cells_ref[0]
-    off = off_ref[0]
-    cells_f = cells.astype(F32)
     weight = 1.0 - lam_ref[0] * coup_ref[...]
     charge = charge_ref[...] * weight
 
-    data_ref[0:3, :] = cells_f + off
+    for i in range(3):
+        cell = cells_ref[i].astype(F32)
+        move_ref[i : i + 1, :] = off_ref[i]
+        move_ref[3 + i : 4 + i, :] = cell
+        move_ref[8 + i : 9 + i, :] = vel_ref[i]
+        data_ref[i : i + 1, :] = cell + off_ref[i]
+    move_ref[6:7, :] = jnp.full((1, A_DEV), flag_ref[0, 0].astype(F32))
+    move_ref[7:8, :] = jnp.full((1, A_DEV), flag_ref[0, 1].astype(F32))
+    move_ref[11:16, :] = jnp.zeros((5, A_DEV), F32)
     data_ref[3:4, :] = charge
     data_ref[4:5, :] = weight
     data_ref[5:6, :] = mass_ref[...]
     data_ref[6:8, :] = jnp.zeros((2, A_DEV), F32)
     write_halo(data_ref[...], lists_ref, low_ref, high_ref)
 
-    move_ref[0:3, :] = off
-    move_ref[3:6, :] = cells_f
-    move_ref[6:7, :] = jnp.full((1, A_DEV), flag_ref[0, 0].astype(F32))
-    move_ref[7:8, :] = jnp.full((1, A_DEV), flag_ref[1, 0].astype(F32))
-    move_ref[8:11, :] = vel_ref[0]
-    move_ref[11:16, :] = jnp.zeros((5, A_DEV), F32)
-
+    off = move_ref[0:3, :]
+    cells = [cells_ref[i] for i in range(3)]
     weights, _ = spline_set(off)
     row = iota_rows(16, A_DEV)
     plane = jnp.where(row < 8, row, 8 + (row & 3))
-    x_table = chosen(plane - (cells[0:1] & 7), [m[0:1] for m in weights]) * charge
-    z_table = chosen((iota_rows(MODES, A_DEV) - cells[2:3]) & (MODES - 1), [m[2:3] for m in weights])
+    x_table = chosen(plane - (cells[0] & 7), [m[0:1] for m in weights]) * charge
+    z_table = chosen((iota_rows(MODES, A_DEV) - cells[2]) & (MODES - 1), [m[2:3] for m in weights])
     z_modes = jnp.dot(slab_ref[...], z_table, precision=HIGHEST, preferred_element_type=F32)
-    y_table = chosen((iota_rows(K, A_DEV) - cells[1:2]) & (K - 1), [m[1:2] for m in weights])
+    y_table = chosen((iota_rows(K, A_DEV) - cells[1]) & (K - 1), [m[1:2] for m in weights])
 
     near, far = x_table[0:8], x_table[8:16]
     upper = iota_rows(8, A_DEV) < 4
@@ -240,7 +243,8 @@
     out_ref[...] = dot3((mixed_high[...], mixed_low[...]), split(y_table), (((1,), (1,)), ((), ())))
 
 
-def mesh_kernel(grid_ref, gain_ref, basis_ref, out_ref, block):
+def mesh_kernel(grid_ref, gain_ref, basis_ref, inner_ref, outer_ref, out_ref, block):
+    del inner_ref, outer_ref
     top = iota_rows(8, K) < 4
     for e in range(N_DOM):
         spill = grid_ref[((e - 1) % N_DOM) * SLAB + 16 : ((e - 1) % N_DOM) * SLAB + 24, :]
@@ -305,50 +309,67 @@
     gain_ref[1, K // 2 : K // 2 + 1, :] = two[0:1]
 
 
-def own_forces(lam_ref, tiles_ref, data_ref, force_ref, turns, columns):
+def listed(tiles_ref, row, cluster):
+    count = jnp.int32(0)
+    for slot in range(1, 4):
+        count = count + jnp.where(tiles_ref[slot, 0, row] == cluster, 1, 0)
+    return count.astype(F32)
+
+
+def own_forces(lam_ref, tiles_ref, data_ref, force_ref, turns, near, sides, first, last):
     turns[...] = fixed_turns(data_ref[0:3, :])
+    near[...] = jnp.zeros_like(near)
+    sides[...] = jnp.zeros_like(sides)
+    floor_value = SOFT_FLOOR + SOFT_SCALE * lam_ref[0]
+
+    def one_cluster(b, carry):
+        start = pl.multiple_of(b * CLUSTER, CLUSTER)
+        lanes = pl.ds(start, CLUSTER)
+        turned = jnp.concatenate([turns[:, lanes], data_ref[3:8, lanes]], axis=0).T
+        others = [b, (b + 1) % CLUSTERS, (b + 2) % CLUSTERS]
+        owns = [own_rows(data_ref, turns, pl.multiple_of(a * CLUSTER, CLUSTER)) for a in others]
+        totals = [[jnp.zeros((8, CLUSTER), F32) for _ in range(3)] for _ in others]
+        back = [None] + [listed(tiles_ref, b, a) for a in others[1:]]
+        for chunk in range(CLUSTER // 8):
+            part = turned[chunk * 8 : chunk * 8 + 8]
+            other = [jnp.broadcast_to(part[:, i : i + 1], (8, CLUSTER)) for i in range(5)]
+            other[:3] = [x.astype(jnp.int32) for x in other[:3]]
+            side = []
+            for j in range(3):
+                terms = pair_terms(owns[j], other, floor_value)
+                totals[j] = [p + q for p, q in zip(totals[j], terms)]
+                if j:
+                    side.append([back[j] * p for p in terms])
+            for i in range(3):
+                sides[pl.ds(start + chunk * 8, 8), i : i + 1] = jnp.sum(
+                    side[0][i] + side[1][i], axis=1, keepdims=True
+                )
+        for j, a in enumerate(others):
+            rows = pl.ds(pl.multiple_of(a * 8, 8), 8)
+            for i in range(3):
+                total = listed(tiles_ref, a, b) * totals[j][i] if j else totals[j][i]
+                near[i, rows, :] = near[i, rows, :] + total
+        return carry
+
+    lax.fori_loop(first, last, one_cluster, 0)
     force_ref[...] = jnp.zeros_like(force_ref)
-
-    def prepare(c, carry):
-        start = pl.multiple_of(c * CLUSTER, CLUSTER)
-        lanes = pl.ds(start, CLUSTER)
-        stack = jnp.concatenate([turns[:, lanes], data_ref[3:8, lanes]], axis=0)
-        turned = stack.T
-        for i in range(5):
-            columns[i, lanes, :] = jnp.broadcast_to(turned[:, i : i + 1], (CLUSTER, CLUSTER))
-        return carry
-
-    lax.fori_loop(0, CLUSTERS, prepare, 0)
-    floor_value = SOFT_FLOOR + SOFT_SCALE * lam_ref[0]
-
-    def one_cluster(c, carry):
-        start = pl.multiple_of(c * CLUSTER, CLUSTER)
-        own = own_rows(data_ref, turns, start)
-        total = [jnp.zeros((8, CLUSTER), F32) for _ in range(3)]
-        for slot in range(4):
-            base = c if slot == 0 else tiles_ref[c, slot]
-            for chunk in range(CLUSTER // 8):
-                rows = pl.ds(pl.multiple_of(base * CLUSTER + chunk * 8, 8), 8)
-                other = [columns[i, rows, :] for i in range(5)]
-                other[:3] = [x.astype(jnp.int32) for x in other[:3]]
-                terms = pair_terms(own, other, floor_value)
-                total = [a + b for a, b in zip(total, terms)]
+    for c in range(CLUSTERS):
+        lanes = slice(c * CLUSTER, (c + 1) * CLUSTER)
+        turned = sides[lanes, :].T
         for i in range(3):
-            force_ref[i : i + 1, pl.ds(start, CLUSTER)] = SPAN * jnp.sum(total[i], axis=0, keepdims=True)
-        return carry
-
-    lax.fori_loop(0, CLUSTERS, one_cluster, 0)
-
-
-def own_kernel(lam_ref, tiles_ref, data_ref, force_ref, turns, columns):
-    own_forces(lam_ref, tiles_ref, data_ref, force_ref, turns, columns)
-
-
-def own_gain_kernel(
-    lam_ref, tiles_ref, weights_ref, data_ref, rows_ref, lanes_ref, force_ref, gain_ref, turns, columns
+            total = jnp.sum(near[i, c * 8 : (c + 1) * 8, :], axis=0, keepdims=True) - turned[i : i + 1]
+            force_ref[i : i + 1, lanes] = SPAN * total
+
+
+def own_kernel(lam_ref, tiles_ref, data_ref, force_ref, turns, near, sides):
+    own_forces(lam_ref, tiles_ref, data_ref, force_ref, turns, near, sides, 0, CLUSTERS)
+
+
+def gain_kernel(
+    lam_ref, tiles_ref, weights_ref, data_ref, rows_ref, lanes_ref, force_ref, gain_ref, turns, near, sides
 ):
     write_gain(weights_ref, rows_ref, lanes_ref, gain_ref)
-    own_forces(lam_ref, tiles_ref, data_ref, force_ref, turns, columns)
+    own_forces(lam_ref, tiles_ref, data_ref, force_ref, turns, near, sides, 0, CLUSTERS // 2)
 
 
 def add_halo_forces(lam_ref, data_ref, below_ref, above_ref, partial_ref, force_ref, turns):
@@ -382,9 +403,13 @@
     lax.fori_loop(0, HALO // CLUSTER, one_pair, 0)
 
 
-def halo_kernel(lam_ref, data_ref, below_ref, above_ref, partial_ref, force_ref, turns):
+def rest_kernel(
+    lam_ref, tiles_ref, data_ref, inner_ref, outer_ref, partial_ref, force_ref, turns, near, sides, second
+):
+    own_forces(lam_ref, tiles_ref, data_ref, second, turns, near, sides, CLUSTERS // 2, CLUSTERS)
+    second[...] = second[...] + partial_ref[...]
     force_ref[...] = jnp.zeros_like(force_ref)
-    add_halo_forces(lam_ref, data_ref, below_ref, above_ref, partial_ref, force_ref, turns)
+    add_halo_forces(lam_ref, data_ref, inner_ref, outer_ref, second, force_ref, turns)
 
 
 def advance(force, kicks, data_ref, move_ref, lists_ref, data_out, move_out, low_ref, high_ref):
@@ -461,67 +486,81 @@
 
 
 def halo_last_kernel(
-    lam_ref, data_ref, below_ref, above_ref, partial_ref, long_ref, move_ref, move_out, turns, force
+    lam_ref, data_ref, below_ref, above_ref, partial_ref, long_ref, move_ref, state_ref, turns, force
 ):
     add_halo_forces(lam_ref, data_ref, below_ref, above_ref, partial_ref, force, turns)
     total = force[0:3, :] + long_ref[0:3, :]
-    move_out[...] = move_ref[...]
-    move_out[8:11, :] = move_ref[8:11, :] + 0.5 * STEP_DT * total * data_ref[5:6, :]
-
-
-def swap_flag(round_index, here_ref, there_ref):
+    velocity = move_ref[8:11, :] + 0.5 * STEP_DT * total * data_ref[5:6, :]
+    for i in range(3):
+        state_ref[i] = move_ref[i : i + 1, :]
+        state_ref[3 + i] = velocity[i : i + 1]
+        state_ref[6 + i] = move_ref[3 + i : 4 + i, :]
+    state_ref[9] = move_ref[6:7, :]
+    state_ref[10] = move_ref[7:8, :]
+
+
+def settle_kernel(here_ref, first_ref, second_ref, third_ref, cells_ref, off_ref, vel_ref):
     window = lax.axis_index("lam")
-    windows = lax.axis_size("lam")
-    row = 6 + round_index
-    lower = jnp.logical_and(window % 2 == round_index % 2, window + 1 < windows)
-    upper = jnp.logical_and(window % 2 != round_index % 2, window >= 1)
-    here = jnp.where(lower, here_ref[row : row + 1, :], 0.0)
-    there = jnp.where(upper, there_ref[row : row + 1, :], 0.0)
-    return (here + there) == 1.0
-
-
-def first_swap_kernel(here_ref, there_ref, out_ref):
-    take = swap_flag(0, here_ref, there_ref)
-    out_ref[0:6, :] = jnp.where(take, there_ref[0:6, :], here_ref[0:6, :])
-    out_ref[6:8, :] = here_ref[6:8, :]
-    out_ref[8:16, :] = jnp.where(take, there_ref[8:16, :], here_ref[8:16, :])
-
-
-def last_swap_kernel(here_ref, there_ref, cells_ref, off_ref, vel_ref):
-    take = swap_flag(1, here_ref, there_ref)
-    state = jnp.where(take, there_ref[...], here_ref[...])
-    off_ref[0] = state[0:3]
-    cells_ref[0] = state[3:6].astype(jnp.int32)
-    vel_ref[0] = state[8:11]
-
-
-SMEM = pl.BlockSpec(memory_space=pltpu.SMEM)
-VMEM = pl.BlockSpec(memory_space=pltpu.VMEM)
+    even = window % 2 == 0
+    inside = window + 1 < lax.axis_size("lam")
+    outer = jnp.where(even, second_ref[10], jnp.where(inside, here_ref[10], 0.0)) == 1.0
+    far = jnp.where(even, third_ref[9], second_ref[9]) == 1.0
+    close = jnp.where(even, here_ref[9], first_ref[9]) == 1.0
+    for i in range(9):
+        row = jnp.where(
+            outer,
+            jnp.where(far, third_ref[i], second_ref[i]),
+            jnp.where(close, first_ref[i], here_ref[i]),
+        )
+        if i < 3:
+            off_ref[i] = row
+        elif i < 6:
+            vel_ref[i - 3] = row
+        else:
+            cells_ref[i - 6] = row.astype(jnp.int32)
+
+
+PLACES = {
+    "s": pl.BlockSpec(memory_space=pltpu.SMEM),
+    "v": pl.BlockSpec(memory_space=pltpu.VMEM),
+    "a": pl.BlockSpec(memory_space=pl.ANY),
+}
 
 
 def call(kernel, ins, outs, scratch=(), cost=0):
     return pl.pallas_call(
         kernel,
         out_shape=[jax.ShapeDtypeStruct(shape, dtype) for shape, dtype in outs],
-        in_specs=[SMEM if place == "s" else VMEM for place, _ in ins],
-        out_specs=[VMEM] * len(outs),
+        in_specs=[PLACES[place] for place, _ in ins],
+        out_specs=[PLACES["v"]] * len(outs),
         scratch_shapes=list(scratch),
         compiler_params=pltpu.CompilerParams(vmem_limit_bytes=40 * 2**20),
         cost_estimate=pl.CostEstimate(flops=cost, bytes_accessed=200000, transcendentals=0),
     )(*[value for _, value in ins])
 
 
-def passed_along(value, axis, by):
-    size = lax.axis_size(axis)
-    return lax.ppermute(value, axis, [(i, (i + by) % size) for i in range(size)])
-
-
-def traded(value, round_index):
+def neighbours(inner, outer):
+    size = lax.axis_size("dom")
+    received = []
+    for value, offset in ((inner, 0), (outer, 1)):
+        pairs = []
+        for d in range(offset, size, 2):
+            pairs += [(d, (d + 1) % size), ((d + 1) % size, d)]
+        received.append(lax.ppermute(value, "dom", pairs))
+    return received
+
+
+def ladder_states(state):
     windows = lax.axis_size("lam")
-    pairs = []
-    for w in range(round_index % 2, windows - 1, 2):
-        pairs += [(w, w + 1), (w + 1, w)]
-    return lax.ppermute(value, "lam", pairs)
+    received = []
+    for offset in (0, 1):
+        pairs = []
+        for w in range(offset, windows - 1, 2):
+            pairs += [(w, w + 1), (w + 1, w)]
+        received.append(lax.ppermute(state, "lam", pairs))
+    pairs = [(w - 2, w) for w in range(2, windows, 2)] + [(w + 2, w) for w in range(1, windows - 2, 2)]
+    received.append(lax.ppermute(state, "lam", pairs))
+    return received
 
 
 def exchanged(value):
@@ -532,11 +571,12 @@
     cells, offsets, velocities, charges, coupling, inverse_mass, lambdas, tile_lists, halo_lists, accept_flags
 ):
     wide = ((8, A_DEV), F32)
-    state = ((16, A_DEV), F32)
+    moving = ((16, A_DEV), F32)
     border = ((8, HALO), F32)
     turns = pltpu.VMEM((3, A_DEV), F32)
-    columns = pltpu.VMEM((5, A_DEV, CLUSTER), F32)
-    tiles = tile_lists[0]
+    pair_scratch = [turns, pltpu.VMEM((3, CLUSTERS * 8, CLUSTER), F32), pltpu.VMEM((A_DEV, 8), F32)]
+    spare = pltpu.VMEM((8, A_DEV), F32)
+    tiles = jnp.transpose(tile_lists, (2, 0, 1))
     slab = jnp.asarray(slab_basis())
     square, factor = plane_gain()
     gain_rows = np.zeros((K, 8), np.float32)
@@ -544,82 +584,85 @@
     gain_lanes = np.zeros((8, K), np.float32)
     gain_lanes[0], gain_lanes[1] = square, factor
 
-    grid, data, move, low, high = call(
+    def by_row(x):
+        return jnp.transpose(x, (1, 0, 2))
+
+    grid, data, move, inner, outer = call(
         spread_kernel,
         [
-            ("s", lambdas), ("s", accept_flags), ("v", cells), ("v", offsets), ("v", velocities),
-            ("v", charges[None]), ("v", coupling[None]), ("v", inverse_mass[None]), ("v", halo_lists), ("v", slab),
+            ("s", lambdas), ("s", accept_flags.T), ("v", by_row(cells)), ("v", by_row(offsets)),
+            ("v", by_row(velocities)), ("v", charges[None]), ("v", coupling[None]), ("v", inverse_mass[None]),
+            ("v", halo_lists), ("v", slab),
         ],
-        [((ROWS, K), F32), wide, state, border, border],
+        [((ROWS, K), F32), wide, moving, border, border],
         [pltpu.VMEM((ROWS, A_DEV), BF16), pltpu.VMEM((ROWS, A_DEV), BF16)],
     )
     grid = exchanged(grid)
-    below, above = passed_along(high, "dom", 1), passed_along(low, "dom", -1)
+    inner, outer = neighbours(inner, outer)
     short, gain = call(
-        own_gain_kernel,
+        gain_kernel,
         [
             ("s", lambdas), ("s", tiles), ("s", jnp.asarray(slab_weights())), ("v", data),
             ("v", jnp.asarray(gain_rows)), ("v", jnp.asarray(gain_lanes)),
         ],
         [wide, ((2, K, K), F32)],
-        [turns, columns],
+        pair_scratch,
         cost=2 * 10**9,
     )
     (potential,) = call(
         mesh_kernel,
-        [("v", grid), ("v", gain), ("v", jnp.asarray(basis_table()))],
+        [("v", grid), ("v", gain), ("v", jnp.asarray(basis_table())), ("a", inner), ("a", outer)],
         [((ROWS, K), F32)],
         [pltpu.VMEM((2 * K, K), F32)],
     )
     potential = exchanged(potential)
     (short,) = call(
-        halo_kernel,
-        [("s", lambdas), ("v", data), ("v", below), ("v", above), ("v", short)],
+        rest_kernel,
+        [("s", lambdas), ("s", tiles), ("v", data), ("v", inner), ("v", outer), ("v", short)],
         [wide],
-        [turns],
-        cost=10**9,
-    )
-    far, data, move, low, high = call(
+        [*pair_scratch, spare],
+        cost=2 * 10**9,
+    )
+    far, data, move, inner, outer = call(
         gather_kernel,
         [("v", potential), ("v", data), ("v", move), ("v", short), ("v", halo_lists), ("v", slab)],
-        [wide, wide, state, border, border],
-        [pltpu.VMEM((8, A_DEV), F32)],
+        [wide, wide, moving, border, border],
+        [spare],
     )
 
     def own_call(data):
         (partial,) = call(
-            own_kernel, [("s", lambdas), ("s", tiles), ("v", data)], [wide], [turns, columns], cost=2 * 10**9
+            own_kernel, [("s", lambdas), ("s", tiles), ("v", data)], [wide], pair_scratch, cost=2 * 10**9
         )
         return partial
 
-    below, above = passed_along(high, "dom", 1), passed_along(low, "dom", -1)
+    inner, outer = neighbours(inner, outer)
     short = own_call(data)
-    data, move, low, high = call(
+    data, move, inner, outer = call(
         halo_step_kernel,
         [
-            ("s", lambdas), ("v", data), ("v", below), ("v", above), ("v", short), ("v", far), ("v", move),
+            ("s", lambdas), ("v", data), ("v", inner), ("v", outer), ("v", short), ("v", far), ("v", move),
             ("v", halo_lists),
         ],
-        [wide, state, border, border],
-        [turns, pltpu.VMEM((8, A_DEV), F32)],
-    )
-    below, above = passed_along(high, "dom", 1), passed_along(low, "dom", -1)
+        [wide, moving, border, border],
+        [turns, spare],
+    )
+    inner, outer = neighbours(inner, outer)
     short = own_call(data)
-    (move,) = call(
+    (state,) = call(
         halo_last_kernel,
-        [("s", lambdas), ("v", data), ("v", below), ("v", above), ("v", short), ("v", far), ("v", move)],
-        [state],
-        [turns, pltpu.VMEM((8, A_DEV), F32)],
-    )
-    (move,) = call(first_swap_kernel, [("v", move), ("v", traded(move, 0))], [state])
-    triple = (1, 3, A_DEV)
-    return tuple(
-        call(
-            last_swap_kernel,
-            [("v", move), ("v", traded(move, 1))],
-            [(triple, jnp.int32), (triple, F32), (triple, F32)],
-        )
-    )
+        [("s", lambdas), ("v", data), ("v", inner), ("v", outer), ("v", short), ("v", far), ("v", move)],
+        [((11, 1, A_DEV), F32)],
+        [turns, spare],
+    )
+    first, second, third = ladder_states(state)
+    triple = (3, 1, A_DEV)
+    out = call(
+        settle_kernel,
+        [("v", state), ("v", first), ("v", second), ("v", third)],
+        [(triple, jnp.int32), (triple, F32), (triple, F32)],
+    )
+    return tuple(by_row(x) for x in out)
 
 
 def solution(mesh):

time: 91.3 us -> 112 us (1.23)
  the two profiles are of different devices: /device:TPU:32 before, /device:TPU:30 now
where the time goes in v1:
time: 112 us; the launch traced here: 111 us
  Pallas kernels  54.8 us (49%)
  starting transfers between devices  45.7 us (41%)
  local copies, waits for them, and re-layouts  4.89 us (4%)
  waiting for transfers between devices  4.5 us (4%)
  between operations  1.54 us (1%)
    pallas_call x10, Pallas kernels, call(): pl.pallas_call(kernel, out_shape=[jax.ShapeDtypeStruct(shape, dtype) for...  54.8 us
    ppermute x6, starting transfers between devices, neighbours(): received.append(lax.ppermute(value, 'dom', pairs))  19.1 us
    all_to_all x2, starting transfers between devices, exchanged(): return lax.all_to_all(value, 'dom', split_axis=0, concat_axis=0, tiled=True)  15.2 us
    ppermute x3, starting transfers between devices, ladder_states(): received.append(lax.ppermute(state, 'lam', pairs))  11.5 us
    unnamed x28, local copies, waits for them, and re-layouts  4.89 us
    ppermute x3, waiting for transfers between devices, ladder_states(): received.append(lax.ppermute(state, 'lam', pairs))  4 us
  transfers between devices with their start and end apart: 11, of which 3 were waited for; matrix products, arithmetic and copies ran while one was open for 0% of the time, Pallas kernels for 38%

profile of v1, /device:TPU:30, one launch (start us, length us, event | category | flops | bytes accessed | tf_op | source)
XLA Modules:
  0.0 111.4 jit_solution(8205909505487018823)
XLA Ops:
  1.3 0.0 copy-done.1
  1.4 0.6 copy-done.2
  2.0 0.7 copy-done.3
  2.7 0.7 copy-done.4
  3.4 0.7 copy-done.5
  4.1 0.7 copy-done.6
  4.8 0.7 copy-done.7
  5.5 0.7 copy-done.8
  6.2 2.4 %shard_map.166 = (f32[384,128]{1,0:T(8,128)}, f32[8,1024]{1,0:T(8,128)S(1)}, f32[16,1024]{1,0:T(8,128)S(1)}, f32[8,512]{1,0:T(8,128)S(1)}, f32[8,512]{1,0:T(8,128)S(1)}) custom-call(f32[1]{0:T(128)S(6)} %copy.18.lam_ref, s32[1,2]{1,0:T(1,128)S(1)} %bitcast.23, s32[3,1,1024]{2,1,0:T(1,128)S(1)} %bitcast.17, f32[3,1,1024]{2,1,0:T(1,128)S(1)} %bitcast.18, ...), custom_call_target="tpu_custom_call" | custom-call | bytes 200000 | tf_op jit(solution)/shard_map/pallas_call | solution.py:531
  8.6 10.6 %all-to-all-start = ((f32[16,24,128]{2,1,0:T(8,128)}), f32[16,24,128]{2,1,0:T(8,128)S(1)}, u32[]{:S(2)}, u32[]{:S(2)}) async-start(f32[16,24,128]{2,1,0:T(8,128)} %bitcast.7), calls=%async_computation | async-start | bytes 393216 | tf_op jit(solution)/shard_map/all_to_all | solution.py:567
  19.1 2.3 %collective-permute-start = (f32[8,512]{1,0:T(8,128)S(1)}, f32[8,512]{1,0:T(8,128)S(1)}, u32[]{:S(2)}, u32[]{:S(2)}) collective-permute-start(f32[8,512]{1,0:T(8,128)S(1)} %get-tuple-element.25), channel_id=1, source_target_pairs={{0,1},{1,0},{2,3},{3,2},{4,5},{5,4},{6,7},{7,6},{8,9},{9,8},{10,11... | collective-permute-start | bytes 49160 | tf_op jit(solution)/shard_map/ppermute | solution.py:549
  21.5 4.8 %collective-permute-start.1 = (f32[8,512]{1,0:T(8,128)S(1)}, f32[8,512]{1,0:T(8,128)S(1)}, u32[]{:S(2)}, u32[]{:S(2)}) collective-permute-start(f32[8,512]{1,0:T(8,128)S(1)} %get-tuple-element.26), channel_id=1, source_target_pairs={{1,2},{2,1},{3,4},{4,3},{5,6},{6,5},{7,8},{8,7},{9,10},{10,9},{11,... | collective-permute-start | bytes 49160 | tf_op jit(solution)/shard_map/ppermute | solution.py:549
  26.3 8.2 %shard_map.167 = (f32[8,1024]{1,0:T(8,128)S(1)}, f32[2,128,128]{2,1,0:T(8,128)S(1)}) custom-call(f32[1]{0:T(128)S(6)} %copy.18.lam_ref, s32[6,1,8]{2,1,0:T(1,128)S(1)} %bitcast.24, f32[17,65]{1,0:T(8,128)S(1)} %copy-done.12, f32[8,1024]{1,0:T(8,128)S(1)} %get-tuple-element.23.data_ref, f32[128,8]{1,0:T(8,128)S(1)} %copy-done.11, f32[8,128]{1,0:T(8,128)S(1)} %copy-done.13), custom_call_target="tpu_custom_call" | custom-call | flops 2000000000 | bytes 200000 | tf_op jit(solution)/shard_map/pallas_call | solution.py:531
  34.5 1.5 %shard_map.168 = f32[384,128]{1,0:T(8,128)} custom-call(f32[384,128]{1,0:T(8,128)S(1)} %bitcast.15, f32[2,128,128]{2,1,0:T(8,128)S(1)} %get-tuple-element.24.gain_ref, bf16[512,128]{1,0:T(8,128)(2,1)S(1)} %copy-done, f32[8,512]{1,0:T(8,128)S(1)} %collective-permute-done.inner_ref, f32[8,512]{1,0:T(8,128)S(1)} %collective-permute-done.1.outer_ref), custom_call_target="tpu_custom_call" | custom-call | bytes 200000 | tf_op jit(solution)/shard_map/pallas_call | solution.py:531
  36.0 4.6 %all-to-all-start.1 = ((f32[16,24,128]{2,1,0:T(8,128)}), f32[16,24,128]{2,1,0:T(8,128)S(1)}, u32[]{:S(2)}, u32[]{:S(2)}) async-start(f32[16,24,128]{2,1,0:T(8,128)} %bitcast.10), calls=%async_computation.1 | async-start | bytes 393216 | tf_op jit(solution)/shard_map/all_to_all | solution.py:567
  40.6 9.5 %shard_map.169.short_ref = f32[8,1024]{1,0:T(8,128)S(1)} custom-call(f32[1]{0:T(128)S(6)} %copy.18.lam_ref, s32[6,1,8]{2,1,0:T(1,128)S(1)} %bitcast.25, f32[8,1024]{1,0:T(8,128)S(1)} %get-tuple-element.23.data_ref, f32[8,512]{1,0:T(8,128)S(1)} %collective-permute-done.inner_ref, f32[8,512]{1,0:T(8,128)S(1)} %collective-permute-done.1.outer_ref, ...), custom_call_target="tpu_custom_call" | custom-call | flops 2000000000 | bytes 200000 | tf_op jit(solution)/shard_map/pallas_call | solution.py:531
  50.1 0.5 all-to-all-done.1
  50.6 1.8 %shard_map.170 = (f32[8,1024]{1,0:T(8,128)S(1)}, f32[8,1024]{1,0:T(8,128)S(1)}, f32[16,1024]{1,0:T(8,128)S(1)}, f32[8,512]{1,0:T(8,128)S(1)}, f32[8,512]{1,0:T(8,128)S(1)}) custom-call(f32[384,128]{1,0:T(8,128)S(1)} %bitcast.16, f32[8,1024]{1,0:T(8,128)S(1)} %get-tuple-element.23.data_ref, f32[16,1024]{1,0:T(8,128)S(1)} %get-tuple-element.27.move_ref, ...), custom_call_target="tpu_custom_call" | custom-call | bytes 200000 | tf_op jit(solution)/shard_map/pallas_call | solution.py:531
  52.4 2.7 %collective-permute-start.2 = (f32[8,512]{1,0:T(8,128)S(1)}, f32[8,512]{1,0:T(8,128)S(1)}, u32[]{:S(2)}, u32[]{:S(2)}) collective-permute-start(f32[8,512]{1,0:T(8,128)S(1)} %get-tuple-element.30), channel_id=1, source_target_pairs={{0,1},{1,0},{2,3},{3,2},{4,5},{5,4},{6,7},{7,6},{8,9},{9,8},{10,11... | collective-permute-start | bytes 49160 | tf_op jit(solution)/shard_map/ppermute | solution.py:549
  55.0 3.9 %collective-permute-start.3 = (f32[8,512]{1,0:T(8,128)S(1)}, f32[8,512]{1,0:T(8,128)S(1)}, u32[]{:S(2)}, u32[]{:S(2)}) collective-permute-start(f32[8,512]{1,0:T(8,128)S(1)} %get-tuple-element.31), channel_id=1, source_target_pairs={{1,2},{2,1},{3,4},{4,3},{5,6},{6,5},{7,8},{8,7},{9,10},{10,9},{11,... | collective-permute-start | bytes 49160 | tf_op jit(solution)/shard_map/ppermute | solution.py:549
  59.0 12.6 %shard_map.171.partial_ref = f32[8,1024]{1,0:T(8,128)S(1)} custom-call(f32[1]{0:T(128)S(6)} %copy.18.lam_ref, s32[6,1,8]{2,1,0:T(1,128)S(1)} %bitcast.26, f32[8,1024]{1,0:T(8,128)S(1)} %get-tuple-element.29.data_ref), custom_call_target="tpu_custom_call" | custom-call | flops 2000000000 | bytes 200000 | tf_op jit(solution)/shard_map/pallas_call | solution.py:531
  71.6 2.9 %shard_map.172 = (f32[8,1024]{1,0:T(8,128)S(1)}, f32[16,1024]{1,0:T(8,128)S(1)}, f32[8,512]{1,0:T(8,128)S(1)}, f32[8,512]{1,0:T(8,128)S(1)}) custom-call(f32[1]{0:T(128)S(6)} %copy.18.lam_ref, f32[8,1024]{1,0:T(8,128)S(1)} %get-tuple-element.29.data_ref, f32[8,512]{1,0:T(8,128)S(1)} %collective-permute-done.2.below_ref, ...), custom_call_target="tpu_custom_call" | custom-call | bytes 200000 | tf_op jit(solution)/shard_map/pallas_call | solution.py:531
  74.5 1.9 %collective-permute-start.4 = (f32[8,512]{1,0:T(8,128)S(1)}, f32[8,512]{1,0:T(8,128)S(1)}, u32[]{:S(2)}, u32[]{:S(2)}) collective-permute-start(f32[8,512]{1,0:T(8,128)S(1)} %get-tuple-element.35), channel_id=1, source_target_pairs={{0,1},{1,0},{2,3},{3,2},{4,5},{5,4},{6,7},{7,6},{8,9},{9,8},{10,11... | collective-permute-start | bytes 49160 | tf_op jit(solution)/shard_map/ppermute | solution.py:549
  76.4 3.5 %collective-permute-start.5 = (f32[8,512]{1,0:T(8,128)S(1)}, f32[8,512]{1,0:T(8,128)S(1)}, u32[]{:S(2)}, u32[]{:S(2)}) collective-permute-start(f32[8,512]{1,0:T(8,128)S(1)} %get-tuple-element.36), channel_id=1, source_target_pairs={{1,2},{2,1},{3,4},{4,3},{5,6},{6,5},{7,8},{8,7},{9,10},{10,9},{11,... | collective-permute-start | bytes 49160 | tf_op jit(solution)/shard_map/ppermute | solution.py:549
  79.9 12.6 %shard_map.173.partial_ref = f32[8,1024]{1,0:T(8,128)S(1)} custom-call(f32[1]{0:T(128)S(6)} %copy.18.lam_ref, s32[6,1,8]{2,1,0:T(1,128)S(1)} %bitcast.27, f32[8,1024]{1,0:T(8,128)S(1)} %get-tuple-element.34.data_ref), custom_call_target="tpu_custom_call" | custom-call | flops 2000000000 | bytes 200000 | tf_op jit(solution)/shard_map/pallas_call | solution.py:531
  92.5 2.8 %shard_map.174.here_ref = f32[11,1,1024]{2,1,0:T(1,128)S(1)} custom-call(f32[1]{0:T(128)S(6)} %copy.18.lam_ref, f32[8,1024]{1,0:T(8,128)S(1)} %get-tuple-element.34.data_ref, f32[8,512]{1,0:T(8,128)S(1)} %collective-permute-done.4.below_ref, f32[8,512]{1,0:T(8,128)S(1)} %collective-permute-done.5.above_ref, f32[8,1024]{1,0:T(8,128)S(1)} %shard_map.173.partial_ref, ...), custom_call_target="tpu_custom_call" | custom-call | bytes 200000 | tf_op jit(solution)/shard_map/pallas_call | solution.py:531
  95.3 3.3 %collective-permute-start.8 = (f32[11,1,1024]{2,1,0:T(1,128)S(1)}, f32[11,1,1024]{2,1,0:T(1,128)S(1)}, u32[]{:S(2)}, u32[]{:S(2)}) collective-permute-start(f32[11,1,1024]{2,1,0:T(1,128)S(1)} %shard_map.174.here_ref), channel_id=1, source_target_pairs={{0,32},{32,64},{64,96},{96,128},{128,160},{160,192},{192,224},{224... | collective-permute-start | bytes 135176 | tf_op jit(solution)/shard_map/ppermute | solution.py:562
  98.6 6.2 %collective-permute-start.7 = (f32[11,1,1024]{2,1,0:T(1,128)S(1)}, f32[11,1,1024]{2,1,0:T(1,128)S(1)}, u32[]{:S(2)}, u32[]{:S(2)}) collective-permute-start(f32[11,1,1024]{2,1,0:T(1,128)S(1)} %shard_map.174.here_ref), channel_id=1, source_target_pairs={{16,32},{32,16},{48,64},{64,48},{80,96},{96,80},{112,128},{128,112... | collective-permute-start | bytes 135176 | tf_op jit(solution)/shard_map/ppermute | solution.py:560
  104.8 1.9 %collective-permute-start.6 = (f32[11,1,1024]{2,1,0:T(1,128)S(1)}, f32[11,1,1024]{2,1,0:T(1,128)S(1)}, u32[]{:S(2)}, u32[]{:S(2)}) collective-permute-start(f32[11,1,1024]{2,1,0:T(1,128)S(1)} %shard_map.174.here_ref), channel_id=1, source_target_pairs={{0,16},{16,0},{32,48},{48,32},{64,80},{80,64},{96,112},{112,96},{1... | collective-permute-start | bytes 135176 | tf_op jit(solution)/shard_map/ppermute | solution.py:560
  106.8 1.1 collective-permute-done.7.second_ref
  107.9 2.9 %collective-permute-done.6.first_ref = f32[11,1,1024]{2,1,0:T(1,128)S(1)} collective-permute-done((f32[11,1,1024]{2,1,0:T(1,128)S(1)}, f32[11,1,1024]{2,1,0:T(1,128)S(1)}, u32[]{:S(2)}, u32[]{:S(2)}) %collective-permute-start.6) | collective-permute-done | bytes 45088 | tf_op jit(solution)/shard_map/ppermute | solution.py:560
  110.8 0.6 shard_map.175
  (28 shorter events, 0.1 us)
Async XLA Ops:
  0.6 0.7 copy-start.1
  1.3 0.7 copy-start.2
  1.3 0.7 copy-start.9
  2.0 0.7 copy-start.3
  2.7 0.7 copy-start.4
  3.4 0.7 copy-start.5
  4.1 0.7 copy-start.6
  4.8 0.7 copy-start.7
  5.5 0.7 copy-start.8
  8.6 17.7 %copy-start.11 = (f32[128,8]{1,0:T(8,128)S(1)}, f32[128,8]{1,0:T(8,128)}, u32[]{:S(2)}) copy-start(f32[128,8]{1,0:T(8,128)} %constant.12.clone.rows_ref) | copy-start | bytes 12292
  8.6 17.7 %copy-start.12 = (f32[17,65]{1,0:T(8,128)S(1)}, f32[17,65]{1,0:T(8,128)}, u32[]{:S(2)}) copy-start(f32[17,65]{1,0:T(8,128)} %constant.11.clone.weights_ref) | copy-start | bytes 13264
  8.6 25.9 %all-to-all-start = ((f32[16,24,128]{2,1,0:T(8,128)}), f32[16,24,128]{2,1,0:T(8,128)S(1)}, u32[]{:S(2)}, u32[]{:S(2)}) async-start(f32[16,24,128]{2,1,0:T(8,128)} %bitcast.7), calls=%async_computation | async-start | bytes 393216 | tf_op jit(solution)/shard_map/all_to_all | solution.py:567
  19.1 7.1 %copy-start.13 = (f32[8,128]{1,0:T(8,128)S(1)}, f32[8,128]{1,0:T(8,128)}, u32[]{:S(2)}) copy-start(f32[8,128]{1,0:T(8,128)} %constant.13.clone.lanes_ref) | copy-start | bytes 12292
  19.1 7.1 %copy-start.10 = (s32[1,8,6]{1,0,2:T(1,128)S(1)}, s32[1,8,6]{1,0,2:T(1,128)}, u32[]{:S(2)}) copy-start(s32[1,8,6]{1,0,2:T(1,128)} %param.22) | copy-start | bytes 580
  19.1 15.3 %collective-permute-start = (f32[8,512]{1,0:T(8,128)S(1)}, f32[8,512]{1,0:T(8,128)S(1)}, u32[]{:S(2)}, u32[]{:S(2)}) collective-permute-start(f32[8,512]{1,0:T(8,128)S(1)} %get-tuple-element.25), channel_id=1, source_target_pairs={{0,1},{1,0},{2,3},{3,2},{4,5},{5,4},{6,7},{7,6},{8,9},{9,8},{10,11... | collective-permute-start | bytes 49160 | tf_op jit(solution)/shard_map/ppermute | solution.py:549
  21.5 13.0 %collective-permute-start.1 = (f32[8,512]{1,0:T(8,128)S(1)}, f32[8,512]{1,0:T(8,128)S(1)}, u32[]{:S(2)}, u32[]{:S(2)}) collective-permute-start(f32[8,512]{1,0:T(8,128)S(1)} %get-tuple-element.26), channel_id=1, source_target_pairs={{1,2},{2,1},{3,4},{4,3},{5,6},{6,5},{7,8},{8,7},{9,10},{10,9},{11,... | collective-permute-start | bytes 49160 | tf_op jit(solution)/shard_map/ppermute | solution.py:549
  26.3 8.2 %copy-start = (bf16[512,128]{1,0:T(8,128)(2,1)S(1)}, bf16[512,128]{1,0:T(8,128)(2,1)}, u32[]{:S(2)}) copy-start(bf16[512,128]{1,0:T(8,128)(2,1)} %constant.14.clone.basis_ref) | copy-start | bytes 393220
  36.0 14.6 %all-to-all-start.1 = ((f32[16,24,128]{2,1,0:T(8,128)}), f32[16,24,128]{2,1,0:T(8,128)S(1)}, u32[]{:S(2)}, u32[]{:S(2)}) async-start(f32[16,24,128]{2,1,0:T(8,128)} %bitcast.10), calls=%async_computation.1 | async-start | bytes 393216 | tf_op jit(solution)/shard_map/all_to_all | solution.py:567
  52.4 19.2 %collective-permute-start.2 = (f32[8,512]{1,0:T(8,128)S(1)}, f32[8,512]{1,0:T(8,128)S(1)}, u32[]{:S(2)}, u32[]{:S(2)}) collective-permute-start(f32[8,512]{1,0:T(8,128)S(1)} %get-tuple-element.30), channel_id=1, source_target_pairs={{0,1},{1,0},{2,3},{3,2},{4,5},{5,4},{6,7},{7,6},{8,9},{9,8},{10,11... | collective-permute-start | bytes 49160 | tf_op jit(solution)/shard_map/ppermute | solution.py:549
  55.0 16.5 %collective-permute-start.3 = (f32[8,512]{1,0:T(8,128)S(1)}, f32[8,512]{1,0:T(8,128)S(1)}, u32[]{:S(2)}, u32[]{:S(2)}) collective-permute-start(f32[8,512]{1,0:T(8,128)S(1)} %get-tuple-element.31), channel_id=1, source_target_pairs={{1,2},{2,1},{3,4},{4,3},{5,6},{6,5},{7,8},{8,7},{9,10},{10,9},{11,... | collective-permute-start | bytes 49160 | tf_op jit(solution)/shard_map/ppermute | solution.py:549
  74.5 18.0 %collective-permute-start.4 = (f32[8,512]{1,0:T(8,128)S(1)}, f32[8,512]{1,0:T(8,128)S(1)}, u32[]{:S(2)}, u32[]{:S(2)}) collective-permute-start(f32[8,512]{1,0:T(8,128)S(1)} %get-tuple-element.35), channel_id=1, source_target_pairs={{0,1},{1,0},{2,3},{3,2},{4,5},{5,4},{6,7},{7,6},{8,9},{9,8},{10,11... | collective-permute-start | bytes 49160 | tf_op jit(solution)/shard_map/ppermute | solution.py:549
  76.4 16.1 %collective-permute-start.5 = (f32[8,512]{1,0:T(8,128)S(1)}, f32[8,512]{1,0:T(8,128)S(1)}, u32[]{:S(2)}, u32[]{:S(2)}) collective-permute-start(f32[8,512]{1,0:T(8,128)S(1)} %get-tuple-element.36), channel_id=1, source_target_pairs={{1,2},{2,1},{3,4},{4,3},{5,6},{6,5},{7,8},{8,7},{9,10},{10,9},{11,... | collective-permute-start | bytes 49160 | tf_op jit(solution)/shard_map/ppermute | solution.py:549
  95.3 11.5 %collective-permute-start.8 = (f32[11,1,1024]{2,1,0:T(1,128)S(1)}, f32[11,1,1024]{2,1,0:T(1,128)S(1)}, u32[]{:S(2)}, u32[]{:S(2)}) collective-permute-start(f32[11,1,1024]{2,1,0:T(1,128)S(1)} %shard_map.174.here_ref), channel_id=1, source_target_pairs={{0,32},{32,64},{64,96},{96,128},{128,160},{160,192},{192,224},{224... | collective-permute-start | bytes 135176 | tf_op jit(solution)/shard_map/ppermute | solution.py:562
  98.6 9.3 %collective-permute-start.7 = (f32[11,1,1024]{2,1,0:T(1,128)S(1)}, f32[11,1,1024]{2,1,0:T(1,128)S(1)}, u32[]{:S(2)}, u32[]{:S(2)}) collective-permute-start(f32[11,1,1024]{2,1,0:T(1,128)S(1)} %shard_map.174.here_ref), channel_id=1, source_target_pairs={{16,32},{32,16},{48,64},{64,48},{80,96},{96,80},{112,128},{128,112... | collective-permute-start | bytes 135176 | tf_op jit(solution)/shard_map/ppermute | solution.py:560
  104.8 5.9 %collective-permute-start.6 = (f32[11,1,1024]{2,1,0:T(1,128)S(1)}, f32[11,1,1024]{2,1,0:T(1,128)S(1)}, u32[]{:S(2)}, u32[]{:S(2)}) collective-permute-start(f32[11,1,1024]{2,1,0:T(1,128)S(1)} %shard_map.174.here_ref), channel_id=1, source_target_pairs={{0,16},{16,0},{32,48},{48,32},{64,80},{80,64},{96,112},{112,96},{1... | collective-permute-start | bytes 135176 | tf_op jit(solution)/shard_map/ppermute | solution.py:560

commit v2 on v1

--- a/solution.py
+++ b/solution.py
@@ -179,15 +179,12 @@
     return (*xyz, q, w)
 
 
-def write_halo(data, lists_ref, inner_ref, outer_ref):
-    even = lax.axis_index("dom") % 2 == 0
+def write_halo(data, lists_ref, low_ref, high_ref):
     lane = lax.broadcasted_iota(jnp.int32, (8, CLUSTER), 1)
-    for flip, out_ref in ((False, inner_ref), (True, outer_ref)):
+    for row, out_ref in ((0, low_ref), (1, high_ref)):
         for k in range(HALO // CLUSTER):
             columns = slice(k * CLUSTER, (k + 1) * CLUSTER)
-            low, high = lists_ref[0, 0:1, columns], lists_ref[0, 1:2, columns]
-            row = jnp.where(even, low, high) if flip else jnp.where(even, high, low)
-            index = jnp.broadcast_to(row & (CLUSTER - 1), (8, CLUSTER))
+            index = jnp.broadcast_to(lists_ref[0, row : row + 1, columns] & (CLUSTER - 1), (8, CLUSTER))
             first = data[:, 2 * k * CLUSTER : (2 * k + 1) * CLUSTER]
             second = data[:, (2 * k + 1) * CLUSTER : (2 * k + 2) * CLUSTER]
             out_ref[:, columns] = jnp.where(
@@ -198,9 +195,24 @@
 
 
 def spread_kernel(
-    lam_ref, flag_ref, cells_ref, off_ref, vel_ref, charge_ref, coup_ref, mass_ref, lists_ref, slab_ref,
-    out_ref, data_ref, move_ref, low_ref, high_ref, mixed_high, mixed_low,
+    lam_ref, cells_hbm, off_hbm, vel_hbm, charge_hbm, coup_hbm, mass_hbm, lists_hbm, slab_hbm, flag_hbm,
+    out_ref, data_ref, move_ref, low_ref, high_ref, ladder_ref, mixed_high, mixed_low,
+    cells_ref, off_ref, vel_ref, charge_ref, coup_ref, mass_ref, lists_ref, slab_ref, flag_ref, arrived,
 ):
+    copies = [
+        pltpu.make_async_copy(source, target, arrived.at[i])
+        for i, (source, target) in enumerate(
+            (
+                (cells_hbm, cells_ref), (off_hbm, off_ref), (vel_hbm, vel_ref), (charge_hbm, charge_ref),
+                (coup_hbm, coup_ref), (mass_hbm, mass_ref), (lists_hbm, lists_ref), (slab_hbm, slab_ref),
+                (flag_hbm, flag_ref),
+            )
+        )
+    ]
+    for copy in copies:
+        copy.start()
+    for copy in copies:
+        copy.wait()
     weight = 1.0 - lam_ref[0] * coup_ref[...]
     charge = charge_ref[...] * weight
 
@@ -210,8 +222,7 @@
         move_ref[3 + i : 4 + i, :] = cell
         move_ref[8 + i : 9 + i, :] = vel_ref[i]
         data_ref[i : i + 1, :] = cell + off_ref[i]
-    move_ref[6:7, :] = jnp.full((1, A_DEV), flag_ref[0, 0].astype(F32))
-    move_ref[7:8, :] = jnp.full((1, A_DEV), flag_ref[0, 1].astype(F32))
+    move_ref[6:8, :] = jnp.zeros((2, A_DEV), F32)
     move_ref[11:16, :] = jnp.zeros((5, A_DEV), F32)
     data_ref[3:4, :] = charge
     data_ref[4:5, :] = weight
@@ -221,6 +232,10 @@
 
     off = move_ref[0:3, :]
     cells = [cells_ref[i] for i in range(3)]
+    for i in range(3):
+        ladder_ref[i] = cells[i]
+    half = lax.broadcasted_iota(jnp.int32, (1, A_DEV), 1) < A_DEV // 2
+    ladder_ref[3] = jnp.where(half, flag_ref[0:1, 0:1], flag_ref[0:1, 1:2])
     weights, _ = spline_set(off)
     row = iota_rows(16, A_DEV)
     plane = jnp.where(row < 8, row, 8 + (row & 3))
@@ -243,8 +258,8 @@
     out_ref[...] = dot3((mixed_high[...], mixed_low[...]), split(y_table), (((1,), (1,)), ((), ())))
 
 
-def mesh_kernel(grid_ref, gain_ref, basis_ref, inner_ref, outer_ref, out_ref, block):
-    del inner_ref, outer_ref
+def mesh_kernel(grid_ref, gain_ref, basis_ref, below_ref, above_ref, out_ref, block):
+    del below_ref, above_ref
     top = iota_rows(8, K) < 4
     for e in range(N_DOM):
         spill = grid_ref[((e - 1) % N_DOM) * SLAB + 16 : ((e - 1) % N_DOM) * SLAB + 24, :]
@@ -319,7 +334,6 @@
 def own_forces(lam_ref, tiles_ref, data_ref, force_ref, turns, near, sides, first, last):
     turns[...] = fixed_turns(data_ref[0:3, :])
     near[...] = jnp.zeros_like(near)
-    sides[...] = jnp.zeros_like(sides)
     floor_value = SOFT_FLOOR + SOFT_SCALE * lam_ref[0]
 
     def one_cluster(b, carry):
@@ -341,9 +355,7 @@
                 if j:
                     side.append([back[j] * p for p in terms])
             for i in range(3):
-                sides[pl.ds(start + chunk * 8, 8), i : i + 1] = jnp.sum(
-                    side[0][i] + side[1][i], axis=1, keepdims=True
-                )
+                sides[i, pl.ds(pl.multiple_of(start + chunk * 8, 8), 8), :] = side[0][i] + side[1][i]
         for j, a in enumerate(others):
             rows = pl.ds(pl.multiple_of(a * 8, 8), 8)
             for i in range(3):
@@ -353,12 +365,20 @@
 
     lax.fori_loop(first, last, one_cluster, 0)
     force_ref[...] = jnp.zeros_like(force_ref)
+    ones = jnp.ones((8, CLUSTER), BF16)
     for c in range(CLUSTERS):
         lanes = slice(c * CLUSTER, (c + 1) * CLUSTER)
-        turned = sides[lanes, :].T
         for i in range(3):
-            total = jnp.sum(near[i, c * 8 : (c + 1) * 8, :], axis=0, keepdims=True) - turned[i : i + 1]
-            force_ref[i : i + 1, lanes] = SPAN * total
+            force_ref[i : i + 1, lanes] = SPAN * jnp.sum(near[i, c * 8 : (c + 1) * 8, :], axis=0, keepdims=True)
+    rows = slice(first * CLUSTER, last * CLUSTER)
+    for i in range(3):
+        rest = sides[i, rows, :]
+        total = jnp.zeros((8, (last - first) * CLUSTER), F32)
+        for _ in range(3):
+            part = rest.astype(BF16)
+            rest = rest - part.astype(F32)
+            total = total + lax.dot_general(ones, part, (((1,), (1,)), ((), ())), preferred_element_type=F32)
+        force_ref[i : i + 1, rows] = force_ref[i : i + 1, rows] - SPAN * total[0:1]
 
 
 def own_kernel(lam_ref, tiles_ref, data_ref, force_ref, turns, near, sides):
@@ -404,15 +424,15 @@
 
 
 def rest_kernel(
-    lam_ref, tiles_ref, data_ref, inner_ref, outer_ref, partial_ref, force_ref, turns, near, sides, second
+    lam_ref, tiles_ref, data_ref, below_ref, above_ref, partial_ref, force_ref, turns, near, sides, second
 ):
     own_forces(lam_ref, tiles_ref, data_ref, second, turns, near, sides, CLUSTERS // 2, CLUSTERS)
     second[...] = second[...] + partial_ref[...]
     force_ref[...] = jnp.zeros_like(force_ref)
-    add_halo_forces(lam_ref, data_ref, inner_ref, outer_ref, second, force_ref, turns)
-
-
-def advance(force, kicks, data_ref, move_ref, lists_ref, data_out, move_out, low_ref, high_ref):
+    add_halo_forces(lam_ref, data_ref, below_ref, above_ref, second, force_ref, turns)
+
+
+def advance(force, kicks, data_ref, move_ref, lists_ref, data_out, move_out, low_ref, high_ref, off_ref=None):
     mass = data_ref[5:6, :]
     velocity = move_ref[8:11, :]
     for _ in range(kicks):
@@ -423,6 +443,9 @@
     move_out[8:11, :] = velocity
     data_out[...] = data_ref[...]
     data_out[0:3, :] = move_ref[3:6, :] + off
+    if off_ref is not None:
+        for i in range(3):
+            off_ref[i] = off[i : i + 1]
     write_halo(data_out[...], lists_ref, low_ref, high_ref)
 
 
@@ -477,47 +500,44 @@
 
 
 def halo_step_kernel(
-    lam_ref, data_ref, below_ref, above_ref, partial_ref, long_ref, move_ref, lists_ref,
-    data_out, move_out, low_ref, high_ref, turns, force,
+    lam_ref, data_ref, below_ref, above_ref, partial_ref, long_ref, move_ref, lists_ref, ladder_ref,
+    data_out, move_out, low_ref, high_ref, off_ref, turns, force,
 ):
+    del ladder_ref
     add_halo_forces(lam_ref, data_ref, below_ref, above_ref, partial_ref, force, turns)
     total = force[0:3, :] + long_ref[0:3, :]
-    advance(total, 2, data_ref, move_ref, lists_ref, data_out, move_out, low_ref, high_ref)
+    advance(total, 2, data_ref, move_ref, lists_ref, data_out, move_out, low_ref, high_ref, off_ref)
 
 
 def halo_last_kernel(
-    lam_ref, data_ref, below_ref, above_ref, partial_ref, long_ref, move_ref, state_ref, turns, force
+    lam_ref, data_ref, below_ref, above_ref, partial_ref, long_ref, move_ref, offsets_ref, velocity_ref, turns, force
 ):
+    del offsets_ref
     add_halo_forces(lam_ref, data_ref, below_ref, above_ref, partial_ref, force, turns)
     total = force[0:3, :] + long_ref[0:3, :]
     velocity = move_ref[8:11, :] + 0.5 * STEP_DT * total * data_ref[5:6, :]
     for i in range(3):
-        state_ref[i] = move_ref[i : i + 1, :]
-        state_ref[3 + i] = velocity[i : i + 1]
-        state_ref[6 + i] = move_ref[3 + i : 4 + i, :]
-    state_ref[9] = move_ref[6:7, :]
-    state_ref[10] = move_ref[7:8, :]
-
-
-def settle_kernel(here_ref, first_ref, second_ref, third_ref, cells_ref, off_ref, vel_ref):
+        velocity_ref[i] = velocity[i : i + 1]
+
+
+def settle_kernel(ladder_ref, offsets_ref, vel_hbm, cells_ref, off_ref, vel_ref, arrived, done):
     window = lax.axis_index("lam")
-    even = window % 2 == 0
-    inside = window + 1 < lax.axis_size("lam")
-    outer = jnp.where(even, second_ref[10], jnp.where(inside, here_ref[10], 0.0)) == 1.0
-    far = jnp.where(even, third_ref[9], second_ref[9]) == 1.0
-    close = jnp.where(even, here_ref[9], first_ref[9]) == 1.0
-    for i in range(9):
-        row = jnp.where(
-            outer,
-            jnp.where(far, third_ref[i], second_ref[i]),
-            jnp.where(close, first_ref[i], here_ref[i]),
-        )
-        if i < 3:
-            off_ref[i] = row
-        elif i < 6:
-            vel_ref[i - 3] = row
-        else:
-            cells_ref[i - 6] = row.astype(jnp.int32)
+    windows = lax.axis_size("lam")
+
+    def partner(w, round_index):
+        low = jnp.where(w % 2 == round_index % 2, w, w - 1)
+        inside = jnp.logical_and(low >= 0, low + 1 < windows)
+        flag = jnp.max(ladder_ref[jnp.maximum(low, 0), 3, :, round_index * (A_DEV // 2) : (round_index + 1) * (A_DEV // 2)])
+        return jnp.where(jnp.logical_and(inside, flag == 1), 2 * low + 1 - w, w)
+
+    source = partner(partner(window, 1), 0)
+    copy = pltpu.make_async_copy(vel_hbm.at[source], arrived, done)
+    copy.start()
+    for i in range(3):
+        cells_ref[i] = ladder_ref[source, i]
+        off_ref[i] = offsets_ref[source, i]
+    copy.wait()
+    vel_ref[...] = arrived[...]
 
 
 PLACES = {
@@ -527,40 +547,23 @@
 }
 
 
-def call(kernel, ins, outs, scratch=(), cost=0):
+def call(kernel, ins, outs, scratch=(), cost=0, limit=40):
     return pl.pallas_call(
         kernel,
         out_shape=[jax.ShapeDtypeStruct(shape, dtype) for shape, dtype in outs],
         in_specs=[PLACES[place] for place, _ in ins],
         out_specs=[PLACES["v"]] * len(outs),
         scratch_shapes=list(scratch),
-        compiler_params=pltpu.CompilerParams(vmem_limit_bytes=40 * 2**20),
+        compiler_params=pltpu.CompilerParams(vmem_limit_bytes=limit * 2**20),
         cost_estimate=pl.CostEstimate(flops=cost, bytes_accessed=200000, transcendentals=0),
     )(*[value for _, value in ins])
 
 
-def neighbours(inner, outer):
+def neighbours(low, high):
     size = lax.axis_size("dom")
-    received = []
-    for value, offset in ((inner, 0), (outer, 1)):
-        pairs = []
-        for d in range(offset, size, 2):
-            pairs += [(d, (d + 1) % size), ((d + 1) % size, d)]
-        received.append(lax.ppermute(value, "dom", pairs))
-    return received
-
-
-def ladder_states(state):
-    windows = lax.axis_size("lam")
-    received = []
-    for offset in (0, 1):
-        pairs = []
-        for w in range(offset, windows - 1, 2):
-            pairs += [(w, w + 1), (w + 1, w)]
-        received.append(lax.ppermute(state, "lam", pairs))
-    pairs = [(w - 2, w) for w in range(2, windows, 2)] + [(w + 2, w) for w in range(1, windows - 2, 2)]
-    received.append(lax.ppermute(state, "lam", pairs))
-    return received
+    below = lax.ppermute(high, "dom", [(i, (i + 1) % size) for i in range(size)])
+    above = lax.ppermute(low, "dom", [(i, (i - 1) % size) for i in range(size)])
+    return below, above
 
 
 def exchanged(value):
@@ -574,7 +577,7 @@
     moving = ((16, A_DEV), F32)
     border = ((8, HALO), F32)
     turns = pltpu.VMEM((3, A_DEV), F32)
-    pair_scratch = [turns, pltpu.VMEM((3, CLUSTERS * 8, CLUSTER), F32), pltpu.VMEM((A_DEV, 8), F32)]
+    pair_scratch = [turns, pltpu.VMEM((3, CLUSTERS * 8, CLUSTER), F32), pltpu.VMEM((3, A_DEV, CLUSTER), F32)]
     spare = pltpu.VMEM((8, A_DEV), F32)
     tiles = jnp.transpose(tile_lists, (2, 0, 1))
     slab = jnp.asarray(slab_basis())
@@ -584,21 +587,35 @@
     gain_lanes = np.zeros((8, K), np.float32)
     gain_lanes[0], gain_lanes[1] = square, factor
 
+    triple = (3, 1, A_DEV)
+
     def by_row(x):
         return jnp.transpose(x, (1, 0, 2))
 
-    grid, data, move, inner, outer = call(
+    def everywhere(x):
+        return lax.all_gather(x, "lam", axis=0, tiled=False)
+
+
+    grid, data, move, low, high, ladder = call(
         spread_kernel,
         [
-            ("s", lambdas), ("s", accept_flags.T), ("v", by_row(cells)), ("v", by_row(offsets)),
-            ("v", by_row(velocities)), ("v", charges[None]), ("v", coupling[None]), ("v", inverse_mass[None]),
-            ("v", halo_lists), ("v", slab),
+            ("s", lambdas), ("a", by_row(cells)), ("a", by_row(offsets)), ("a", by_row(velocities)),
+            ("a", charges[None]), ("a", coupling[None]), ("a", inverse_mass[None]), ("a", halo_lists), ("a", slab),
+            ("a", accept_flags.T),
         ],
-        [((ROWS, K), F32), wide, moving, border, border],
-        [pltpu.VMEM((ROWS, A_DEV), BF16), pltpu.VMEM((ROWS, A_DEV), BF16)],
-    )
+        [((ROWS, K), F32), wide, moving, border, border, ((4, 1, A_DEV), jnp.int32)],
+        [
+            pltpu.VMEM((ROWS, A_DEV), BF16), pltpu.VMEM((ROWS, A_DEV), BF16),
+            pltpu.VMEM((3, 1, A_DEV), jnp.int32), pltpu.VMEM((3, 1, A_DEV), F32), pltpu.VMEM((3, 1, A_DEV), F32),
+            pltpu.VMEM((1, A_DEV), F32), pltpu.VMEM((1, A_DEV), F32), pltpu.VMEM((1, A_DEV), F32),
+            pltpu.VMEM((1, 2, HALO), jnp.int32), pltpu.VMEM((MODES, MODES), F32), pltpu.VMEM((1, 2), jnp.int32),
+            pltpu.SemaphoreType.DMA((9,)),
+        ],
+        limit=60,
+    )
+    ladder = everywhere(ladder)
     grid = exchanged(grid)
-    inner, outer = neighbours(inner, outer)
+    below, above = neighbours(low, high)
     short, gain = call(
         gain_kernel,
         [
@@ -611,19 +628,19 @@
     )
     (potential,) = call(
         mesh_kernel,
-        [("v", grid), ("v", gain), ("v", jnp.asarray(basis_table())), ("a", inner), ("a", outer)],
+        [("v", grid), ("v", gain), ("v", jnp.asarray(basis_table())), ("a", below), ("a", above)],
         [((ROWS, K), F32)],
         [pltpu.VMEM((2 * K, K), F32)],
     )
     potential = exchanged(potential)
     (short,) = call(
         rest_kernel,
-        [("s", lambdas), ("s", tiles), ("v", data), ("v", inner), ("v", outer), ("v", short)],
+        [("s", lambdas), ("s", tiles), ("v", data), ("v", below), ("v", above), ("v", short)],
         [wide],
         [*pair_scratch, spare],
         cost=2 * 10**9,
     )
-    far, data, move, inner, outer = call(
+    far, data, move, low, high = call(
         gather_kernel,
         [("v", potential), ("v", data), ("v", move), ("v", short), ("v", halo_lists), ("v", slab)],
         [wide, wide, moving, border, border],
@@ -636,31 +653,35 @@
         )
         return partial
 
-    inner, outer = neighbours(inner, outer)
+    below, above = neighbours(low, high)
     short = own_call(data)
-    data, move, inner, outer = call(
+    data, move, low, high, offset = call(
         halo_step_kernel,
         [
-            ("s", lambdas), ("v", data), ("v", inner), ("v", outer), ("v", short), ("v", far), ("v", move),
-            ("v", halo_lists),
+            ("s", lambdas), ("v", data), ("v", below), ("v", above), ("v", short), ("v", far), ("v", move),
+            ("v", halo_lists), ("a", ladder),
         ],
-        [wide, moving, border, border],
+        [wide, moving, border, border, (triple, F32)],
         [turns, spare],
     )
-    inner, outer = neighbours(inner, outer)
+    all_offsets = everywhere(offset)
+    below, above = neighbours(low, high)
     short = own_call(data)
-    (state,) = call(
+    (velocity,) = call(
         halo_last_kernel,
-        [("s", lambdas), ("v", data), ("v", inner), ("v", outer), ("v", short), ("v", far), ("v", move)],
-        [((11, 1, A_DEV), F32)],
+        [
+            ("s", lambdas), ("v", data), ("v", below), ("v", above), ("v", short), ("v", far), ("v", move),
+            ("a", all_offsets),
+        ],
+        [(triple, F32)],
         [turns, spare],
     )
-    first, second, third = ladder_states(state)
-    triple = (3, 1, A_DEV)
     out = call(
         settle_kernel,
-        [("v", state), ("v", first), ("v", second), ("v", third)],
+        [("v", ladder), ("v", all_offsets), ("a", everywhere(velocity))],
         [(triple, jnp.int32), (triple, F32), (triple, F32)],
+        [pltpu.VMEM(triple, F32), pltpu.SemaphoreType.DMA],
+        limit=60,
     )
     return tuple(by_row(x) for x in out)
 

time: 112 us -> 215 us (1.92)
  the two profiles are of different devices: /device:TPU:30 before, /device:TPU:16 now
where the time goes in v2:
time: 215 us
  blocking collectives  150 us (70%)
  Pallas kernels  36.7 us (17%)
  starting transfers between devices  24.7 us (11%)
  waiting for transfers between devices  2.16 us (1%)
    all_gather x3, blocking collectives, everywhere(): return lax.all_gather(x, 'lam', axis=0, tiled=False)  150 us
    pallas_call x10, Pallas kernels, call(): pl.pallas_call(kernel, out_shape=[jax.ShapeDtypeStruct(shape, dtype) for...  36.7 us
    all_to_all x2, starting transfers between devices, exchanged(): return lax.all_to_all(value, 'dom', split_axis=0, concat_axis=0, tiled=True)  15.8 us
    ppermute x3, starting transfers between devices, neighbours(): above = lax.ppermute(low, 'dom', [(i, (i - 1) % size) for i in range(size)])  8.46 us
  transfers between devices with their start and end apart: 8, of which 1 were waited for; matrix products, arithmetic and copies ran while one was open for 0% of the time, Pallas kernels for 10%

profile of v2, /device:TPU:16, one launch (start us, length us, event | category | flops | bytes accessed | tf_op | source)
XLA Modules:
  0.0 214.8 jit_solution(13893698937502126369)
XLA Ops:
  1.3 2.8 %shard_map.166 = (f32[384,128]{1,0:T(8,128)}, f32[8,1024]{1,0:T(8,128)}, f32[16,1024]{1,0:T(8,128)}, f32[8,512]{1,0:T(8,128)}, f32[8,512]{1,0:T(8,128)}, /*index=5*/s32[4,1,1024]{2,1,0:T(1,128)}) custom-call(f32[1]{0:T(128)S(6)} %copy.18.lam_ref, s32[3,1,1024]{2,1,0:T(1,128)} %bitcast.30, f32[3,1,1024]{2,1,0:T(1,128)} %bitcast.31, f32[3,1,1024]{2,1,0:T(1,128)} %bitcast.32, ...), custom_call_target="tpu_custom_call" | custom-call | bytes 200000 | tf_op jit(solution)/shard_map/pallas_call | solution.py:551
  4.1 0.0 copy-start.8
  4.1 0.0 copy-start.9
  4.1 10.6 %all-to-all-start = ((f32[16,24,128]{2,1,0:T(8,128)}), f32[16,24,128]{2,1,0:T(8,128)S(1)}, u32[]{:S(2)}, u32[]{:S(2)}) async-start(f32[16,24,128]{2,1,0:T(8,128)} %bitcast.29), calls=%async_computation | async-start | bytes 393216 | tf_op jit(solution)/shard_map/all_to_all | solution.py:570
  14.7 0.0 copy-start.10
  14.7 0.0 copy-start.7
  14.7 0.4 collective-permute-start
  15.2 2.6 %collective-permute-start.1 = (f32[8,512]{1,0:T(8,128)S(1)}, f32[8,512]{1,0:T(8,128)S(1)}, u32[]{:S(2)}, u32[]{:S(2)}) collective-permute-start(f32[8,512]{1,0:T(8,128)S(1)} %copy-done.12), channel_id=1, source_target_pairs={{0,15},{1,0},{2,1},{3,2},{4,3},{5,4},{6,5},{7,6},{8,7},{9,8},{10,9... | collective-permute-start | bytes 49160 | tf_op jit(solution)/shard_map/ppermute | solution.py:565
  17.7 0.0 copy-start.2
  17.7 4.7 %shard_map.167 = (f32[8,1024]{1,0:T(8,128)S(1)}, f32[2,128,128]{2,1,0:T(8,128)S(1)}) custom-call(f32[1]{0:T(128)S(6)} %copy.18.lam_ref, s32[6,1,8]{2,1,0:T(1,128)S(1)} %bitcast.24, f32[17,65]{1,0:T(8,128)S(1)} %copy-done.9, f32[8,1024]{1,0:T(8,128)S(1)} %copy-done.6, f32[128,8]{1,0:T(8,128)S(1)} %copy-done.8, f32[8,128]{1,0:T(8,128)S(1)} %copy-done.10), custom_call_target="tpu_custom_call" | custom-call | flops 2000000000 | bytes 200000 | tf_op jit(solution)/shard_map/pallas_call | solution.py:551
  22.5 0.0 collective-permute-done.below_ref
  22.5 2.1 all-to-all-done
  24.7 1.5 shard_map.168
  26.1 5.2 %all-to-all-start.1 = ((f32[16,24,128]{2,1,0:T(8,128)}), f32[16,24,128]{2,1,0:T(8,128)S(1)}, u32[]{:S(2)}, u32[]{:S(2)}) async-start(f32[16,24,128]{2,1,0:T(8,128)} %bitcast.11), calls=%async_computation.1 | async-start | bytes 393216 | tf_op jit(solution)/shard_map/all_to_all | solution.py:570
  31.4 50.0 %all-gather = s32[128,1,1024]{2,1,0:T(1,128)S(1)} all-gather(s32[4,1,1024]{2,1,0:T(1,128)S(1)} %copy-done.11), channel_id=2, replica_groups=mesh['lam'=32,'dom'=16] {'lam'}, dimensions={0}, use_global_device_ids=true | all-gather | bytes 540672 | tf_op jit(solution)/shard_map/all_gather | solution.py:596
  81.4 0.0 copy-start.5
  81.4 6.0 %shard_map.169.short_ref = f32[8,1024]{1,0:T(8,128)S(1)} custom-call(f32[1]{0:T(128)S(6)} %copy.18.lam_ref, s32[6,1,8]{2,1,0:T(1,128)S(1)} %bitcast.25, f32[8,1024]{1,0:T(8,128)S(1)} %copy-done.6, f32[8,512]{1,0:T(8,128)S(1)} %collective-permute-done.below_ref, f32[8,512]{1,0:T(8,128)S(1)} %collective-permute-done.1.above_ref, ...), custom_call_target="tpu_custom_call" | custom-call | flops 2000000000 | bytes 200000 | tf_op jit(solution)/shard_map/pallas_call | solution.py:551
  87.4 1.8 shard_map.170
  89.2 0.0 collective-permute-start.2
  89.2 3.0 %collective-permute-start.3 = (f32[8,512]{1,0:T(8,128)S(1)}, f32[8,512]{1,0:T(8,128)S(1)}, u32[]{:S(2)}, u32[]{:S(2)}) collective-permute-start(f32[8,512]{1,0:T(8,128)S(1)} %get-tuple-element.34), channel_id=1, source_target_pairs={{0,15},{1,0},{2,1},{3,2},{4,3},{5,4},{6,5},{7,6},{8,7},{9,8},{10,9... | collective-permute-start | bytes 49160 | tf_op jit(solution)/shard_map/ppermute | solution.py:565
  92.2 5.7 %shard_map.171.partial_ref = f32[8,1024]{1,0:T(8,128)S(1)} custom-call(f32[1]{0:T(128)S(6)} %copy.18.lam_ref, s32[6,1,8]{2,1,0:T(1,128)S(1)} %bitcast.26, f32[8,1024]{1,0:T(8,128)S(1)} %get-tuple-element.32.data_ref), custom_call_target="tpu_custom_call" | custom-call | flops 2000000000 | bytes 200000 | tf_op jit(solution)/shard_map/pallas_call | solution.py:551
  97.9 0.0 collective-permute-done.2.below_ref
  97.9 0.0 collective-permute-done.3.above_ref
  97.9 2.9 %shard_map.172 = (f32[8,1024]{1,0:T(8,128)S(1)}, f32[16,1024]{1,0:T(8,128)S(1)}, f32[8,512]{1,0:T(8,128)S(1)}, f32[8,512]{1,0:T(8,128)S(1)}, f32[3,1,1024]{2,1,0:T(1,128)S(1)}) custom-call(f32[1]{0:T(128)S(6)} %copy.18.lam_ref, f32[8,1024]{1,0:T(8,128)S(1)} %get-tuple-element.32.data_ref, f32[8,512]{1,0:T(8,128)S(1)} %collective-permute-done.2.below_ref, ...), custom_call_target="tpu_custom_call" | custom-call | bytes 200000 | tf_op jit(solution)/shard_map/pallas_call | solution.py:551
  100.8 0.0 collective-permute-start.4
  100.8 2.9 %collective-permute-start.5 = (f32[8,512]{1,0:T(8,128)S(1)}, f32[8,512]{1,0:T(8,128)S(1)}, u32[]{:S(2)}, u32[]{:S(2)}) collective-permute-start(f32[8,512]{1,0:T(8,128)S(1)} %get-tuple-element.40), channel_id=1, source_target_pairs={{0,15},{1,0},{2,1},{3,2},{4,3},{5,4},{6,5},{7,6},{8,7},{9,8},{10,9... | collective-permute-start | bytes 49160 | tf_op jit(solution)/shard_map/ppermute | solution.py:565
  103.8 5.7 %shard_map.173.partial_ref = f32[8,1024]{1,0:T(8,128)S(1)} custom-call(f32[1]{0:T(128)S(6)} %copy.18.lam_ref, s32[6,1,8]{2,1,0:T(1,128)S(1)} %bitcast.27, f32[8,1024]{1,0:T(8,128)S(1)} %get-tuple-element.38.data_ref), custom_call_target="tpu_custom_call" | custom-call | flops 2000000000 | bytes 200000 | tf_op jit(solution)/shard_map/pallas_call | solution.py:551
  109.5 47.0 %all-gather.1 = f32[96,1,1024]{2,1,0:T(1,128)S(1)} all-gather(f32[3,1,1024]{2,1,0:T(1,128)S(1)} %get-tuple-element.37), channel_id=3, replica_groups=mesh['lam'=32,'dom'=16] {'lam'}, dimensions={0}, use_global_device_ids=true | all-gather | bytes 405504 | tf_op jit(solution)/shard_map/all_gather | solution.py:596
  156.5 0.0 collective-permute-done.5.above_ref
  156.5 2.8 %shard_map.174 = f32[3,1,1024]{2,1,0:T(1,128)S(1)} custom-call(f32[1]{0:T(128)S(6)} %copy.18.lam_ref, f32[8,1024]{1,0:T(8,128)S(1)} %get-tuple-element.38.data_ref, f32[8,512]{1,0:T(8,128)S(1)} %collective-permute-done.4.below_ref, f32[8,512]{1,0:T(8,128)S(1)} %collective-permute-done.5.above_ref, f32[8,1024]{1,0:T(8,128)S(1)} %shard_map.173.partial_ref, ...), custom_call_target="tpu_custom_call" | custom-call | bytes 200000 | tf_op jit(solution)/shard_map/pallas_call | solution.py:551
  159.3 52.6 %all-gather.2 = f32[96,1,1024]{2,1,0:T(1,128)} all-gather(f32[3,1,1024]{2,1,0:T(1,128)S(1)} %shard_map.174), channel_id=4, replica_groups=mesh['lam'=32,'dom'=16] {'lam'}, dimensions={0}, use_global_device_ids=true | all-gather | bytes 405504 | tf_op jit(solution)/shard_map/all_gather | solution.py:596
  211.9 2.9 %shard_map.175 = (s32[3,1,1024]{2,1,0:T(1,128)}, f32[3,1,1024]{2,1,0:T(1,128)}, f32[3,1,1024]{2,1,0:T(1,128)}) custom-call(s32[32,4,1,1024]{3,2,1,0:T(1,128)} %bitcast.19, f32[32,3,1,1024]{3,2,1,0:T(1,128)} %bitcast.21, f32[32,3,1,1024]{3,2,1,0:T(1,128)} %bitcast.28), custom_call_target="tpu_custom_call" | custom-call | bytes 200000 | tf_op jit(solution)/shard_map/pallas_call | solution.py:551
  (25 shorter events, 0.1 us)
Async XLA Ops:
  4.1 10.6 %copy-start.13 = (f32[8,512]{1,0:T(8,128)S(1)}, f32[8,512]{1,0:T(8,128)}, u32[]{:S(2)}) copy-start(f32[8,512]{1,0:T(8,128)} %get-tuple-element.28) | copy-start | bytes 49156
  4.1 11.1 %copy-start.12 = (f32[8,512]{1,0:T(8,128)S(1)}, f32[8,512]{1,0:T(8,128)}, u32[]{:S(2)}) copy-start(f32[8,512]{1,0:T(8,128)} %get-tuple-element.29) | copy-start | bytes 49156
  4.1 13.6 %copy-start.6 = (f32[8,1024]{1,0:T(8,128)S(1)}, f32[8,1024]{1,0:T(8,128)}, u32[]{:S(2)}) copy-start(f32[8,1024]{1,0:T(8,128)} %get-tuple-element.26.data_ref) | copy-start | bytes 98308
  4.1 13.6 %copy-start.8 = (f32[128,8]{1,0:T(8,128)S(1)}, f32[128,8]{1,0:T(8,128)}, u32[]{:S(2)}) copy-start(f32[128,8]{1,0:T(8,128)} %constant.12.clone.rows_ref) | copy-start | bytes 12292
  4.1 13.6 %copy-start.9 = (f32[17,65]{1,0:T(8,128)S(1)}, f32[17,65]{1,0:T(8,128)}, u32[]{:S(2)}) copy-start(f32[17,65]{1,0:T(8,128)} %constant.11.clone.weights_ref) | copy-start | bytes 13264
  4.1 20.5 %all-to-all-start = ((f32[16,24,128]{2,1,0:T(8,128)}), f32[16,24,128]{2,1,0:T(8,128)S(1)}, u32[]{:S(2)}, u32[]{:S(2)}) async-start(f32[16,24,128]{2,1,0:T(8,128)} %bitcast.29), calls=%async_computation | async-start | bytes 393216 | tf_op jit(solution)/shard_map/all_to_all | solution.py:570
  14.7 3.0 %copy-start.10 = (f32[8,128]{1,0:T(8,128)S(1)}, f32[8,128]{1,0:T(8,128)}, u32[]{:S(2)}) copy-start(f32[8,128]{1,0:T(8,128)} %constant.13.clone.lanes_ref) | copy-start | bytes 12292
  14.7 3.0 %copy-start.7 = (s32[1,8,6]{1,0,2:T(1,128)S(1)}, s32[1,8,6]{1,0,2:T(1,128)}, u32[]{:S(2)}) copy-start(s32[1,8,6]{1,0,2:T(1,128)} %param.22) | copy-start | bytes 580
  14.7 7.8 %collective-permute-start = (f32[8,512]{1,0:T(8,128)S(1)}, f32[8,512]{1,0:T(8,128)S(1)}, u32[]{:S(2)}, u32[]{:S(2)}) collective-permute-start(f32[8,512]{1,0:T(8,128)S(1)} %copy-done.13), channel_id=1, source_target_pairs={{0,1},{1,2},{2,3},{3,4},{4,5},{5,6},{6,7},{7,8},{8,9},{9,10},{10,1... | collective-permute-start | bytes 49160 | tf_op jit(solution)/shard_map/ppermute | solution.py:564
  15.2 7.3 %collective-permute-start.1 = (f32[8,512]{1,0:T(8,128)S(1)}, f32[8,512]{1,0:T(8,128)S(1)}, u32[]{:S(2)}, u32[]{:S(2)}) collective-permute-start(f32[8,512]{1,0:T(8,128)S(1)} %copy-done.12), channel_id=1, source_target_pairs={{0,15},{1,0},{2,1},{3,2},{4,3},{5,4},{6,5},{7,6},{8,7},{9,8},{10,9... | collective-permute-start | bytes 49160 | tf_op jit(solution)/shard_map/ppermute | solution.py:565
  17.7 6.9 %copy-start.2 = (bf16[512,128]{1,0:T(8,128)(2,1)S(1)}, bf16[512,128]{1,0:T(8,128)(2,1)}, u32[]{:S(2)}) copy-start(bf16[512,128]{1,0:T(8,128)(2,1)} %constant.14.clone.basis_ref) | copy-start | bytes 393220
  26.1 5.2 %copy-start.11 = (s32[4,1,1024]{2,1,0:T(1,128)S(1)}, s32[4,1,1024]{2,1,0:T(1,128)}, u32[]{:S(2)}) copy-start(s32[4,1,1024]{2,1,0:T(1,128)} %get-tuple-element.24) | copy-start | bytes 49156
  26.1 61.3 %all-to-all-start.1 = ((f32[16,24,128]{2,1,0:T(8,128)}), f32[16,24,128]{2,1,0:T(8,128)S(1)}, u32[]{:S(2)}, u32[]{:S(2)}) async-start(f32[16,24,128]{2,1,0:T(8,128)} %bitcast.11), calls=%async_computation.1 | async-start | bytes 393216 | tf_op jit(solution)/shard_map/all_to_all | solution.py:570
  81.4 16.5 %copy-start = (s32[128,1,1024]{2,1,0:T(1,128)}, s32[128,1,1024]{2,1,0:T(1,128)S(1)}, u32[]{:S(2)}) copy-start(s32[128,1,1024]{2,1,0:T(1,128)S(1)} %all-gather) | copy-start | bytes 1572868
  81.4 6.0 %copy-start.3 = (f32[32,32]{1,0:T(8,128)S(1)}, f32[32,32]{1,0:T(8,128)}, u32[]{:S(2)}) copy-start(f32[32,32]{1,0:T(8,128)} %constant.10.clone.slab_hbm.slab_ref) | copy-start | bytes 12292
  81.4 6.0 %copy-start.4 = (f32[16,1024]{1,0:T(8,128)S(1)}, f32[16,1024]{1,0:T(8,128)}, u32[]{:S(2)}) copy-start(f32[16,1024]{1,0:T(8,128)} %get-tuple-element.30.move_ref) | copy-start | bytes 196612
  81.4 6.0 %copy-start.5 = (s32[1,2,512]{2,1,0:T(2,128)S(1)}, s32[1,2,512]{2,1,0:T(2,128)}, u32[]{:S(2)}) copy-start(s32[1,2,512]{2,1,0:T(2,128)} %lists_ref.3) | copy-start | bytes 12292
  89.2 8.7 %collective-permute-start.2 = (f32[8,512]{1,0:T(8,128)S(1)}, f32[8,512]{1,0:T(8,128)S(1)}, u32[]{:S(2)}, u32[]{:S(2)}) collective-permute-start(f32[8,512]{1,0:T(8,128)S(1)} %get-tuple-element.33), channel_id=1, source_target_pairs={{0,1},{1,2},{2,3},{3,4},{4,5},{5,6},{6,7},{7,8},{8,9},{9,10},{10,1... | collective-permute-start | bytes 49160 | tf_op jit(solution)/shard_map/ppermute | solution.py:564
  89.2 8.7 %collective-permute-start.3 = (f32[8,512]{1,0:T(8,128)S(1)}, f32[8,512]{1,0:T(8,128)S(1)}, u32[]{:S(2)}, u32[]{:S(2)}) collective-permute-start(f32[8,512]{1,0:T(8,128)S(1)} %get-tuple-element.34), channel_id=1, source_target_pairs={{0,15},{1,0},{2,1},{3,2},{4,3},{5,4},{6,5},{7,6},{8,7},{9,8},{10,9... | collective-permute-start | bytes 49160 | tf_op jit(solution)/shard_map/ppermute | solution.py:565
  100.8 55.7 %collective-permute-start.4 = (f32[8,512]{1,0:T(8,128)S(1)}, f32[8,512]{1,0:T(8,128)S(1)}, u32[]{:S(2)}, u32[]{:S(2)}) collective-permute-start(f32[8,512]{1,0:T(8,128)S(1)} %get-tuple-element.39), channel_id=1, source_target_pairs={{0,1},{1,2},{2,3},{3,4},{4,5},{5,6},{6,7},{7,8},{8,9},{9,10},{10,1... | collective-permute-start | bytes 49160 | tf_op jit(solution)/shard_map/ppermute | solution.py:564
  100.8 55.6 %collective-permute-start.5 = (f32[8,512]{1,0:T(8,128)S(1)}, f32[8,512]{1,0:T(8,128)S(1)}, u32[]{:S(2)}, u32[]{:S(2)}) collective-permute-start(f32[8,512]{1,0:T(8,128)S(1)} %get-tuple-element.40), channel_id=1, source_target_pairs={{0,15},{1,0},{2,1},{3,2},{4,3},{5,4},{6,5},{7,6},{8,7},{9,8},{10,9... | collective-permute-start | bytes 49160 | tf_op jit(solution)/shard_map/ppermute | solution.py:565
  156.5 55.5 %copy-start.1 = (f32[96,1,1024]{2,1,0:T(1,128)}, f32[96,1,1024]{2,1,0:T(1,128)S(1)}, u32[]{:S(2)}) copy-start(f32[96,1,1024]{2,1,0:T(1,128)S(1)} %all-gather.1) | copy-start | bytes 1179652

commit v3 on v2

--- a/solution.py
+++ b/solution.py
@@ -162,9 +162,8 @@
     for c in SCREEN[1:]:
         screen = screen * w + c
     gauss = jnp.exp2(s * (-(EWALD_BETA**2) * math.log2(math.e)))
-    a = LJ_SIGMA_SQ * u
-    t = a * a * a
-    g = u * ((qa * qb) * (gauss * screen) + (wa * wb) * (t * (t - 0.5)))
+    t = u * u * u
+    g = u * ((qa * qb) * (gauss * screen) + (wa * wb) * (t * (t - 0.5 / LJ_SIGMA_SQ**3)))
     return g * dx, g * dy, g * dz
 
 
@@ -175,7 +174,7 @@
     columns = pl.ds(start, CLUSTER)
     xyz = [spread(turns[i : i + 1, columns].astype(jnp.int32)) for i in range(3)]
     q = spread(data_ref[3:4, columns] * (2.0 * COULOMB))
-    w = spread(data_ref[4:5, columns] * (48.0 * LJ_DEPTH))
+    w = spread(data_ref[4:5, columns] * (48.0 * LJ_DEPTH * LJ_SIGMA_SQ**6))
     return (*xyz, q, w)
 
 
@@ -196,7 +195,7 @@
 
 def spread_kernel(
     lam_ref, cells_hbm, off_hbm, vel_hbm, charge_hbm, coup_hbm, mass_hbm, lists_hbm, slab_hbm, flag_hbm,
-    out_ref, data_ref, move_ref, low_ref, high_ref, ladder_ref, mixed_high, mixed_low,
+    out_ref, data_ref, move_ref, low_ref, high_ref, mixed_high, mixed_low,
     cells_ref, off_ref, vel_ref, charge_ref, coup_ref, mass_ref, lists_ref, slab_ref, flag_ref, arrived,
 ):
     copies = [
@@ -222,7 +221,8 @@
         move_ref[3 + i : 4 + i, :] = cell
         move_ref[8 + i : 9 + i, :] = vel_ref[i]
         data_ref[i : i + 1, :] = cell + off_ref[i]
-    move_ref[6:8, :] = jnp.zeros((2, A_DEV), F32)
+    move_ref[6:7, :] = jnp.broadcast_to(flag_ref[0:1, 0:1].astype(F32), (1, A_DEV))
+    move_ref[7:8, :] = jnp.broadcast_to(flag_ref[0:1, 1:2].astype(F32), (1, A_DEV))
     move_ref[11:16, :] = jnp.zeros((5, A_DEV), F32)
     data_ref[3:4, :] = charge
     data_ref[4:5, :] = weight
@@ -232,10 +232,6 @@
 
     off = move_ref[0:3, :]
     cells = [cells_ref[i] for i in range(3)]
-    for i in range(3):
-        ladder_ref[i] = cells[i]
-    half = lax.broadcasted_iota(jnp.int32, (1, A_DEV), 1) < A_DEV // 2
-    ladder_ref[3] = jnp.where(half, flag_ref[0:1, 0:1], flag_ref[0:1, 1:2])
     weights, _ = spline_set(off)
     row = iota_rows(16, A_DEV)
     plane = jnp.where(row < 8, row, 8 + (row & 3))
@@ -432,7 +428,7 @@
     add_halo_forces(lam_ref, data_ref, below_ref, above_ref, second, force_ref, turns)
 
 
-def advance(force, kicks, data_ref, move_ref, lists_ref, data_out, move_out, low_ref, high_ref, off_ref=None):
+def advance(force, kicks, data_ref, move_ref, lists_ref, data_out, move_out, low_ref, high_ref):
     mass = data_ref[5:6, :]
     velocity = move_ref[8:11, :]
     for _ in range(kicks):
@@ -443,9 +439,6 @@
     move_out[8:11, :] = velocity
     data_out[...] = data_ref[...]
     data_out[0:3, :] = move_ref[3:6, :] + off
-    if off_ref is not None:
-        for i in range(3):
-            off_ref[i] = off[i : i + 1]
     write_halo(data_out[...], lists_ref, low_ref, high_ref)
 
 
@@ -500,44 +493,46 @@
 
 
 def halo_step_kernel(
-    lam_ref, data_ref, below_ref, above_ref, partial_ref, long_ref, move_ref, lists_ref, ladder_ref,
-    data_out, move_out, low_ref, high_ref, off_ref, turns, force,
+    lam_ref, data_ref, below_ref, above_ref, partial_ref, long_ref, move_ref, lists_ref,
+    data_out, move_out, low_ref, high_ref, turns, force,
 ):
-    del ladder_ref
     add_halo_forces(lam_ref, data_ref, below_ref, above_ref, partial_ref, force, turns)
     total = force[0:3, :] + long_ref[0:3, :]
-    advance(total, 2, data_ref, move_ref, lists_ref, data_out, move_out, low_ref, high_ref, off_ref)
+    advance(total, 2, data_ref, move_ref, lists_ref, data_out, move_out, low_ref, high_ref)
 
 
 def halo_last_kernel(
-    lam_ref, data_ref, below_ref, above_ref, partial_ref, long_ref, move_ref, offsets_ref, velocity_ref, turns, force
+    lam_ref, data_ref, below_ref, above_ref, partial_ref, long_ref, move_ref, state_ref, turns, force
 ):
-    del offsets_ref
     add_halo_forces(lam_ref, data_ref, below_ref, above_ref, partial_ref, force, turns)
     total = force[0:3, :] + long_ref[0:3, :]
     velocity = move_ref[8:11, :] + 0.5 * STEP_DT * total * data_ref[5:6, :]
     for i in range(3):
-        velocity_ref[i] = velocity[i : i + 1]
-
-
-def settle_kernel(ladder_ref, offsets_ref, vel_hbm, cells_ref, off_ref, vel_ref, arrived, done):
-    window = lax.axis_index("lam")
-    windows = lax.axis_size("lam")
-
-    def partner(w, round_index):
-        low = jnp.where(w % 2 == round_index % 2, w, w - 1)
-        inside = jnp.logical_and(low >= 0, low + 1 < windows)
-        flag = jnp.max(ladder_ref[jnp.maximum(low, 0), 3, :, round_index * (A_DEV // 2) : (round_index + 1) * (A_DEV // 2)])
-        return jnp.where(jnp.logical_and(inside, flag == 1), 2 * low + 1 - w, w)
-
-    source = partner(partner(window, 1), 0)
-    copy = pltpu.make_async_copy(vel_hbm.at[source], arrived, done)
-    copy.start()
-    for i in range(3):
-        cells_ref[i] = ladder_ref[source, i]
-        off_ref[i] = offsets_ref[source, i]
-    copy.wait()
-    vel_ref[...] = arrived[...]
+        state_ref[i] = move_ref[i : i + 1, :]
+        state_ref[3 + i] = velocity[i : i + 1]
+        state_ref[6 + i] = move_ref[3 + i : 4 + i, :]
+    for i in range(2):
+        state_ref[9 + i] = move_ref[6 + i : 7 + i, :]
+
+
+def settle_kernel(here_ref, third_ref, second_ref, first_ref, cells_ref, off_ref, vel_ref):
+    even = lax.axis_index("lam") % 2 == 0
+    inside = lax.axis_index("lam") + 1 < lax.axis_size("lam")
+    outer = jnp.where(even, second_ref[10], jnp.where(inside, here_ref[10], 0.0)) == 1.0
+    far = jnp.where(even, third_ref[9], second_ref[9]) == 1.0
+    close = jnp.where(even, here_ref[9], first_ref[9]) == 1.0
+    for i in range(9):
+        row = jnp.where(
+            outer,
+            jnp.where(far, third_ref[i], second_ref[i]),
+            jnp.where(close, first_ref[i], here_ref[i]),
+        )
+        if i < 3:
+            off_ref[i] = row
+        elif i < 6:
+            vel_ref[i - 3] = row
+        else:
+            cells_ref[i - 6] = row.astype(jnp.int32)
 
 
 PLACES = {
@@ -564,6 +559,18 @@
     below = lax.ppermute(high, "dom", [(i, (i + 1) % size) for i in range(size)])
     above = lax.ppermute(low, "dom", [(i, (i - 1) % size) for i in range(size)])
     return below, above
+
+
+def ladder_states(state):
+    windows = lax.axis_size("lam")
+    pairs = [(w - 2, w) for w in range(2, windows, 2)] + [(w + 2, w) for w in range(1, windows - 2, 2)]
+    received = [lax.ppermute(state, "lam", pairs)]
+    for offset in (1, 0):
+        pairs = []
+        for w in range(offset, windows - 1, 2):
+            pairs += [(w, w + 1), (w + 1, w)]
+        received.append(lax.ppermute(state, "lam", pairs))
+    return received
 
 
 def exchanged(value):
@@ -592,18 +599,15 @@
     def by_row(x):
         return jnp.transpose(x, (1, 0, 2))
 
-    def everywhere(x):
-        return lax.all_gather(x, "lam", axis=0, tiled=False)
-
-
-    grid, data, move, low, high, ladder = call(
+
+    grid, data, move, low, high = call(
         spread_kernel,
         [
             ("s", lambdas), ("a", by_row(cells)), ("a", by_row(offsets)), ("a", by_row(velocities)),
             ("a", charges[None]), ("a", coupling[None]), ("a", inverse_mass[None]), ("a", halo_lists), ("a", slab),
             ("a", accept_flags.T),
         ],
-        [((ROWS, K), F32), wide, moving, border, border, ((4, 1, A_DEV), jnp.int32)],
+        [((ROWS, K), F32), wide, moving, border, border],
         [
             pltpu.VMEM((ROWS, A_DEV), BF16), pltpu.VMEM((ROWS, A_DEV), BF16),
             pltpu.VMEM((3, 1, A_DEV), jnp.int32), pltpu.VMEM((3, 1, A_DEV), F32), pltpu.VMEM((3, 1, A_DEV), F32),
@@ -613,7 +617,6 @@
         ],
         limit=60,
     )
-    ladder = everywhere(ladder)
     grid = exchanged(grid)
     below, above = neighbours(low, high)
     short, gain = call(
@@ -655,33 +658,29 @@
 
     below, above = neighbours(low, high)
     short = own_call(data)
-    data, move, low, high, offset = call(
+    data, move, low, high = call(
         halo_step_kernel,
         [
             ("s", lambdas), ("v", data), ("v", below), ("v", above), ("v", short), ("v", far), ("v", move),
-            ("v", halo_lists), ("a", ladder),
+            ("v", halo_lists),
         ],
-        [wide, moving, border, border, (triple, F32)],
+        [wide, moving, border, border],
         [turns, spare],
     )
-    all_offsets = everywhere(offset)
     below, above = neighbours(low, high)
     short = own_call(data)
-    (velocity,) = call(
+    (state,) = call(
         halo_last_kernel,
         [
             ("s", lambdas), ("v", data), ("v", below), ("v", above), ("v", short), ("v", far), ("v", move),
-            ("a", all_offsets),
         ],
-        [(triple, F32)],
+        [((11, 1, A_DEV), F32)],
         [turns, spare],
     )
     out = call(
         settle_kernel,
-        [("v", ladder), ("v", all_offsets), ("a", everywhere(velocity))],
+        [("v", state), *(("v", x) for x in ladder_states(state))],
         [(triple, jnp.int32), (triple, F32), (triple, F32)],
-        [pltpu.VMEM(triple, F32), pltpu.SemaphoreType.DMA],
-        limit=60,
     )
     return tuple(by_row(x) for x in out)
 

time: 215 us -> 84.6 us (0.39)
  the two profiles are of different devices: /device:TPU:16 before, /device:TPU:30 now
where the time goes in v3:
time: 84.6 us; the launch traced here: 84 us
  starting transfers between devices  34.4 us (41%)
  Pallas kernels  34.2 us (40%)
  waiting for transfers between devices  13.8 us (16%)
  between operations  1.52 us (2%)
    pallas_call x10, Pallas kernels, call(): pl.pallas_call(kernel, out_shape=[jax.ShapeDtypeStruct(shape, dtype) for...  34.2 us
    all_to_all x2, starting transfers between devices, exchanged(): return lax.all_to_all(value, 'dom', split_axis=0, concat_axis=0, tiled=True)  15.6 us
    ppermute x2, starting transfers between devices, ladder_states(): received.append(lax.ppermute(state, 'lam', pairs))  8.01 us
    ppermute x3, starting transfers between devices, neighbours(): above = lax.ppermute(low, 'dom', [(i, (i - 1) % size) for i in range(size)])  7.67 us
    all_to_all x2, waiting for transfers between devices, exchanged(): return lax.all_to_all(value, 'dom', split_axis=0, concat_axis=0, tiled=True)  6.16 us
    ppermute x1, waiting for transfers between devices, ladder_states(): received = [lax.ppermute(state, 'lam', pairs)]  5.57 us
    ppermute x2, waiting for transfers between devices, ladder_states(): received.append(lax.ppermute(state, 'lam', pairs))  2.05 us
    ppermute x1, starting transfers between devices, ladder_states(): received = [lax.ppermute(state, 'lam', pairs)]  1.92 us
  transfers between devices with their start and end apart: 11, of which 4 were waited for; matrix products, arithmetic and copies ran while one was open for 0% of the time, Pallas kernels for 26%

profile of v3, /device:TPU:30, one launch (start us, length us, event | category | flops | bytes accessed | tf_op | source)
XLA Modules:
  0.0 84.0 jit_solution(7635747209661638953)
XLA Ops:
  1.3 2.8 %shard_map.166 = (f32[384,128]{1,0:T(8,128)}, f32[8,1024]{1,0:T(8,128)}, f32[16,1024]{1,0:T(8,128)}, f32[8,512]{1,0:T(8,128)}, f32[8,512]{1,0:T(8,128)}) custom-call(f32[1]{0:T(128)S(6)} %copy.18.lam_ref, s32[3,1,1024]{2,1,0:T(1,128)} %bitcast.22, f32[3,1,1024]{2,1,0:T(1,128)} %bitcast.23, f32[3,1,1024]{2,1,0:T(1,128)} %bitcast.24, f32[1,1024]{1,0:T(1,128)} %bitcast.25, ...), custom_call_target="tpu_custom_call" | custom-call | bytes 200000 | tf_op jit(solution)/shard_map/pallas_call | solution.py:546
  4.1 0.0 copy-start.6
  4.1 0.0 copy-start.7
  4.1 10.6 %all-to-all-start = ((f32[16,24,128]{2,1,0:T(8,128)}), f32[16,24,128]{2,1,0:T(8,128)S(1)}, u32[]{:S(2)}, u32[]{:S(2)}) async-start(f32[16,24,128]{2,1,0:T(8,128)} %bitcast.21), calls=%async_computation | async-start | bytes 393216 | tf_op jit(solution)/shard_map/all_to_all | solution.py:577
  14.7 0.0 copy-start.8
  14.7 0.4 collective-permute-start
  15.2 2.6 %collective-permute-start.1 = (f32[8,512]{1,0:T(8,128)S(1)}, f32[8,512]{1,0:T(8,128)S(1)}, u32[]{:S(2)}, u32[]{:S(2)}) collective-permute-start(f32[8,512]{1,0:T(8,128)S(1)} %copy-done.9), channel_id=1, source_target_pairs={{0,15},{1,0},{2,1},{3,2},{4,3},{5,4},{6,5},{7,6},{8,7},{9,8},{10,9... | collective-permute-start | bytes 49160 | tf_op jit(solution)/shard_map/ppermute | solution.py:560
  17.7 0.0 copy-start
  17.7 4.7 %shard_map.167 = (f32[8,1024]{1,0:T(8,128)S(1)}, f32[2,128,128]{2,1,0:T(8,128)S(1)}) custom-call(f32[1]{0:T(128)S(6)} %copy.18.lam_ref, s32[6,1,8]{2,1,0:T(1,128)S(1)} %bitcast.17, f32[17,65]{1,0:T(8,128)S(1)} %copy-done.7, f32[8,1024]{1,0:T(8,128)S(1)} %copy-done.4, f32[128,8]{1,0:T(8,128)S(1)} %copy-done.6, f32[8,128]{1,0:T(8,128)S(1)} %copy-done.8), custom_call_target="tpu_custom_call" | custom-call | flops 2000000000 | bytes 200000 | tf_op jit(solution)/shard_map/pallas_call | solution.py:546
  22.5 0.0 collective-permute-done.below_ref
  22.5 2.2 %all-to-all-done = f32[16,24,128]{2,1,0:T(8,128)S(1)} async-done(((f32[16,24,128]{2,1,0:T(8,128)}), f32[16,24,128]{2,1,0:T(8,128)S(1)}, u32[]{:S(2)}, u32[]{:S(2)}) %all-to-all-start) | async-done | bytes 196640 | tf_op jit(solution)/shard_map/all_to_all | solution.py:577
  24.7 1.5 %shard_map.168 = f32[384,128]{1,0:T(8,128)} custom-call(f32[384,128]{1,0:T(8,128)S(1)} %bitcast.15, f32[2,128,128]{2,1,0:T(8,128)S(1)} %get-tuple-element.24.gain_ref, bf16[512,128]{1,0:T(8,128)(2,1)S(1)} %copy-done, f32[8,512]{1,0:T(8,128)S(1)} %collective-permute-done.below_ref, f32[8,512]{1,0:T(8,128)S(1)} %collective-permute-done.1.above_ref), custom_call_target="tpu_custom_call" | custom-call | bytes 200000 | tf_op jit(solution)/shard_map/pallas_call | solution.py:546
  26.1 5.1 %all-to-all-start.1 = ((f32[16,24,128]{2,1,0:T(8,128)}), f32[16,24,128]{2,1,0:T(8,128)S(1)}, u32[]{:S(2)}, u32[]{:S(2)}) async-start(f32[16,24,128]{2,1,0:T(8,128)} %bitcast.10), calls=%async_computation.1 | async-start | bytes 393216 | tf_op jit(solution)/shard_map/all_to_all | solution.py:577
  31.2 0.0 copy-start.1
  31.2 0.0 copy-start.3
  31.2 5.9 %shard_map.169.short_ref = f32[8,1024]{1,0:T(8,128)S(1)} custom-call(f32[1]{0:T(128)S(6)} %copy.18.lam_ref, s32[6,1,8]{2,1,0:T(1,128)S(1)} %bitcast.18, f32[8,1024]{1,0:T(8,128)S(1)} %copy-done.4, f32[8,512]{1,0:T(8,128)S(1)} %collective-permute-done.below_ref, f32[8,512]{1,0:T(8,128)S(1)} %collective-permute-done.1.above_ref, ...), custom_call_target="tpu_custom_call" | custom-call | flops 2000000000 | bytes 200000 | tf_op jit(solution)/shard_map/pallas_call | solution.py:546
  37.2 4.0 %all-to-all-done.1 = f32[16,24,128]{2,1,0:T(8,128)S(1)} async-done(((f32[16,24,128]{2,1,0:T(8,128)}), f32[16,24,128]{2,1,0:T(8,128)S(1)}, u32[]{:S(2)}, u32[]{:S(2)}) %all-to-all-start.1) | async-done | bytes 196640 | tf_op jit(solution)/shard_map/all_to_all | solution.py:577
  41.2 1.8 %shard_map.170 = (f32[8,1024]{1,0:T(8,128)S(1)}, f32[8,1024]{1,0:T(8,128)S(1)}, f32[16,1024]{1,0:T(8,128)S(1)}, f32[8,512]{1,0:T(8,128)S(1)}, f32[8,512]{1,0:T(8,128)S(1)}) custom-call(f32[384,128]{1,0:T(8,128)S(1)} %bitcast.16, f32[8,1024]{1,0:T(8,128)S(1)} %copy-done.4, f32[16,1024]{1,0:T(8,128)S(1)} %copy-done.2, f32[8,1024]{1,0:T(8,128)S(1)} %shard_map.169.short_ref, ...), custom_call_target="tpu_custom_call" | custom-call | bytes 200000 | tf_op jit(solution)/shard_map/pallas_call | solution.py:546
  43.0 0.8 collective-permute-start.2
  43.8 2.2 %collective-permute-start.3 = (f32[8,512]{1,0:T(8,128)S(1)}, f32[8,512]{1,0:T(8,128)S(1)}, u32[]{:S(2)}, u32[]{:S(2)}) collective-permute-start(f32[8,512]{1,0:T(8,128)S(1)} %get-tuple-element.31), channel_id=1, source_target_pairs={{0,15},{1,0},{2,1},{3,2},{4,3},{5,4},{6,5},{7,6},{8,7},{9,8},{10,9... | collective-permute-start | bytes 49160 | tf_op jit(solution)/shard_map/ppermute | solution.py:560
  45.9 5.6 %shard_map.171.partial_ref = f32[8,1024]{1,0:T(8,128)S(1)} custom-call(f32[1]{0:T(128)S(6)} %copy.18.lam_ref, s32[6,1,8]{2,1,0:T(1,128)S(1)} %bitcast.19, f32[8,1024]{1,0:T(8,128)S(1)} %get-tuple-element.29.data_ref), custom_call_target="tpu_custom_call" | custom-call | flops 2000000000 | bytes 200000 | tf_op jit(solution)/shard_map/pallas_call | solution.py:546
  51.6 2.8 %shard_map.172 = (f32[8,1024]{1,0:T(8,128)S(1)}, f32[16,1024]{1,0:T(8,128)S(1)}, f32[8,512]{1,0:T(8,128)S(1)}, f32[8,512]{1,0:T(8,128)S(1)}) custom-call(f32[1]{0:T(128)S(6)} %copy.18.lam_ref, f32[8,1024]{1,0:T(8,128)S(1)} %get-tuple-element.29.data_ref, f32[8,512]{1,0:T(8,128)S(1)} %collective-permute-done.2.below_ref, ...), custom_call_target="tpu_custom_call" | custom-call | bytes 200000 | tf_op jit(solution)/shard_map/pallas_call | solution.py:546
  54.4 0.0 collective-permute-start.4
  54.5 2.9 %collective-permute-start.5 = (f32[8,512]{1,0:T(8,128)S(1)}, f32[8,512]{1,0:T(8,128)S(1)}, u32[]{:S(2)}, u32[]{:S(2)}) collective-permute-start(f32[8,512]{1,0:T(8,128)S(1)} %get-tuple-element.36), channel_id=1, source_target_pairs={{0,15},{1,0},{2,1},{3,2},{4,3},{5,4},{6,5},{7,6},{8,7},{9,8},{10,9... | collective-permute-start | bytes 49160 | tf_op jit(solution)/shard_map/ppermute | solution.py:560
  57.4 5.6 %shard_map.173.partial_ref = f32[8,1024]{1,0:T(8,128)S(1)} custom-call(f32[1]{0:T(128)S(6)} %copy.18.lam_ref, s32[6,1,8]{2,1,0:T(1,128)S(1)} %bitcast.20, f32[8,1024]{1,0:T(8,128)S(1)} %get-tuple-element.34.data_ref), custom_call_target="tpu_custom_call" | custom-call | flops 2000000000 | bytes 200000 | tf_op jit(solution)/shard_map/pallas_call | solution.py:546
  63.1 2.7 %shard_map.174.here_ref = f32[11,1,1024]{2,1,0:T(1,128)S(1)} custom-call(f32[1]{0:T(128)S(6)} %copy.18.lam_ref, f32[8,1024]{1,0:T(8,128)S(1)} %get-tuple-element.34.data_ref, f32[8,512]{1,0:T(8,128)S(1)} %collective-permute-done.4.below_ref, f32[8,512]{1,0:T(8,128)S(1)} %collective-permute-done.5.above_ref, f32[8,1024]{1,0:T(8,128)S(1)} %shard_map.173.partial_ref, ...), custom_call_target="tpu_custom_call" | custom-call | bytes 200000 | tf_op jit(solution)/shard_map/pallas_call | solution.py:546
  65.8 2.7 %collective-permute-start.8 = (f32[11,1,1024]{2,1,0:T(1,128)S(1)}, f32[11,1,1024]{2,1,0:T(1,128)S(1)}, u32[]{:S(2)}, u32[]{:S(2)}) collective-permute-start(f32[11,1,1024]{2,1,0:T(1,128)S(1)} %shard_map.174.here_ref), channel_id=1, source_target_pairs={{0,16},{16,0},{32,48},{48,32},{64,80},{80,64},{96,112},{112,96},{1... | collective-permute-start | bytes 135176 | tf_op jit(solution)/shard_map/ppermute | solution.py:572
  68.6 5.3 %collective-permute-start.7 = (f32[11,1,1024]{2,1,0:T(1,128)S(1)}, f32[11,1,1024]{2,1,0:T(1,128)S(1)}, u32[]{:S(2)}, u32[]{:S(2)}) collective-permute-start(f32[11,1,1024]{2,1,0:T(1,128)S(1)} %shard_map.174.here_ref), channel_id=1, source_target_pairs={{16,32},{32,16},{48,64},{64,48},{80,96},{96,80},{112,128},{128,112... | collective-permute-start | bytes 135176 | tf_op jit(solution)/shard_map/ppermute | solution.py:572
  73.8 1.9 %collective-permute-start.6 = (f32[11,1,1024]{2,1,0:T(1,128)S(1)}, f32[11,1,1024]{2,1,0:T(1,128)S(1)}, u32[]{:S(2)}, u32[]{:S(2)}) collective-permute-start(f32[11,1,1024]{2,1,0:T(1,128)S(1)} %shard_map.174.here_ref), channel_id=1, source_target_pairs={{0,32},{32,64},{64,96},{96,128},{128,160},{160,192},{192,224},{224... | collective-permute-start | bytes 135176 | tf_op jit(solution)/shard_map/ppermute | solution.py:567
  75.8 2.0 %collective-permute-done.7.second_ref = f32[11,1,1024]{2,1,0:T(1,128)S(1)} collective-permute-done((f32[11,1,1024]{2,1,0:T(1,128)S(1)}, f32[11,1,1024]{2,1,0:T(1,128)S(1)}, u32[]{:S(2)}, u32[]{:S(2)}) %collective-permute-start.7) | collective-permute-done | bytes 45088 | tf_op jit(solution)/shard_map/ppermute | solution.py:572
  77.8 5.6 %collective-permute-done.6.third_ref = f32[11,1,1024]{2,1,0:T(1,128)S(1)} collective-permute-done((f32[11,1,1024]{2,1,0:T(1,128)S(1)}, f32[11,1,1024]{2,1,0:T(1,128)S(1)}, u32[]{:S(2)}, u32[]{:S(2)}) %collective-permute-start.6) | collective-permute-done | bytes 45088 | tf_op jit(solution)/shard_map/ppermute | solution.py:567
  83.4 0.6 shard_map.175
  (22 shorter events, 0.1 us)
Async XLA Ops:
  4.1 10.6 %copy-start.10 = (f32[8,512]{1,0:T(8,128)S(1)}, f32[8,512]{1,0:T(8,128)}, u32[]{:S(2)}) copy-start(f32[8,512]{1,0:T(8,128)} %get-tuple-element.25) | copy-start | bytes 49156
  4.1 11.1 %copy-start.9 = (f32[8,512]{1,0:T(8,128)S(1)}, f32[8,512]{1,0:T(8,128)}, u32[]{:S(2)}) copy-start(f32[8,512]{1,0:T(8,128)} %get-tuple-element.26) | copy-start | bytes 49156
  4.1 13.6 %copy-start.4 = (f32[8,1024]{1,0:T(8,128)S(1)}, f32[8,1024]{1,0:T(8,128)}, u32[]{:S(2)}) copy-start(f32[8,1024]{1,0:T(8,128)} %get-tuple-element.23.data_ref) | copy-start | bytes 98308
  4.1 13.6 %copy-start.6 = (f32[128,8]{1,0:T(8,128)S(1)}, f32[128,8]{1,0:T(8,128)}, u32[]{:S(2)}) copy-start(f32[128,8]{1,0:T(8,128)} %constant.12.clone.rows_ref) | copy-start | bytes 12292
  4.1 13.6 %copy-start.7 = (f32[17,65]{1,0:T(8,128)S(1)}, f32[17,65]{1,0:T(8,128)}, u32[]{:S(2)}) copy-start(f32[17,65]{1,0:T(8,128)} %constant.11.clone.weights_ref) | copy-start | bytes 13264
  4.1 20.5 %all-to-all-start = ((f32[16,24,128]{2,1,0:T(8,128)}), f32[16,24,128]{2,1,0:T(8,128)S(1)}, u32[]{:S(2)}, u32[]{:S(2)}) async-start(f32[16,24,128]{2,1,0:T(8,128)} %bitcast.21), calls=%async_computation | async-start | bytes 393216 | tf_op jit(solution)/shard_map/all_to_all | solution.py:577
  14.7 3.0 %copy-start.8 = (f32[8,128]{1,0:T(8,128)S(1)}, f32[8,128]{1,0:T(8,128)}, u32[]{:S(2)}) copy-start(f32[8,128]{1,0:T(8,128)} %constant.13.clone.lanes_ref) | copy-start | bytes 12292
  14.7 3.0 %copy-start.5 = (s32[1,8,6]{1,0,2:T(1,128)S(1)}, s32[1,8,6]{1,0,2:T(1,128)}, u32[]{:S(2)}) copy-start(s32[1,8,6]{1,0,2:T(1,128)} %param.22) | copy-start | bytes 580
  14.7 7.7 %collective-permute-start = (f32[8,512]{1,0:T(8,128)S(1)}, f32[8,512]{1,0:T(8,128)S(1)}, u32[]{:S(2)}, u32[]{:S(2)}) collective-permute-start(f32[8,512]{1,0:T(8,128)S(1)} %copy-done.10), channel_id=1, source_target_pairs={{0,1},{1,2},{2,3},{3,4},{4,5},{5,6},{6,7},{7,8},{8,9},{9,10},{10,1... | collective-permute-start | bytes 49160 | tf_op jit(solution)/shard_map/ppermute | solution.py:559
  15.2 7.3 %collective-permute-start.1 = (f32[8,512]{1,0:T(8,128)S(1)}, f32[8,512]{1,0:T(8,128)S(1)}, u32[]{:S(2)}, u32[]{:S(2)}) collective-permute-start(f32[8,512]{1,0:T(8,128)S(1)} %copy-done.9), channel_id=1, source_target_pairs={{0,15},{1,0},{2,1},{3,2},{4,3},{5,4},{6,5},{7,6},{8,7},{9,8},{10,9... | collective-permute-start | bytes 49160 | tf_op jit(solution)/shard_map/ppermute | solution.py:560
  17.7 6.9 %copy-start = (bf16[512,128]{1,0:T(8,128)(2,1)S(1)}, bf16[512,128]{1,0:T(8,128)(2,1)}, u32[]{:S(2)}) copy-start(bf16[512,128]{1,0:T(8,128)(2,1)} %constant.14.clone.basis_ref) | copy-start | bytes 393220
  26.1 15.0 %all-to-all-start.1 = ((f32[16,24,128]{2,1,0:T(8,128)}), f32[16,24,128]{2,1,0:T(8,128)S(1)}, u32[]{:S(2)}, u32[]{:S(2)}) async-start(f32[16,24,128]{2,1,0:T(8,128)} %bitcast.10), calls=%async_computation.1 | async-start | bytes 393216 | tf_op jit(solution)/shard_map/all_to_all | solution.py:577
  31.2 10.0 %copy-start.1 = (f32[32,32]{1,0:T(8,128)S(1)}, f32[32,32]{1,0:T(8,128)}, u32[]{:S(2)}) copy-start(f32[32,32]{1,0:T(8,128)} %constant.10.clone.slab_hbm.slab_ref) | copy-start | bytes 12292
  31.2 9.9 %copy-start.2 = (f32[16,1024]{1,0:T(8,128)S(1)}, f32[16,1024]{1,0:T(8,128)}, u32[]{:S(2)}) copy-start(f32[16,1024]{1,0:T(8,128)} %get-tuple-element.27.move_ref) | copy-start | bytes 196612
  31.2 9.9 %copy-start.3 = (s32[1,2,512]{2,1,0:T(2,128)S(1)}, s32[1,2,512]{2,1,0:T(2,128)}, u32[]{:S(2)}) copy-start(s32[1,2,512]{2,1,0:T(2,128)} %lists_ref.3) | copy-start | bytes 12292
  43.0 8.6 %collective-permute-start.2 = (f32[8,512]{1,0:T(8,128)S(1)}, f32[8,512]{1,0:T(8,128)S(1)}, u32[]{:S(2)}, u32[]{:S(2)}) collective-permute-start(f32[8,512]{1,0:T(8,128)S(1)} %get-tuple-element.30), channel_id=1, source_target_pairs={{0,1},{1,2},{2,3},{3,4},{4,5},{5,6},{6,7},{7,8},{8,9},{9,10},{10,1... | collective-permute-start | bytes 49160 | tf_op jit(solution)/shard_map/ppermute | solution.py:559
  43.8 7.8 %collective-permute-start.3 = (f32[8,512]{1,0:T(8,128)S(1)}, f32[8,512]{1,0:T(8,128)S(1)}, u32[]{:S(2)}, u32[]{:S(2)}) collective-permute-start(f32[8,512]{1,0:T(8,128)S(1)} %get-tuple-element.31), channel_id=1, source_target_pairs={{0,15},{1,0},{2,1},{3,2},{4,3},{5,4},{6,5},{7,6},{8,7},{9,8},{10,9... | collective-permute-start | bytes 49160 | tf_op jit(solution)/shard_map/ppermute | solution.py:560
  54.4 8.6 %collective-permute-start.4 = (f32[8,512]{1,0:T(8,128)S(1)}, f32[8,512]{1,0:T(8,128)S(1)}, u32[]{:S(2)}, u32[]{:S(2)}) collective-permute-start(f32[8,512]{1,0:T(8,128)S(1)} %get-tuple-element.35), channel_id=1, source_target_pairs={{0,1},{1,2},{2,3},{3,4},{4,5},{5,6},{6,7},{7,8},{8,9},{9,10},{10,1... | collective-permute-start | bytes 49160 | tf_op jit(solution)/shard_map/ppermute | solution.py:559
  54.5 8.6 %collective-permute-start.5 = (f32[8,512]{1,0:T(8,128)S(1)}, f32[8,512]{1,0:T(8,128)S(1)}, u32[]{:S(2)}, u32[]{:S(2)}) collective-permute-start(f32[8,512]{1,0:T(8,128)S(1)} %get-tuple-element.36), channel_id=1, source_target_pairs={{0,15},{1,0},{2,1},{3,2},{4,3},{5,4},{6,5},{7,6},{8,7},{9,8},{10,9... | collective-permute-start | bytes 49160 | tf_op jit(solution)/shard_map/ppermute | solution.py:560
  65.8 10.0 %collective-permute-start.8 = (f32[11,1,1024]{2,1,0:T(1,128)S(1)}, f32[11,1,1024]{2,1,0:T(1,128)S(1)}, u32[]{:S(2)}, u32[]{:S(2)}) collective-permute-start(f32[11,1,1024]{2,1,0:T(1,128)S(1)} %shard_map.174.here_ref), channel_id=1, source_target_pairs={{0,16},{16,0},{32,48},{48,32},{64,80},{80,64},{96,112},{112,96},{1... | collective-permute-start | bytes 135176 | tf_op jit(solution)/shard_map/ppermute | solution.py:572
  68.6 9.3 %collective-permute-start.7 = (f32[11,1,1024]{2,1,0:T(1,128)S(1)}, f32[11,1,1024]{2,1,0:T(1,128)S(1)}, u32[]{:S(2)}, u32[]{:S(2)}) collective-permute-start(f32[11,1,1024]{2,1,0:T(1,128)S(1)} %shard_map.174.here_ref), channel_id=1, source_target_pairs={{16,32},{32,16},{48,64},{64,48},{80,96},{96,80},{112,128},{128,112... | collective-permute-start | bytes 135176 | tf_op jit(solution)/shard_map/ppermute | solution.py:572
  73.8 9.6 %collective-permute-start.6 = (f32[11,1,1024]{2,1,0:T(1,128)S(1)}, f32[11,1,1024]{2,1,0:T(1,128)S(1)}, u32[]{:S(2)}, u32[]{:S(2)}) collective-permute-start(f32[11,1,1024]{2,1,0:T(1,128)S(1)} %shard_map.174.here_ref), channel_id=1, source_target_pairs={{0,32},{32,64},{64,96},{96,128},{128,160},{160,192},{192,224},{224... | collective-permute-start | bytes 135176 | tf_op jit(solution)/shard_map/ppermute | solution.py:567

commit v4 on v3

--- a/solution.py
+++ b/solution.py
@@ -327,36 +327,44 @@
     return count.astype(F32)
 
 
-def own_forces(lam_ref, tiles_ref, data_ref, force_ref, turns, near, sides, first, last):
+def own_forces(lam_ref, tiles_ref, data_ref, force_ref, turns, near, sides, columns, places, factors, first, last):
     turns[...] = fixed_turns(data_ref[0:3, :])
     near[...] = jnp.zeros_like(near)
     floor_value = SOFT_FLOOR + SOFT_SCALE * lam_ref[0]
+    for b in range(first, last):
+        lanes = slice(b * CLUSTER, (b + 1) * CLUSTER)
+        columns[lanes, :] = jnp.concatenate([turns[:, lanes], data_ref[3:8, lanes]], axis=0).T
 
     def one_cluster(b, carry):
         start = pl.multiple_of(b * CLUSTER, CLUSTER)
-        lanes = pl.ds(start, CLUSTER)
-        turned = jnp.concatenate([turns[:, lanes], data_ref[3:8, lanes]], axis=0).T
-        others = [b, (b + 1) % CLUSTERS, (b + 2) % CLUSTERS]
-        owns = [own_rows(data_ref, turns, pl.multiple_of(a * CLUSTER, CLUSTER)) for a in others]
-        totals = [[jnp.zeros((8, CLUSTER), F32) for _ in range(3)] for _ in others]
-        back = [None] + [listed(tiles_ref, b, a) for a in others[1:]]
-        for chunk in range(CLUSTER // 8):
-            part = turned[chunk * 8 : chunk * 8 + 8]
-            other = [jnp.broadcast_to(part[:, i : i + 1], (8, CLUSTER)) for i in range(5)]
-            other[:3] = [x.astype(jnp.int32) for x in other[:3]]
-            side = []
-            for j in range(3):
-                terms = pair_terms(owns[j], other, floor_value)
-                totals[j] = [p + q for p, q in zip(totals[j], terms)]
-                if j:
-                    side.append([back[j] * p for p in terms])
-            for i in range(3):
-                sides[i, pl.ds(pl.multiple_of(start + chunk * 8, 8), 8), :] = side[0][i] + side[1][i]
-        for j, a in enumerate(others):
+        for j in range(3):
+            a = b if j == 0 else (b + j) % CLUSTERS
+            own = own_rows(data_ref, turns, pl.multiple_of(a * CLUSTER, CLUSTER))
+            total = [jnp.zeros((8, CLUSTER), F32) for _ in range(3)]
+            back = listed(tiles_ref, b, a) if j else None
+            for chunk in range(CLUSTER // 8):
+                here = slice(chunk * 8, chunk * 8 + 8)
+                rows = pl.ds(pl.multiple_of(start + chunk * 8, 8), 8)
+                if j == 0:
+                    part = columns[rows, :]
+                    other = [jnp.broadcast_to(part[:, i : i + 1], (8, CLUSTER)) for i in range(5)]
+                    other[:3] = [x.astype(jnp.int32) for x in other[:3]]
+                    for i in range(3):
+                        places[i, here, :] = other[i]
+                    for i in range(2):
+                        factors[i, here, :] = other[3 + i]
+                else:
+                    other = [places[i, here, :] for i in range(3)] + [factors[i, here, :] for i in range(2)]
+                terms = pair_terms(own, other, floor_value)
+                total = [p + q for p, q in zip(total, terms)]
+                for i in range(3):
+                    if j == 1:
+                        sides[i, rows, :] = back * terms[i]
+                    elif j == 2:
+                        sides[i, rows, :] = sides[i, rows, :] + back * terms[i]
             rows = pl.ds(pl.multiple_of(a * 8, 8), 8)
             for i in range(3):
-                total = listed(tiles_ref, a, b) * totals[j][i] if j else totals[j][i]
-                near[i, rows, :] = near[i, rows, :] + total
+                near[i, rows, :] = near[i, rows, :] + (listed(tiles_ref, a, b) * total[i] if j else total[i])
         return carry
 
     lax.fori_loop(first, last, one_cluster, 0)
@@ -377,15 +385,15 @@
         force_ref[i : i + 1, rows] = force_ref[i : i + 1, rows] - SPAN * total[0:1]
 
 
-def own_kernel(lam_ref, tiles_ref, data_ref, force_ref, turns, near, sides):
-    own_forces(lam_ref, tiles_ref, data_ref, force_ref, turns, near, sides, 0, CLUSTERS)
+def own_kernel(lam_ref, tiles_ref, data_ref, force_ref, turns, near, sides, *kept):
+    own_forces(lam_ref, tiles_ref, data_ref, force_ref, turns, near, sides, *kept, 0, CLUSTERS)
 
 
 def gain_kernel(
-    lam_ref, tiles_ref, weights_ref, data_ref, rows_ref, lanes_ref, force_ref, gain_ref, turns, near, sides
+    lam_ref, tiles_ref, weights_ref, data_ref, rows_ref, lanes_ref, force_ref, gain_ref, turns, near, sides, *kept
 ):
     write_gain(weights_ref, rows_ref, lanes_ref, gain_ref)
-    own_forces(lam_ref, tiles_ref, data_ref, force_ref, turns, near, sides, 0, CLUSTERS // 2)
+    own_forces(lam_ref, tiles_ref, data_ref, force_ref, turns, near, sides, *kept, 0, CLUSTERS // 2)
 
 
 def add_halo_forces(lam_ref, data_ref, below_ref, above_ref, partial_ref, force_ref, turns):
@@ -420,9 +428,9 @@
 
 
 def rest_kernel(
-    lam_ref, tiles_ref, data_ref, below_ref, above_ref, partial_ref, force_ref, turns, near, sides, second
+    lam_ref, tiles_ref, data_ref, below_ref, above_ref, partial_ref, force_ref, second, turns, near, sides, *kept
 ):
-    own_forces(lam_ref, tiles_ref, data_ref, second, turns, near, sides, CLUSTERS // 2, CLUSTERS)
+    own_forces(lam_ref, tiles_ref, data_ref, second, turns, near, sides, *kept, CLUSTERS // 2, CLUSTERS)
     second[...] = second[...] + partial_ref[...]
     force_ref[...] = jnp.zeros_like(force_ref)
     add_halo_forces(lam_ref, data_ref, below_ref, above_ref, second, force_ref, turns)
@@ -511,28 +519,29 @@
         state_ref[i] = move_ref[i : i + 1, :]
         state_ref[3 + i] = velocity[i : i + 1]
         state_ref[6 + i] = move_ref[3 + i : 4 + i, :]
-    for i in range(2):
-        state_ref[9 + i] = move_ref[6 + i : 7 + i, :]
-
-
-def settle_kernel(here_ref, third_ref, second_ref, first_ref, cells_ref, off_ref, vel_ref):
-    even = lax.axis_index("lam") % 2 == 0
-    inside = lax.axis_index("lam") + 1 < lax.axis_size("lam")
-    outer = jnp.where(even, second_ref[10], jnp.where(inside, here_ref[10], 0.0)) == 1.0
-    far = jnp.where(even, third_ref[9], second_ref[9]) == 1.0
-    close = jnp.where(even, here_ref[9], first_ref[9]) == 1.0
+    state_ref[9] = move_ref[6:7, :]
+
+
+def takes(round_index, here_ref, there_ref):
+    window = lax.axis_index("lam")
+    lower = window % 2 == round_index % 2
+    inside = window + 1 < lax.axis_size("lam")
+    return jnp.where(lower, jnp.where(inside, here_ref[9], 0.0), there_ref[9]) == 1.0
+
+
+def first_trade_kernel(here_ref, there_ref, move_ref, out_ref):
+    take = takes(0, here_ref, there_ref)
     for i in range(9):
-        row = jnp.where(
-            outer,
-            jnp.where(far, third_ref[i], second_ref[i]),
-            jnp.where(close, first_ref[i], here_ref[i]),
-        )
-        if i < 3:
-            off_ref[i] = row
-        elif i < 6:
-            vel_ref[i - 3] = row
-        else:
-            cells_ref[i - 6] = row.astype(jnp.int32)
+        out_ref[i] = jnp.where(take, there_ref[i], here_ref[i])
+    out_ref[9] = move_ref[7:8, :]
+
+
+def last_trade_kernel(here_ref, there_ref, cells_ref, off_ref, vel_ref):
+    take = takes(1, here_ref, there_ref)
+    for i in range(3):
+        off_ref[i] = jnp.where(take, there_ref[i], here_ref[i])
+        vel_ref[i] = jnp.where(take, there_ref[3 + i], here_ref[3 + i])
+        cells_ref[i] = jnp.where(take, there_ref[6 + i], here_ref[6 + i]).astype(jnp.int32)
 
 
 PLACES = {
@@ -561,16 +570,11 @@
     return below, above
 
 
-def ladder_states(state):
-    windows = lax.axis_size("lam")
-    pairs = [(w - 2, w) for w in range(2, windows, 2)] + [(w + 2, w) for w in range(1, windows - 2, 2)]
-    received = [lax.ppermute(state, "lam", pairs)]
-    for offset in (1, 0):
-        pairs = []
-        for w in range(offset, windows - 1, 2):
-            pairs += [(w, w + 1), (w + 1, w)]
-        received.append(lax.ppermute(state, "lam", pairs))
-    return received
+def traded(state, round_index):
+    pairs = []
+    for w in range(round_index % 2, lax.axis_size("lam") - 1, 2):
+        pairs += [(w, w + 1), (w + 1, w)]
+    return lax.ppermute(state, "lam", pairs)
 
 
 def exchanged(value):
@@ -584,7 +588,10 @@
     moving = ((16, A_DEV), F32)
     border = ((8, HALO), F32)
     turns = pltpu.VMEM((3, A_DEV), F32)
-    pair_scratch = [turns, pltpu.VMEM((3, CLUSTERS * 8, CLUSTER), F32), pltpu.VMEM((3, A_DEV, CLUSTER), F32)]
+    pair_scratch = [
+        turns, pltpu.VMEM((3, CLUSTERS * 8, CLUSTER), F32), pltpu.VMEM((3, A_DEV, CLUSTER), F32),
+        pltpu.VMEM((A_DEV, 8), F32), pltpu.VMEM((3, CLUSTER, CLUSTER), jnp.int32), pltpu.VMEM((2, CLUSTER, CLUSTER), F32),
+    ]
     spare = pltpu.VMEM((8, A_DEV), F32)
     tiles = jnp.transpose(tile_lists, (2, 0, 1))
     slab = jnp.asarray(slab_basis())
@@ -640,7 +647,7 @@
         rest_kernel,
         [("s", lambdas), ("s", tiles), ("v", data), ("v", below), ("v", above), ("v", short)],
         [wide],
-        [*pair_scratch, spare],
+        [spare, *pair_scratch],
         cost=2 * 10**9,
     )
     far, data, move, low, high = call(
@@ -674,12 +681,15 @@
         [
             ("s", lambdas), ("v", data), ("v", below), ("v", above), ("v", short), ("v", far), ("v", move),
         ],
-        [((11, 1, A_DEV), F32)],
+        [((10, 1, A_DEV), F32)],
         [turns, spare],
     )
+    (state,) = call(
+        first_trade_kernel, [("v", state), ("v", traded(state, 0)), ("v", move)], [((10, 1, A_DEV), F32)]
+    )
     out = call(
-        settle_kernel,
-        [("v", state), *(("v", x) for x in ladder_states(state))],
+        last_trade_kernel,
+        [("v", state), ("v", traded(state, 1))],
         [(triple, jnp.int32), (triple, F32), (triple, F32)],
     )
     return tuple(by_row(x) for x in out)

time: 84.6 us -> 81.2 us (0.960)
  the two profiles are of different devices: /device:TPU:30 before, /device:TPU:32 now
where the time goes in v4:
time: 81.2 us; the launch traced here: 80.7 us
  Pallas kernels  33.2 us (41%)
  starting transfers between devices  32.2 us (40%)
  waiting for transfers between devices  13.7 us (17%)
  between operations  1.51 us (2%)
    pallas_call x11, Pallas kernels, call(): pl.pallas_call(kernel, out_shape=[jax.ShapeDtypeStruct(shape, dtype) for...  33.2 us
    all_to_all x2, starting transfers between devices, exchanged(): return lax.all_to_all(value, 'dom', split_axis=0, concat_axis=0, tiled=True)  15.4 us
    ppermute x2, starting transfers between devices, traded(): return lax.ppermute(state, 'lam', pairs)  7.95 us
    ppermute x3, starting transfers between devices, neighbours(): above = lax.ppermute(low, 'dom', [(i, (i - 1) % size) for i in range(size)])  7.67 us
    ppermute x2, waiting for transfers between devices, traded(): return lax.ppermute(state, 'lam', pairs)  7.15 us
    all_to_all x2, waiting for transfers between devices, exchanged(): return lax.all_to_all(value, 'dom', split_axis=0, concat_axis=0, tiled=True)  6.52 us
  transfers between devices with their start and end apart: 10, of which 4 were waited for; matrix products, arithmetic and copies ran while one was open for 0% of the time, Pallas kernels for 26%

profile of v4, /device:TPU:32, one launch (start us, length us, event | category | flops | bytes accessed | tf_op | source)
XLA Modules:
  0.0 80.7 jit_solution(15414728265132320355)
XLA Ops:
  1.3 2.8 %shard_map.166 = (f32[384,128]{1,0:T(8,128)}, f32[8,1024]{1,0:T(8,128)}, f32[16,1024]{1,0:T(8,128)}, f32[8,512]{1,0:T(8,128)}, f32[8,512]{1,0:T(8,128)}) custom-call(f32[1]{0:T(128)S(6)} %copy.18.lam_ref, s32[3,1,1024]{2,1,0:T(1,128)} %bitcast.22, f32[3,1,1024]{2,1,0:T(1,128)} %bitcast.23, f32[3,1,1024]{2,1,0:T(1,128)} %bitcast.24, f32[1,1024]{1,0:T(1,128)} %bitcast.25, ...), custom_call_target="tpu_custom_call" | custom-call | bytes 200000 | tf_op jit(solution)/shard_map/pallas_call | solution.py:555
  4.1 0.0 copy-start.6
  4.1 0.0 copy-start.7
  4.1 10.6 %all-to-all-start = ((f32[16,24,128]{2,1,0:T(8,128)}), f32[16,24,128]{2,1,0:T(8,128)S(1)}, u32[]{:S(2)}, u32[]{:S(2)}) async-start(f32[16,24,128]{2,1,0:T(8,128)} %bitcast.21), calls=%async_computation | async-start | bytes 393216 | tf_op jit(solution)/shard_map/all_to_all | solution.py:581
  14.7 0.0 copy-start.8
  14.7 0.0 copy-start.5
  14.7 0.4 collective-permute-start
  15.1 2.6 %collective-permute-start.1 = (f32[8,512]{1,0:T(8,128)S(1)}, f32[8,512]{1,0:T(8,128)S(1)}, u32[]{:S(2)}, u32[]{:S(2)}) collective-permute-start(f32[8,512]{1,0:T(8,128)S(1)} %copy-done.9), channel_id=1, source_target_pairs={{0,15},{1,0},{2,1},{3,2},{4,3},{5,4},{6,5},{7,6},{8,7},{9,8},{10,9... | collective-permute-start | bytes 49160 | tf_op jit(solution)/shard_map/ppermute | solution.py:569
  17.7 0.0 copy-start
  17.7 4.5 %shard_map.167 = (f32[8,1024]{1,0:T(8,128)S(1)}, f32[2,128,128]{2,1,0:T(8,128)S(1)}) custom-call(f32[1]{0:T(128)S(6)} %copy.18.lam_ref, s32[6,1,8]{2,1,0:T(1,128)S(1)} %bitcast.17, f32[17,65]{1,0:T(8,128)S(1)} %copy-done.7, f32[8,1024]{1,0:T(8,128)S(1)} %copy-done.4, f32[128,8]{1,0:T(8,128)S(1)} %copy-done.6, f32[8,128]{1,0:T(8,128)S(1)} %copy-done.8), custom_call_target="tpu_custom_call" | custom-call | flops 2000000000 | bytes 200000 | tf_op jit(solution)/shard_map/pallas_call | solution.py:555
  22.2 0.0 collective-permute-done.below_ref
  22.2 2.4 %all-to-all-done = f32[16,24,128]{2,1,0:T(8,128)S(1)} async-done(((f32[16,24,128]{2,1,0:T(8,128)}), f32[16,24,128]{2,1,0:T(8,128)S(1)}, u32[]{:S(2)}, u32[]{:S(2)}) %all-to-all-start) | async-done | bytes 196640 | tf_op jit(solution)/shard_map/all_to_all | solution.py:581
  24.6 1.5 %shard_map.168 = f32[384,128]{1,0:T(8,128)} custom-call(f32[384,128]{1,0:T(8,128)S(1)} %bitcast.15, f32[2,128,128]{2,1,0:T(8,128)S(1)} %get-tuple-element.24.gain_ref, bf16[512,128]{1,0:T(8,128)(2,1)S(1)} %copy-done, f32[8,512]{1,0:T(8,128)S(1)} %collective-permute-done.below_ref, f32[8,512]{1,0:T(8,128)S(1)} %collective-permute-done.1.above_ref), custom_call_target="tpu_custom_call" | custom-call | bytes 200000 | tf_op jit(solution)/shard_map/pallas_call | solution.py:555
  26.1 4.8 %all-to-all-start.1 = ((f32[16,24,128]{2,1,0:T(8,128)}), f32[16,24,128]{2,1,0:T(8,128)S(1)}, u32[]{:S(2)}, u32[]{:S(2)}) async-start(f32[16,24,128]{2,1,0:T(8,128)} %bitcast.10), calls=%async_computation.1 | async-start | bytes 393216 | tf_op jit(solution)/shard_map/all_to_all | solution.py:581
  30.9 0.0 copy-start.1
  30.9 0.0 copy-start.3
  30.9 5.8 %shard_map.169.short_ref = f32[8,1024]{1,0:T(8,128)S(1)} custom-call(f32[1]{0:T(128)S(6)} %copy.18.lam_ref, s32[6,1,8]{2,1,0:T(1,128)S(1)} %bitcast.18, f32[8,1024]{1,0:T(8,128)S(1)} %copy-done.4, f32[8,512]{1,0:T(8,128)S(1)} %collective-permute-done.below_ref, f32[8,512]{1,0:T(8,128)S(1)} %collective-permute-done.1.above_ref, ...), custom_call_target="tpu_custom_call" | custom-call | flops 2000000000 | bytes 200000 | tf_op jit(solution)/shard_map/pallas_call | solution.py:555
  36.8 4.1 %all-to-all-done.1 = f32[16,24,128]{2,1,0:T(8,128)S(1)} async-done(((f32[16,24,128]{2,1,0:T(8,128)}), f32[16,24,128]{2,1,0:T(8,128)S(1)}, u32[]{:S(2)}, u32[]{:S(2)}) %all-to-all-start.1) | async-done | bytes 196640 | tf_op jit(solution)/shard_map/all_to_all | solution.py:581
  40.9 1.8 %shard_map.170 = (f32[8,1024]{1,0:T(8,128)S(1)}, f32[8,1024]{1,0:T(8,128)S(1)}, f32[16,1024]{1,0:T(8,128)S(1)}, f32[8,512]{1,0:T(8,128)S(1)}, f32[8,512]{1,0:T(8,128)S(1)}) custom-call(f32[384,128]{1,0:T(8,128)S(1)} %bitcast.16, f32[8,1024]{1,0:T(8,128)S(1)} %copy-done.4, f32[16,1024]{1,0:T(8,128)S(1)} %copy-done.2, f32[8,1024]{1,0:T(8,128)S(1)} %shard_map.169.short_ref, ...), custom_call_target="tpu_custom_call" | custom-call | bytes 200000 | tf_op jit(solution)/shard_map/pallas_call | solution.py:555
  42.7 0.8 collective-permute-start.2
  43.5 2.2 %collective-permute-start.3 = (f32[8,512]{1,0:T(8,128)S(1)}, f32[8,512]{1,0:T(8,128)S(1)}, u32[]{:S(2)}, u32[]{:S(2)}) collective-permute-start(f32[8,512]{1,0:T(8,128)S(1)} %get-tuple-element.31), channel_id=1, source_target_pairs={{0,15},{1,0},{2,1},{3,2},{4,3},{5,4},{6,5},{7,6},{8,7},{9,8},{10,9... | collective-permute-start | bytes 49160 | tf_op jit(solution)/shard_map/ppermute | solution.py:569
  45.6 5.4 %shard_map.171.partial_ref = f32[8,1024]{1,0:T(8,128)S(1)} custom-call(f32[1]{0:T(128)S(6)} %copy.18.lam_ref, s32[6,1,8]{2,1,0:T(1,128)S(1)} %bitcast.19, f32[8,1024]{1,0:T(8,128)S(1)} %get-tuple-element.29.data_ref), custom_call_target="tpu_custom_call" | custom-call | flops 2000000000 | bytes 200000 | tf_op jit(solution)/shard_map/pallas_call | solution.py:555
  51.0 2.8 %shard_map.172 = (f32[8,1024]{1,0:T(8,128)S(1)}, f32[16,1024]{1,0:T(8,128)S(1)}, f32[8,512]{1,0:T(8,128)S(1)}, f32[8,512]{1,0:T(8,128)S(1)}) custom-call(f32[1]{0:T(128)S(6)} %copy.18.lam_ref, f32[8,1024]{1,0:T(8,128)S(1)} %get-tuple-element.29.data_ref, f32[8,512]{1,0:T(8,128)S(1)} %collective-permute-done.2.below_ref, ...), custom_call_target="tpu_custom_call" | custom-call | bytes 200000 | tf_op jit(solution)/shard_map/pallas_call | solution.py:555
  53.9 0.0 collective-permute-start.4
  53.9 2.9 %collective-permute-start.5 = (f32[8,512]{1,0:T(8,128)S(1)}, f32[8,512]{1,0:T(8,128)S(1)}, u32[]{:S(2)}, u32[]{:S(2)}) collective-permute-start(f32[8,512]{1,0:T(8,128)S(1)} %get-tuple-element.36), channel_id=1, source_target_pairs={{0,15},{1,0},{2,1},{3,2},{4,3},{5,4},{6,5},{7,6},{8,7},{9,8},{10,9... | collective-permute-start | bytes 49160 | tf_op jit(solution)/shard_map/ppermute | solution.py:569
  56.8 5.4 %shard_map.173.partial_ref = f32[8,1024]{1,0:T(8,128)S(1)} custom-call(f32[1]{0:T(128)S(6)} %copy.18.lam_ref, s32[6,1,8]{2,1,0:T(1,128)S(1)} %bitcast.20, f32[8,1024]{1,0:T(8,128)S(1)} %get-tuple-element.34.data_ref), custom_call_target="tpu_custom_call" | custom-call | flops 2000000000 | bytes 200000 | tf_op jit(solution)/shard_map/pallas_call | solution.py:555
  62.2 2.7 %shard_map.174.here_ref = f32[10,1,1024]{2,1,0:T(1,128)S(1)} custom-call(f32[1]{0:T(128)S(6)} %copy.18.lam_ref, f32[8,1024]{1,0:T(8,128)S(1)} %get-tuple-element.34.data_ref, f32[8,512]{1,0:T(8,128)S(1)} %collective-permute-done.4.below_ref, f32[8,512]{1,0:T(8,128)S(1)} %collective-permute-done.5.above_ref, f32[8,1024]{1,0:T(8,128)S(1)} %shard_map.173.partial_ref, ...), custom_call_target="tpu_custom_call" | custom-call | bytes 200000 | tf_op jit(solution)/shard_map/pallas_call | solution.py:555
  65.0 3.4 %collective-permute-start.6 = (f32[10,1,1024]{2,1,0:T(1,128)S(1)}, f32[10,1,1024]{2,1,0:T(1,128)S(1)}, u32[]{:S(2)}, u32[]{:S(2)}) collective-permute-start(f32[10,1,1024]{2,1,0:T(1,128)S(1)} %shard_map.174.here_ref), channel_id=1, source_target_pairs={{0,16},{16,0},{32,48},{48,32},{64,80},{80,64},{96,112},{112,96},{1... | collective-permute-start | bytes 122888 | tf_op jit(solution)/shard_map/ppermute | solution.py:577
  68.4 2.5 %collective-permute-done.6.there_ref = f32[10,1,1024]{2,1,0:T(1,128)S(1)} collective-permute-done((f32[10,1,1024]{2,1,0:T(1,128)S(1)}, f32[10,1,1024]{2,1,0:T(1,128)S(1)}, u32[]{:S(2)}, u32[]{:S(2)}) %collective-permute-start.6) | collective-permute-done | bytes 40992 | tf_op jit(solution)/shard_map/ppermute | solution.py:577
  70.9 4.6 %collective-permute-start.7 = (f32[10,1,1024]{2,1,0:T(1,128)S(1)}, f32[10,1,1024]{2,1,0:T(1,128)S(1)}, u32[]{:S(2)}, u32[]{:S(2)}) collective-permute-start(f32[10,1,1024]{2,1,0:T(1,128)S(1)} %shard_map.175.here_ref), channel_id=1, source_target_pairs={{16,32},{32,16},{48,64},{64,48},{80,96},{96,80},{112,128},{128,112... | collective-permute-start | bytes 122888 | tf_op jit(solution)/shard_map/ppermute | solution.py:577
  75.4 4.7 %collective-permute-done.7.there_ref = f32[10,1,1024]{2,1,0:T(1,128)S(1)} collective-permute-done((f32[10,1,1024]{2,1,0:T(1,128)S(1)}, f32[10,1,1024]{2,1,0:T(1,128)S(1)}, u32[]{:S(2)}, u32[]{:S(2)}) %collective-permute-start.7) | collective-permute-done | bytes 40992 | tf_op jit(solution)/shard_map/ppermute | solution.py:577
  80.1 0.6 shard_map.176
  (21 shorter events, 0.1 us)
Async XLA Ops:
  4.1 10.6 %copy-start.10 = (f32[8,512]{1,0:T(8,128)S(1)}, f32[8,512]{1,0:T(8,128)}, u32[]{:S(2)}) copy-start(f32[8,512]{1,0:T(8,128)} %get-tuple-element.25) | copy-start | bytes 49156
  4.1 11.1 %copy-start.9 = (f32[8,512]{1,0:T(8,128)S(1)}, f32[8,512]{1,0:T(8,128)}, u32[]{:S(2)}) copy-start(f32[8,512]{1,0:T(8,128)} %get-tuple-element.26) | copy-start | bytes 49156
  4.1 13.6 %copy-start.4 = (f32[8,1024]{1,0:T(8,128)S(1)}, f32[8,1024]{1,0:T(8,128)}, u32[]{:S(2)}) copy-start(f32[8,1024]{1,0:T(8,128)} %get-tuple-element.23.data_ref) | copy-start | bytes 98308
  4.1 13.6 %copy-start.6 = (f32[128,8]{1,0:T(8,128)S(1)}, f32[128,8]{1,0:T(8,128)}, u32[]{:S(2)}) copy-start(f32[128,8]{1,0:T(8,128)} %constant.12.clone.rows_ref) | copy-start | bytes 12292
  4.1 13.6 %copy-start.7 = (f32[17,65]{1,0:T(8,128)S(1)}, f32[17,65]{1,0:T(8,128)}, u32[]{:S(2)}) copy-start(f32[17,65]{1,0:T(8,128)} %constant.11.clone.weights_ref) | copy-start | bytes 13264
  4.1 20.5 %all-to-all-start = ((f32[16,24,128]{2,1,0:T(8,128)}), f32[16,24,128]{2,1,0:T(8,128)S(1)}, u32[]{:S(2)}, u32[]{:S(2)}) async-start(f32[16,24,128]{2,1,0:T(8,128)} %bitcast.21), calls=%async_computation | async-start | bytes 393216 | tf_op jit(solution)/shard_map/all_to_all | solution.py:581
  14.7 3.0 %copy-start.8 = (f32[8,128]{1,0:T(8,128)S(1)}, f32[8,128]{1,0:T(8,128)}, u32[]{:S(2)}) copy-start(f32[8,128]{1,0:T(8,128)} %constant.13.clone.lanes_ref) | copy-start | bytes 12292
  14.7 3.0 %copy-start.5 = (s32[1,8,6]{1,0,2:T(1,128)S(1)}, s32[1,8,6]{1,0,2:T(1,128)}, u32[]{:S(2)}) copy-start(s32[1,8,6]{1,0,2:T(1,128)} %param.22) | copy-start | bytes 580
  14.7 7.5 %collective-permute-start = (f32[8,512]{1,0:T(8,128)S(1)}, f32[8,512]{1,0:T(8,128)S(1)}, u32[]{:S(2)}, u32[]{:S(2)}) collective-permute-start(f32[8,512]{1,0:T(8,128)S(1)} %copy-done.10), channel_id=1, source_target_pairs={{0,1},{1,2},{2,3},{3,4},{4,5},{5,6},{6,7},{7,8},{8,9},{9,10},{10,1... | collective-permute-start | bytes 49160 | tf_op jit(solution)/shard_map/ppermute | solution.py:568
  15.1 7.1 %collective-permute-start.1 = (f32[8,512]{1,0:T(8,128)S(1)}, f32[8,512]{1,0:T(8,128)S(1)}, u32[]{:S(2)}, u32[]{:S(2)}) collective-permute-start(f32[8,512]{1,0:T(8,128)S(1)} %copy-done.9), channel_id=1, source_target_pairs={{0,15},{1,0},{2,1},{3,2},{4,3},{5,4},{6,5},{7,6},{8,7},{9,8},{10,9... | collective-permute-start | bytes 49160 | tf_op jit(solution)/shard_map/ppermute | solution.py:569
  17.7 6.9 %copy-start = (bf16[512,128]{1,0:T(8,128)(2,1)S(1)}, bf16[512,128]{1,0:T(8,128)(2,1)}, u32[]{:S(2)}) copy-start(bf16[512,128]{1,0:T(8,128)(2,1)} %constant.14.clone.basis_ref) | copy-start | bytes 393220
  26.1 14.8 %all-to-all-start.1 = ((f32[16,24,128]{2,1,0:T(8,128)}), f32[16,24,128]{2,1,0:T(8,128)S(1)}, u32[]{:S(2)}, u32[]{:S(2)}) async-start(f32[16,24,128]{2,1,0:T(8,128)} %bitcast.10), calls=%async_computation.1 | async-start | bytes 393216 | tf_op jit(solution)/shard_map/all_to_all | solution.py:581
  30.9 10.0 %copy-start.1 = (f32[32,32]{1,0:T(8,128)S(1)}, f32[32,32]{1,0:T(8,128)}, u32[]{:S(2)}) copy-start(f32[32,32]{1,0:T(8,128)} %constant.10.clone.slab_hbm.slab_ref) | copy-start | bytes 12292
  30.9 9.9 %copy-start.2 = (f32[16,1024]{1,0:T(8,128)S(1)}, f32[16,1024]{1,0:T(8,128)}, u32[]{:S(2)}) copy-start(f32[16,1024]{1,0:T(8,128)} %get-tuple-element.27.move_ref) | copy-start | bytes 196612
  30.9 9.9 %copy-start.3 = (s32[1,2,512]{2,1,0:T(2,128)S(1)}, s32[1,2,512]{2,1,0:T(2,128)}, u32[]{:S(2)}) copy-start(s32[1,2,512]{2,1,0:T(2,128)} %lists_ref.3) | copy-start | bytes 12292
  42.7 8.3 %collective-permute-start.2 = (f32[8,512]{1,0:T(8,128)S(1)}, f32[8,512]{1,0:T(8,128)S(1)}, u32[]{:S(2)}, u32[]{:S(2)}) collective-permute-start(f32[8,512]{1,0:T(8,128)S(1)} %get-tuple-element.30), channel_id=1, source_target_pairs={{0,1},{1,2},{2,3},{3,4},{4,5},{5,6},{6,7},{7,8},{8,9},{9,10},{10,1... | collective-permute-start | bytes 49160 | tf_op jit(solution)/shard_map/ppermute | solution.py:568
  43.5 7.6 %collective-permute-start.3 = (f32[8,512]{1,0:T(8,128)S(1)}, f32[8,512]{1,0:T(8,128)S(1)}, u32[]{:S(2)}, u32[]{:S(2)}) collective-permute-start(f32[8,512]{1,0:T(8,128)S(1)} %get-tuple-element.31), channel_id=1, source_target_pairs={{0,15},{1,0},{2,1},{3,2},{4,3},{5,4},{6,5},{7,6},{8,7},{9,8},{10,9... | collective-permute-start | bytes 49160 | tf_op jit(solution)/shard_map/ppermute | solution.py:569
  53.9 8.3 %collective-permute-start.4 = (f32[8,512]{1,0:T(8,128)S(1)}, f32[8,512]{1,0:T(8,128)S(1)}, u32[]{:S(2)}, u32[]{:S(2)}) collective-permute-start(f32[8,512]{1,0:T(8,128)S(1)} %get-tuple-element.35), channel_id=1, source_target_pairs={{0,1},{1,2},{2,3},{3,4},{4,5},{5,6},{6,7},{7,8},{8,9},{9,10},{10,1... | collective-permute-start | bytes 49160 | tf_op jit(solution)/shard_map/ppermute | solution.py:568
  53.9 8.3 %collective-permute-start.5 = (f32[8,512]{1,0:T(8,128)S(1)}, f32[8,512]{1,0:T(8,128)S(1)}, u32[]{:S(2)}, u32[]{:S(2)}) collective-permute-start(f32[8,512]{1,0:T(8,128)S(1)} %get-tuple-element.36), channel_id=1, source_target_pairs={{0,15},{1,0},{2,1},{3,2},{4,3},{5,4},{6,5},{7,6},{8,7},{9,8},{10,9... | collective-permute-start | bytes 49160 | tf_op jit(solution)/shard_map/ppermute | solution.py:569
  65.0 5.9 %collective-permute-start.6 = (f32[10,1,1024]{2,1,0:T(1,128)S(1)}, f32[10,1,1024]{2,1,0:T(1,128)S(1)}, u32[]{:S(2)}, u32[]{:S(2)}) collective-permute-start(f32[10,1,1024]{2,1,0:T(1,128)S(1)} %shard_map.174.here_ref), channel_id=1, source_target_pairs={{0,16},{16,0},{32,48},{48,32},{64,80},{80,64},{96,112},{112,96},{1... | collective-permute-start | bytes 122888 | tf_op jit(solution)/shard_map/ppermute | solution.py:577
  70.9 9.2 %collective-permute-start.7 = (f32[10,1,1024]{2,1,0:T(1,128)S(1)}, f32[10,1,1024]{2,1,0:T(1,128)S(1)}, u32[]{:S(2)}, u32[]{:S(2)}) collective-permute-start(f32[10,1,1024]{2,1,0:T(1,128)S(1)} %shard_map.175.here_ref), channel_id=1, source_target_pairs={{16,32},{32,16},{48,64},{64,48},{80,96},{96,80},{112,128},{128,112... | collective-permute-start | bytes 122888 | tf_op jit(solution)/shard_map/ppermute | solution.py:577

commit v5 on v4

--- a/solution.py
+++ b/solution.py
@@ -357,11 +357,9 @@
                     other = [places[i, here, :] for i in range(3)] + [factors[i, here, :] for i in range(2)]
                 terms = pair_terms(own, other, floor_value)
                 total = [p + q for p, q in zip(total, terms)]
-                for i in range(3):
-                    if j == 1:
-                        sides[i, rows, :] = back * terms[i]
-                    elif j == 2:
-                        sides[i, rows, :] = sides[i, rows, :] + back * terms[i]
+                if j:
+                    for i in range(3):
+                        sides[3 * j - 3 + i, rows, :] = back * terms[i]
             rows = pl.ds(pl.multiple_of(a * 8, 8), 8)
             for i in range(3):
                 near[i, rows, :] = near[i, rows, :] + (listed(tiles_ref, a, b) * total[i] if j else total[i])
@@ -376,11 +374,8 @@
             force_ref[i : i + 1, lanes] = SPAN * jnp.sum(near[i, c * 8 : (c + 1) * 8, :], axis=0, keepdims=True)
     rows = slice(first * CLUSTER, last * CLUSTER)
     for i in range(3):
-        rest = sides[i, rows, :]
         total = jnp.zeros((8, (last - first) * CLUSTER), F32)
-        for _ in range(3):
-            part = rest.astype(BF16)
-            rest = rest - part.astype(F32)
+        for part in split(sides[i, rows, :] + sides[3 + i, rows, :]):
             total = total + lax.dot_general(ones, part, (((1,), (1,)), ((), ())), preferred_element_type=F32)
         force_ref[i : i + 1, rows] = force_ref[i : i + 1, rows] - SPAN * total[0:1]
 
@@ -428,8 +423,10 @@
 
 
 def rest_kernel(
-    lam_ref, tiles_ref, data_ref, below_ref, above_ref, partial_ref, force_ref, second, turns, near, sides, *kept
+    lam_ref, tiles_ref, data_ref, below_ref, above_ref, partial_ref, move_ref, slab_ref,
+    force_ref, y_high, y_low, z_ref, x_ref, second, turns, near, sides, *kept
 ):
+    write_tables(move_ref, slab_ref, y_high, y_low, z_ref, x_ref)
     own_forces(lam_ref, tiles_ref, data_ref, second, turns, near, sides, *kept, CLUSTERS // 2, CLUSTERS)
     second[...] = second[...] + partial_ref[...]
     force_ref[...] = jnp.zeros_like(force_ref)
@@ -450,39 +447,46 @@
     write_halo(data_out[...], lists_ref, low_ref, high_ref)
 
 
-def gather_kernel(
-    pot_ref, data_ref, move_ref, short_ref, lists_ref, slab_ref,
-    long_ref, data_out, move_out, low_ref, high_ref, force,
-):
+def write_tables(move_ref, slab_ref, y_high, y_low, z_ref, x_ref):
     off = move_ref[0:3, :]
     cells = move_ref[3:6, :].astype(jnp.int32)
-    charge = data_ref[3:4, :]
     weights, slopes = spline_set(off)
     row = iota_rows(16, A_DEV)
     reach = jnp.where(row < 8, row, 8 + (row & 3)) - (cells[0:1] & 7)
-    x_table = chosen(reach, [m[0:1] for m in weights])
-    x_slope = chosen(reach, [m[0:1] for m in slopes])
+    x_ref[0:16, :] = chosen(reach, [m[0:1] for m in weights])
+    x_ref[16:32, :] = chosen(reach, [m[0:1] for m in slopes])
     reach = (iota_rows(MODES, A_DEV) - cells[2:3]) & (MODES - 1)
-    z_table = chosen(reach, [m[2:3] for m in weights])
-    z_slope = chosen(reach, [m[2:3] for m in slopes])
-    z_modes = jnp.dot(slab_ref[...], z_table, precision=HIGHEST, preferred_element_type=F32)
-    z_tilts = jnp.dot(slab_ref[...], z_slope, precision=HIGHEST, preferred_element_type=F32)
+    for i, rows in enumerate((weights, slopes)):
+        table = chosen(reach, [m[2:3] for m in rows])
+        z_ref[i * MODES : (i + 1) * MODES, :] = jnp.dot(
+            slab_ref[...], table, precision=HIGHEST, preferred_element_type=F32
+        )
+    for c in range(CLUSTERS):
+        lanes = slice(c * CLUSTER, (c + 1) * CLUSTER)
+        reach = (iota_rows(K, CLUSTER) - cells[1:2, lanes]) & (K - 1)
+        for i, rows in enumerate((weights, slopes)):
+            target = slice((2 * c + i) * CLUSTER, (2 * c + i + 1) * CLUSTER)
+            y_high[:, target], y_low[:, target] = split(chosen(reach, [m[1:2, lanes] for m in rows]))
+
+
+def gather_kernel(
+    pot_ref, data_ref, move_ref, short_ref, lists_ref, y_high, y_low, z_ref, x_ref,
+    long_ref, data_out, move_out, low_ref, high_ref, force,
+):
+    charge = data_ref[3:4, :]
     potential = split(pot_ref[...])
     upper = iota_rows(8, CLUSTER) < 4
     for c in range(CLUSTERS):
         lanes = slice(c * CLUSTER, (c + 1) * CLUSTER)
-        reach = (iota_rows(K, CLUSTER) - cells[1:2, lanes]) & (K - 1)
-        y_both = jnp.concatenate(
-            [chosen(reach, [m[1:2, lanes] for m in weights]), chosen(reach, [m[1:2, lanes] for m in slopes])], axis=1
-        )
-        along = dot3(potential, split(y_both))
+        both = slice(2 * c * CLUSTER, (2 * c + 2) * CLUSTER)
+        along = dot3(potential, (y_high[:, both], y_low[:, both]))
         value, tilt = along[:, :CLUSTER], along[:, CLUSTER:]
         sums = [[jnp.zeros((8, CLUSTER), F32) for _ in range(2)] for _ in range(3)]
         for i in range(N_DOM):
             pairs = []
-            for table in (z_modes, z_tilts):
-                first = jnp.broadcast_to(table[2 * i : 2 * i + 1, lanes], (8, CLUSTER))
-                second = jnp.broadcast_to(table[2 * i + 1 : 2 * i + 2, lanes], (8, CLUSTER))
+            for k in (2 * i, MODES + 2 * i):
+                first = jnp.broadcast_to(z_ref[k : k + 1, lanes], (8, CLUSTER))
+                second = jnp.broadcast_to(z_ref[k + 1 : k + 2, lanes], (8, CLUSTER))
                 pairs.append((first, second, jnp.where(upper, first, second)))
             for which, (source, table) in enumerate(((value, 0), (tilt, 0), (value, 1))):
                 block = source[i * SLAB : (i + 1) * SLAB]
@@ -490,8 +494,8 @@
                 sums[which][0] = sums[which][0] + (first * block[0:8] + second * block[8:16])
                 sums[which][1] = sums[which][1] + mixed * block[16:24]
         for i in range(3):
-            table = x_slope if i == 0 else x_table
-            near = table[0:8, lanes] * sums[i][0] + table[8:16, lanes] * sums[i][1]
+            k = 16 if i == 0 else 0
+            near = x_ref[k : k + 8, lanes] * sums[i][0] + x_ref[k + 8 : k + 16, lanes] * sums[i][1]
             force[i : i + 1, lanes] = -charge[:, lanes] * jnp.sum(near, axis=0, keepdims=True)
     long_ref[...] = jnp.zeros_like(long_ref)
     long_ref[0:3, :] = force[0:3, :]
@@ -589,7 +593,7 @@
     border = ((8, HALO), F32)
     turns = pltpu.VMEM((3, A_DEV), F32)
     pair_scratch = [
-        turns, pltpu.VMEM((3, CLUSTERS * 8, CLUSTER), F32), pltpu.VMEM((3, A_DEV, CLUSTER), F32),
+        turns, pltpu.VMEM((3, CLUSTERS * 8, CLUSTER), F32), pltpu.VMEM((6, A_DEV, CLUSTER), F32),
         pltpu.VMEM((A_DEV, 8), F32), pltpu.VMEM((3, CLUSTER, CLUSTER), jnp.int32), pltpu.VMEM((2, CLUSTER, CLUSTER), F32),
     ]
     spare = pltpu.VMEM((8, A_DEV), F32)
@@ -643,16 +647,18 @@
         [pltpu.VMEM((2 * K, K), F32)],
     )
     potential = exchanged(potential)
-    (short,) = call(
+    short, *tables = call(
         rest_kernel,
-        [("s", lambdas), ("s", tiles), ("v", data), ("v", below), ("v", above), ("v", short)],
-        [wide],
+        [
+            ("s", lambdas), ("s", tiles), ("v", data), ("v", below), ("v", above), ("v", short), ("v", move), ("v", slab),
+        ],
+        [wide, *[((K, 2 * A_DEV), BF16)] * 2, ((2 * MODES, A_DEV), F32), ((32, A_DEV), F32)],
         [spare, *pair_scratch],
         cost=2 * 10**9,
     )
     far, data, move, low, high = call(
         gather_kernel,
-        [("v", potential), ("v", data), ("v", move), ("v", short), ("v", halo_lists), ("v", slab)],
+        [("v", potential), ("v", data), ("v", move), ("v", short), ("v", halo_lists), *(("v", x) for x in tables)],
         [wide, wide, moving, border, border],
         [spare],
     )

time: 81.2 us -> 81.2 us (level)
  no operation moved by 1% of the time
where the time goes in v5:
time: 81.2 us; the launch traced here: 80.7 us
  Pallas kernels  33.2 us (41%)
  starting transfers between devices  32.2 us (40%)
  waiting for transfers between devices  13 us (16%)
  between operations  1.5 us (2%)
    pallas_call x11, Pallas kernels, call(): pl.pallas_call(kernel, out_shape=[jax.ShapeDtypeStruct(shape, dtype) for...  33.2 us
    all_to_all x2, starting transfers between devices, exchanged(): return lax.all_to_all(value, 'dom', split_axis=0, concat_axis=0, tiled=True)  15.4 us
    ppermute x2, starting transfers between devices, traded(): return lax.ppermute(state, 'lam', pairs)  7.95 us
    ppermute x3, starting transfers between devices, neighbours(): above = lax.ppermute(low, 'dom', [(i, (i - 1) % size) for i in range(size)])  7.66 us
    ppermute x2, waiting for transfers between devices, traded(): return lax.ppermute(state, 'lam', pairs)  7.15 us
    all_to_all x2, waiting for transfers between devices, exchanged(): return lax.all_to_all(value, 'dom', split_axis=0, concat_axis=0, tiled=True)  5.84 us
  transfers between devices with their start and end apart: 10, of which 4 were waited for; matrix products, arithmetic and copies ran while one was open for 0% of the time, Pallas kernels for 26%

profile of v5, /device:TPU:32, one launch (start us, length us, event | category | flops | bytes accessed | tf_op | source)
XLA Modules:
  0.0 80.7 jit_solution(4981103442138219830)
XLA Ops:
  1.3 2.8 %shard_map.166 = (f32[384,128]{1,0:T(8,128)}, f32[8,1024]{1,0:T(8,128)}, f32[16,1024]{1,0:T(8,128)}, f32[8,512]{1,0:T(8,128)}, f32[8,512]{1,0:T(8,128)}) custom-call(f32[1]{0:T(128)S(6)} %copy.18.lam_ref, s32[3,1,1024]{2,1,0:T(1,128)} %bitcast.22, f32[3,1,1024]{2,1,0:T(1,128)} %bitcast.23, f32[3,1,1024]{2,1,0:T(1,128)} %bitcast.24, f32[1,1024]{1,0:T(1,128)} %bitcast.25, ...), custom_call_target="tpu_custom_call" | custom-call | bytes 200000 | tf_op jit(solution)/shard_map/pallas_call | solution.py:559
  4.1 0.0 copy-start.6
  4.1 0.0 copy-start.7
  4.1 10.6 %all-to-all-start = ((f32[16,24,128]{2,1,0:T(8,128)}), f32[16,24,128]{2,1,0:T(8,128)S(1)}, u32[]{:S(2)}, u32[]{:S(2)}) async-start(f32[16,24,128]{2,1,0:T(8,128)} %bitcast.21), calls=%async_computation | async-start | bytes 393216 | tf_op jit(solution)/shard_map/all_to_all | solution.py:585
  14.7 0.0 copy-start.8
  14.7 0.0 copy-start.5
  14.7 0.4 collective-permute-start
  15.2 2.6 %collective-permute-start.1 = (f32[8,512]{1,0:T(8,128)S(1)}, f32[8,512]{1,0:T(8,128)S(1)}, u32[]{:S(2)}, u32[]{:S(2)}) collective-permute-start(f32[8,512]{1,0:T(8,128)S(1)} %copy-done.9), channel_id=1, source_target_pairs={{0,15},{1,0},{2,1},{3,2},{4,3},{5,4},{6,5},{7,6},{8,7},{9,8},{10,9... | collective-permute-start | bytes 49160 | tf_op jit(solution)/shard_map/ppermute | solution.py:573
  17.7 0.0 copy-start
  17.7 4.3 %shard_map.167 = (f32[8,1024]{1,0:T(8,128)S(1)}, f32[2,128,128]{2,1,0:T(8,128)S(1)}) custom-call(f32[1]{0:T(128)S(6)} %copy.18.lam_ref, s32[6,1,8]{2,1,0:T(1,128)S(1)} %bitcast.17, f32[17,65]{1,0:T(8,128)S(1)} %copy-done.7, f32[8,1024]{1,0:T(8,128)S(1)} %copy-done.3, f32[128,8]{1,0:T(8,128)S(1)} %copy-done.6, f32[8,128]{1,0:T(8,128)S(1)} %copy-done.8), custom_call_target="tpu_custom_call" | custom-call | flops 2000000000 | bytes 200000 | tf_op jit(solution)/shard_map/pallas_call | solution.py:559
  22.1 0.0 collective-permute-done.below_ref
  22.1 2.5 %all-to-all-done = f32[16,24,128]{2,1,0:T(8,128)S(1)} async-done(((f32[16,24,128]{2,1,0:T(8,128)}), f32[16,24,128]{2,1,0:T(8,128)S(1)}, u32[]{:S(2)}, u32[]{:S(2)}) %all-to-all-start) | async-done | bytes 196640 | tf_op jit(solution)/shard_map/all_to_all | solution.py:585
  24.7 1.5 %shard_map.168 = f32[384,128]{1,0:T(8,128)} custom-call(f32[384,128]{1,0:T(8,128)S(1)} %bitcast.16, f32[2,128,128]{2,1,0:T(8,128)S(1)} %get-tuple-element.29.gain_ref, bf16[512,128]{1,0:T(8,128)(2,1)S(1)} %copy-done, f32[8,512]{1,0:T(8,128)S(1)} %collective-permute-done.below_ref, f32[8,512]{1,0:T(8,128)S(1)} %collective-permute-done.1.above_ref), custom_call_target="tpu_custom_call" | custom-call | bytes 200000 | tf_op jit(solution)/shard_map/pallas_call | solution.py:559
  26.1 4.8 %all-to-all-start.1 = ((f32[16,24,128]{2,1,0:T(8,128)}), f32[16,24,128]{2,1,0:T(8,128)S(1)}, u32[]{:S(2)}, u32[]{:S(2)}) async-start(f32[16,24,128]{2,1,0:T(8,128)} %bitcast.10), calls=%async_computation.1 | async-start | bytes 393216 | tf_op jit(solution)/shard_map/all_to_all | solution.py:585
  31.0 6.6 %shard_map.169 = (f32[8,1024]{1,0:T(8,128)S(1)}, bf16[128,2048]{1,0:T(8,128)(2,1)S(1)}, bf16[128,2048]{1,0:T(8,128)(2,1)S(1)}, f32[64,1024]{1,0:T(8,128)S(1)}, f32[32,1024]{1,0:T(8,128)S(1)}) custom-call(f32[1]{0:T(128)S(6)} %copy.18.lam_ref, s32[6,1,8]{2,1,0:T(1,128)S(1)} %bitcast.18, f32[8,1024]{1,0:T(8,128)S(1)} %copy-done.3, ...), custom_call_target="tpu_custom_call" | custom-call | flops 2000000000 | bytes 200000 | tf_op jit(solution)/shard_map/pallas_call | solution.py:559
  37.6 3.3 %all-to-all-done.1 = f32[16,24,128]{2,1,0:T(8,128)S(1)} async-done(((f32[16,24,128]{2,1,0:T(8,128)}), f32[16,24,128]{2,1,0:T(8,128)S(1)}, u32[]{:S(2)}, u32[]{:S(2)}) %all-to-all-start.1) | async-done | bytes 196640 | tf_op jit(solution)/shard_map/all_to_all | solution.py:585
  40.9 0.7 copy-done.2
  41.6 1.5 %shard_map.170 = (f32[8,1024]{1,0:T(8,128)S(1)}, f32[8,1024]{1,0:T(8,128)S(1)}, f32[16,1024]{1,0:T(8,128)S(1)}, f32[8,512]{1,0:T(8,128)S(1)}, f32[8,512]{1,0:T(8,128)S(1)}) custom-call(f32[384,128]{1,0:T(8,128)S(1)} %bitcast.15, f32[8,1024]{1,0:T(8,128)S(1)} %copy-done.3, f32[16,1024]{1,0:T(8,128)S(1)} %copy-done.1, ...), custom_call_target="tpu_custom_call" | custom-call | bytes 200000 | tf_op jit(solution)/shard_map/pallas_call | solution.py:559
  43.1 0.8 collective-permute-start.2
  43.9 2.2 %collective-permute-start.3 = (f32[8,512]{1,0:T(8,128)S(1)}, f32[8,512]{1,0:T(8,128)S(1)}, u32[]{:S(2)}, u32[]{:S(2)}) collective-permute-start(f32[8,512]{1,0:T(8,128)S(1)} %get-tuple-element.41), channel_id=1, source_target_pairs={{0,15},{1,0},{2,1},{3,2},{4,3},{5,4},{6,5},{7,6},{8,7},{9,8},{10,9... | collective-permute-start | bytes 49160 | tf_op jit(solution)/shard_map/ppermute | solution.py:573
  46.1 5.1 %shard_map.171.partial_ref = f32[8,1024]{1,0:T(8,128)S(1)} custom-call(f32[1]{0:T(128)S(6)} %copy.18.lam_ref, s32[6,1,8]{2,1,0:T(1,128)S(1)} %bitcast.19, f32[8,1024]{1,0:T(8,128)S(1)} %get-tuple-element.39.data_ref), custom_call_target="tpu_custom_call" | custom-call | flops 2000000000 | bytes 200000 | tf_op jit(solution)/shard_map/pallas_call | solution.py:559
  51.2 0.0 collective-permute-done.2.below_ref
  51.2 2.8 %shard_map.172 = (f32[8,1024]{1,0:T(8,128)S(1)}, f32[16,1024]{1,0:T(8,128)S(1)}, f32[8,512]{1,0:T(8,128)S(1)}, f32[8,512]{1,0:T(8,128)S(1)}) custom-call(f32[1]{0:T(128)S(6)} %copy.18.lam_ref, f32[8,1024]{1,0:T(8,128)S(1)} %get-tuple-element.39.data_ref, f32[8,512]{1,0:T(8,128)S(1)} %collective-permute-done.2.below_ref, ...), custom_call_target="tpu_custom_call" | custom-call | bytes 200000 | tf_op jit(solution)/shard_map/pallas_call | solution.py:559
  54.1 0.0 collective-permute-start.4
  54.1 2.9 %collective-permute-start.5 = (f32[8,512]{1,0:T(8,128)S(1)}, f32[8,512]{1,0:T(8,128)S(1)}, u32[]{:S(2)}, u32[]{:S(2)}) collective-permute-start(f32[8,512]{1,0:T(8,128)S(1)} %get-tuple-element.46), channel_id=1, source_target_pairs={{0,15},{1,0},{2,1},{3,2},{4,3},{5,4},{6,5},{7,6},{8,7},{9,8},{10,9... | collective-permute-start | bytes 49160 | tf_op jit(solution)/shard_map/ppermute | solution.py:573
  57.0 5.1 %shard_map.173.partial_ref = f32[8,1024]{1,0:T(8,128)S(1)} custom-call(f32[1]{0:T(128)S(6)} %copy.18.lam_ref, s32[6,1,8]{2,1,0:T(1,128)S(1)} %bitcast.20, f32[8,1024]{1,0:T(8,128)S(1)} %get-tuple-element.44.data_ref), custom_call_target="tpu_custom_call" | custom-call | flops 2000000000 | bytes 200000 | tf_op jit(solution)/shard_map/pallas_call | solution.py:559
  62.2 2.7 %shard_map.174.here_ref = f32[10,1,1024]{2,1,0:T(1,128)S(1)} custom-call(f32[1]{0:T(128)S(6)} %copy.18.lam_ref, f32[8,1024]{1,0:T(8,128)S(1)} %get-tuple-element.44.data_ref, f32[8,512]{1,0:T(8,128)S(1)} %collective-permute-done.4.below_ref, f32[8,512]{1,0:T(8,128)S(1)} %collective-permute-done.5.above_ref, f32[8,1024]{1,0:T(8,128)S(1)} %shard_map.173.partial_ref, ...), custom_call_target="tpu_custom_call" | custom-call | bytes 200000 | tf_op jit(solution)/shard_map/pallas_call | solution.py:559
  64.9 3.4 %collective-permute-start.6 = (f32[10,1,1024]{2,1,0:T(1,128)S(1)}, f32[10,1,1024]{2,1,0:T(1,128)S(1)}, u32[]{:S(2)}, u32[]{:S(2)}) collective-permute-start(f32[10,1,1024]{2,1,0:T(1,128)S(1)} %shard_map.174.here_ref), channel_id=1, source_target_pairs={{0,16},{16,0},{32,48},{48,32},{64,80},{80,64},{96,112},{112,96},{1... | collective-permute-start | bytes 122888 | tf_op jit(solution)/shard_map/ppermute | solution.py:581
  68.3 2.5 %collective-permute-done.6.there_ref = f32[10,1,1024]{2,1,0:T(1,128)S(1)} collective-permute-done((f32[10,1,1024]{2,1,0:T(1,128)S(1)}, f32[10,1,1024]{2,1,0:T(1,128)S(1)}, u32[]{:S(2)}, u32[]{:S(2)}) %collective-permute-start.6) | collective-permute-done | bytes 40992 | tf_op jit(solution)/shard_map/ppermute | solution.py:581
  70.8 4.5 %collective-permute-start.7 = (f32[10,1,1024]{2,1,0:T(1,128)S(1)}, f32[10,1,1024]{2,1,0:T(1,128)S(1)}, u32[]{:S(2)}, u32[]{:S(2)}) collective-permute-start(f32[10,1,1024]{2,1,0:T(1,128)S(1)} %shard_map.175.here_ref), channel_id=1, source_target_pairs={{16,32},{32,16},{48,64},{64,48},{80,96},{96,80},{112,128},{128,112... | collective-permute-start | bytes 122888 | tf_op jit(solution)/shard_map/ppermute | solution.py:581
  75.4 4.7 %collective-permute-done.7.there_ref = f32[10,1,1024]{2,1,0:T(1,128)S(1)} collective-permute-done((f32[10,1,1024]{2,1,0:T(1,128)S(1)}, f32[10,1,1024]{2,1,0:T(1,128)S(1)}, u32[]{:S(2)}, u32[]{:S(2)}) %collective-permute-start.7) | collective-permute-done | bytes 40992 | tf_op jit(solution)/shard_map/ppermute | solution.py:581
  80.0 0.6 shard_map.176
  (21 shorter events, 0.1 us)
Async XLA Ops:
  4.1 10.6 %copy-start.10 = (f32[8,512]{1,0:T(8,128)S(1)}, f32[8,512]{1,0:T(8,128)}, u32[]{:S(2)}) copy-start(f32[8,512]{1,0:T(8,128)} %get-tuple-element.30) | copy-start | bytes 49156
  4.1 11.1 %copy-start.9 = (f32[8,512]{1,0:T(8,128)S(1)}, f32[8,512]{1,0:T(8,128)}, u32[]{:S(2)}) copy-start(f32[8,512]{1,0:T(8,128)} %get-tuple-element.31) | copy-start | bytes 49156
  4.1 13.6 %copy-start.3 = (f32[8,1024]{1,0:T(8,128)S(1)}, f32[8,1024]{1,0:T(8,128)}, u32[]{:S(2)}) copy-start(f32[8,1024]{1,0:T(8,128)} %get-tuple-element.28.data_ref) | copy-start | bytes 98308
  4.1 13.6 %copy-start.6 = (f32[128,8]{1,0:T(8,128)S(1)}, f32[128,8]{1,0:T(8,128)}, u32[]{:S(2)}) copy-start(f32[128,8]{1,0:T(8,128)} %constant.12.clone.rows_ref) | copy-start | bytes 12292
  4.1 13.6 %copy-start.7 = (f32[17,65]{1,0:T(8,128)S(1)}, f32[17,65]{1,0:T(8,128)}, u32[]{:S(2)}) copy-start(f32[17,65]{1,0:T(8,128)} %constant.11.clone.weights_ref) | copy-start | bytes 13264
  4.1 20.5 %all-to-all-start = ((f32[16,24,128]{2,1,0:T(8,128)}), f32[16,24,128]{2,1,0:T(8,128)S(1)}, u32[]{:S(2)}, u32[]{:S(2)}) async-start(f32[16,24,128]{2,1,0:T(8,128)} %bitcast.21), calls=%async_computation | async-start | bytes 393216 | tf_op jit(solution)/shard_map/all_to_all | solution.py:585
  14.7 3.0 %copy-start.8 = (f32[8,128]{1,0:T(8,128)S(1)}, f32[8,128]{1,0:T(8,128)}, u32[]{:S(2)}) copy-start(f32[8,128]{1,0:T(8,128)} %constant.13.clone.lanes_ref) | copy-start | bytes 12292
  14.7 3.0 %copy-start.5 = (s32[1,8,6]{1,0,2:T(1,128)S(1)}, s32[1,8,6]{1,0,2:T(1,128)}, u32[]{:S(2)}) copy-start(s32[1,8,6]{1,0,2:T(1,128)} %param.22) | copy-start | bytes 580
  14.7 7.4 %collective-permute-start = (f32[8,512]{1,0:T(8,128)S(1)}, f32[8,512]{1,0:T(8,128)S(1)}, u32[]{:S(2)}, u32[]{:S(2)}) collective-permute-start(f32[8,512]{1,0:T(8,128)S(1)} %copy-done.10), channel_id=1, source_target_pairs={{0,1},{1,2},{2,3},{3,4},{4,5},{5,6},{6,7},{7,8},{8,9},{9,10},{10,1... | collective-permute-start | bytes 49160 | tf_op jit(solution)/shard_map/ppermute | solution.py:572
  15.2 6.9 %collective-permute-start.1 = (f32[8,512]{1,0:T(8,128)S(1)}, f32[8,512]{1,0:T(8,128)S(1)}, u32[]{:S(2)}, u32[]{:S(2)}) collective-permute-start(f32[8,512]{1,0:T(8,128)S(1)} %copy-done.9), channel_id=1, source_target_pairs={{0,15},{1,0},{2,1},{3,2},{4,3},{5,4},{6,5},{7,6},{8,7},{9,8},{10,9... | collective-permute-start | bytes 49160 | tf_op jit(solution)/shard_map/ppermute | solution.py:573
  17.7 6.9 %copy-start = (bf16[512,128]{1,0:T(8,128)(2,1)S(1)}, bf16[512,128]{1,0:T(8,128)(2,1)}, u32[]{:S(2)}) copy-start(bf16[512,128]{1,0:T(8,128)(2,1)} %constant.14.clone.basis_ref) | copy-start | bytes 393220
  26.1 4.8 %copy-start.1 = (f32[16,1024]{1,0:T(8,128)S(1)}, f32[16,1024]{1,0:T(8,128)}, u32[]{:S(2)}) copy-start(f32[16,1024]{1,0:T(8,128)} %get-tuple-element.32.move_ref) | copy-start | bytes 196612
  26.1 4.8 %copy-start.4 = (f32[32,32]{1,0:T(8,128)S(1)}, f32[32,32]{1,0:T(8,128)}, u32[]{:S(2)}) copy-start(f32[32,32]{1,0:T(8,128)} %constant.10.clone.slab_hbm.slab_ref) | copy-start | bytes 12292
  26.1 14.8 %all-to-all-start.1 = ((f32[16,24,128]{2,1,0:T(8,128)}), f32[16,24,128]{2,1,0:T(8,128)S(1)}, u32[]{:S(2)}, u32[]{:S(2)}) async-start(f32[16,24,128]{2,1,0:T(8,128)} %bitcast.10), calls=%async_computation.1 | async-start | bytes 393216 | tf_op jit(solution)/shard_map/all_to_all | solution.py:585
  40.9 0.7 copy-start.2
  43.1 8.1 %collective-permute-start.2 = (f32[8,512]{1,0:T(8,128)S(1)}, f32[8,512]{1,0:T(8,128)S(1)}, u32[]{:S(2)}, u32[]{:S(2)}) collective-permute-start(f32[8,512]{1,0:T(8,128)S(1)} %get-tuple-element.40), channel_id=1, source_target_pairs={{0,1},{1,2},{2,3},{3,4},{4,5},{5,6},{6,7},{7,8},{8,9},{9,10},{10,1... | collective-permute-start | bytes 49160 | tf_op jit(solution)/shard_map/ppermute | solution.py:572
  43.9 7.3 %collective-permute-start.3 = (f32[8,512]{1,0:T(8,128)S(1)}, f32[8,512]{1,0:T(8,128)S(1)}, u32[]{:S(2)}, u32[]{:S(2)}) collective-permute-start(f32[8,512]{1,0:T(8,128)S(1)} %get-tuple-element.41), channel_id=1, source_target_pairs={{0,15},{1,0},{2,1},{3,2},{4,3},{5,4},{6,5},{7,6},{8,7},{9,8},{10,9... | collective-permute-start | bytes 49160 | tf_op jit(solution)/shard_map/ppermute | solution.py:573
  54.1 8.1 %collective-permute-start.4 = (f32[8,512]{1,0:T(8,128)S(1)}, f32[8,512]{1,0:T(8,128)S(1)}, u32[]{:S(2)}, u32[]{:S(2)}) collective-permute-start(f32[8,512]{1,0:T(8,128)S(1)} %get-tuple-element.45), channel_id=1, source_target_pairs={{0,1},{1,2},{2,3},{3,4},{4,5},{5,6},{6,7},{7,8},{8,9},{9,10},{10,1... | collective-permute-start | bytes 49160 | tf_op jit(solution)/shard_map/ppermute | solution.py:572
  54.1 8.1 %collective-permute-start.5 = (f32[8,512]{1,0:T(8,128)S(1)}, f32[8,512]{1,0:T(8,128)S(1)}, u32[]{:S(2)}, u32[]{:S(2)}) collective-permute-start(f32[8,512]{1,0:T(8,128)S(1)} %get-tuple-element.46), channel_id=1, source_target_pairs={{0,15},{1,0},{2,1},{3,2},{4,3},{5,4},{6,5},{7,6},{8,7},{9,8},{10,9... | collective-permute-start | bytes 49160 | tf_op jit(solution)/shard_map/ppermute | solution.py:573
  64.9 5.9 %collective-permute-start.6 = (f32[10,1,1024]{2,1,0:T(1,128)S(1)}, f32[10,1,1024]{2,1,0:T(1,128)S(1)}, u32[]{:S(2)}, u32[]{:S(2)}) collective-permute-start(f32[10,1,1024]{2,1,0:T(1,128)S(1)} %shard_map.174.here_ref), channel_id=1, source_target_pairs={{0,16},{16,0},{32,48},{48,32},{64,80},{80,64},{96,112},{112,96},{1... | collective-permute-start | bytes 122888 | tf_op jit(solution)/shard_map/ppermute | solution.py:581
  70.8 9.2 %collective-permute-start.7 = (f32[10,1,1024]{2,1,0:T(1,128)S(1)}, f32[10,1,1024]{2,1,0:T(1,128)S(1)}, u32[]{:S(2)}, u32[]{:S(2)}) collective-permute-start(f32[10,1,1024]{2,1,0:T(1,128)S(1)} %shard_map.175.here_ref), channel_id=1, source_target_pairs={{16,32},{32,16},{48,64},{64,48},{80,96},{96,80},{112,128},{128,112... | collective-permute-start | bytes 122888 | tf_op jit(solution)/shard_map/ppermute | solution.py:581

commit v6 on v5

--- a/solution.py
+++ b/solution.py
@@ -178,12 +178,13 @@
     return (*xyz, q, w)
 
 
-def write_halo(data, lists_ref, low_ref, high_ref):
+def write_halo(data, lists, low_ref, high_ref):
     lane = lax.broadcasted_iota(jnp.int32, (8, CLUSTER), 1)
     for row, out_ref in ((0, low_ref), (1, high_ref)):
         for k in range(HALO // CLUSTER):
             columns = slice(k * CLUSTER, (k + 1) * CLUSTER)
-            index = jnp.broadcast_to(lists_ref[0, row : row + 1, columns] & (CLUSTER - 1), (8, CLUSTER))
+            start = row * HALO + k * CLUSTER
+            index = jnp.broadcast_to(lists[:, start : start + CLUSTER].astype(jnp.int32), (8, CLUSTER))
             first = data[:, 2 * k * CLUSTER : (2 * k + 1) * CLUSTER]
             second = data[:, (2 * k + 1) * CLUSTER : (2 * k + 2) * CLUSTER]
             out_ref[:, columns] = jnp.where(
@@ -223,12 +224,14 @@
         data_ref[i : i + 1, :] = cell + off_ref[i]
     move_ref[6:7, :] = jnp.broadcast_to(flag_ref[0:1, 0:1].astype(F32), (1, A_DEV))
     move_ref[7:8, :] = jnp.broadcast_to(flag_ref[0:1, 1:2].astype(F32), (1, A_DEV))
-    move_ref[11:16, :] = jnp.zeros((5, A_DEV), F32)
+    move_ref[11:12, 0:HALO] = (lists_ref[0, 0:1, :] & (CLUSTER - 1)).astype(F32)
+    move_ref[11:12, HALO : 2 * HALO] = (lists_ref[0, 1:2, :] & (CLUSTER - 1)).astype(F32)
+    move_ref[12:16, :] = jnp.zeros((4, A_DEV), F32)
     data_ref[3:4, :] = charge
     data_ref[4:5, :] = weight
     data_ref[5:6, :] = mass_ref[...]
     data_ref[6:8, :] = jnp.zeros((2, A_DEV), F32)
-    write_halo(data_ref[...], lists_ref, low_ref, high_ref)
+    write_halo(data_ref[...], move_ref[11:12, :], low_ref, high_ref)
 
     off = move_ref[0:3, :]
     cells = [cells_ref[i] for i in range(3)]
@@ -335,7 +338,7 @@
         lanes = slice(b * CLUSTER, (b + 1) * CLUSTER)
         columns[lanes, :] = jnp.concatenate([turns[:, lanes], data_ref[3:8, lanes]], axis=0).T
 
-    def one_cluster(b, carry):
+    def one_cluster(b, side):
         start = pl.multiple_of(b * CLUSTER, CLUSTER)
         for j in range(3):
             a = b if j == 0 else (b + j) % CLUSTERS
@@ -350,11 +353,12 @@
                     other = [jnp.broadcast_to(part[:, i : i + 1], (8, CLUSTER)) for i in range(5)]
                     other[:3] = [x.astype(jnp.int32) for x in other[:3]]
                     for i in range(3):
-                        places[i, here, :] = other[i]
+                        places[3 * side + i, here, :] = other[i]
                     for i in range(2):
-                        factors[i, here, :] = other[3 + i]
+                        factors[2 * side + i, here, :] = other[3 + i]
                 else:
-                    other = [places[i, here, :] for i in range(3)] + [factors[i, here, :] for i in range(2)]
+                    other = [places[3 * side + i, here, :] for i in range(3)]
+                    other += [factors[2 * side + i, here, :] for i in range(2)]
                 terms = pair_terms(own, other, floor_value)
                 total = [p + q for p, q in zip(total, terms)]
                 if j:
@@ -363,9 +367,13 @@
             rows = pl.ds(pl.multiple_of(a * 8, 8), 8)
             for i in range(3):
                 near[i, rows, :] = near[i, rows, :] + (listed(tiles_ref, a, b) * total[i] if j else total[i])
+
+    def two_clusters(k, carry):
+        for side in range(2):
+            one_cluster(2 * k + side, side)
         return carry
 
-    lax.fori_loop(first, last, one_cluster, 0)
+    lax.fori_loop(first // 2, last // 2, two_clusters, 0)
     force_ref[...] = jnp.zeros_like(force_ref)
     ones = jnp.ones((8, CLUSTER), BF16)
     for c in range(CLUSTERS):
@@ -433,7 +441,7 @@
     add_halo_forces(lam_ref, data_ref, below_ref, above_ref, second, force_ref, turns)
 
 
-def advance(force, kicks, data_ref, move_ref, lists_ref, data_out, move_out, low_ref, high_ref):
+def advance(force, kicks, data_ref, move_ref, data_out, move_out, low_ref, high_ref):
     mass = data_ref[5:6, :]
     velocity = move_ref[8:11, :]
     for _ in range(kicks):
@@ -444,7 +452,7 @@
     move_out[8:11, :] = velocity
     data_out[...] = data_ref[...]
     data_out[0:3, :] = move_ref[3:6, :] + off
-    write_halo(data_out[...], lists_ref, low_ref, high_ref)
+    write_halo(data_out[...], move_ref[11:12, :], low_ref, high_ref)
 
 
 def write_tables(move_ref, slab_ref, y_high, y_low, z_ref, x_ref):
@@ -470,7 +478,7 @@
 
 
 def gather_kernel(
-    pot_ref, data_ref, move_ref, short_ref, lists_ref, y_high, y_low, z_ref, x_ref,
+    pot_ref, data_ref, move_ref, short_ref, y_high, y_low, z_ref, x_ref,
     long_ref, data_out, move_out, low_ref, high_ref, force,
 ):
     charge = data_ref[3:4, :]
@@ -500,17 +508,17 @@
     long_ref[...] = jnp.zeros_like(long_ref)
     long_ref[0:3, :] = force[0:3, :]
     advance(
-        short_ref[0:3, :] + force[0:3, :], 1, data_ref, move_ref, lists_ref, data_out, move_out, low_ref, high_ref
+        short_ref[0:3, :] + force[0:3, :], 1, data_ref, move_ref, data_out, move_out, low_ref, high_ref
     )
 
 
 def halo_step_kernel(
-    lam_ref, data_ref, below_ref, above_ref, partial_ref, long_ref, move_ref, lists_ref,
+    lam_ref, data_ref, below_ref, above_ref, partial_ref, long_ref, move_ref,
     data_out, move_out, low_ref, high_ref, turns, force,
 ):
     add_halo_forces(lam_ref, data_ref, below_ref, above_ref, partial_ref, force, turns)
     total = force[0:3, :] + long_ref[0:3, :]
-    advance(total, 2, data_ref, move_ref, lists_ref, data_out, move_out, low_ref, high_ref)
+    advance(total, 2, data_ref, move_ref, data_out, move_out, low_ref, high_ref)
 
 
 def halo_last_kernel(
@@ -594,7 +602,7 @@
     turns = pltpu.VMEM((3, A_DEV), F32)
     pair_scratch = [
         turns, pltpu.VMEM((3, CLUSTERS * 8, CLUSTER), F32), pltpu.VMEM((6, A_DEV, CLUSTER), F32),
-        pltpu.VMEM((A_DEV, 8), F32), pltpu.VMEM((3, CLUSTER, CLUSTER), jnp.int32), pltpu.VMEM((2, CLUSTER, CLUSTER), F32),
+        pltpu.VMEM((A_DEV, 8), F32), pltpu.VMEM((6, CLUSTER, CLUSTER), jnp.int32), pltpu.VMEM((4, CLUSTER, CLUSTER), F32),
     ]
     spare = pltpu.VMEM((8, A_DEV), F32)
     tiles = jnp.transpose(tile_lists, (2, 0, 1))
@@ -658,7 +666,7 @@
     )
     far, data, move, low, high = call(
         gather_kernel,
-        [("v", potential), ("v", data), ("v", move), ("v", short), ("v", halo_lists), *(("v", x) for x in tables)],
+        [("v", potential), ("v", data), ("v", move), ("v", short), *(("v", x) for x in tables)],
         [wide, wide, moving, border, border],
         [spare],
     )
@@ -675,7 +683,6 @@
         halo_step_kernel,
         [
             ("s", lambdas), ("v", data), ("v", below), ("v", above), ("v", short), ("v", far), ("v", move),
-            ("v", halo_lists),
         ],
         [wide, moving, border, border],
         [turns, spare],

time: 81.2 us -> 79.7 us (0.982)
  Pallas kernels: 33.2 us -> 32.2 us
    pallas_call x11, Pallas kernels: 33.2 us -> 32.2 us  [call(): pl.pallas_call(kernel, out_shape=[jax.ShapeDtypeStruct(shape, dtype) for...]
  transfers between devices with their start and end apart: 10 -> 10, of which waited for: 4 -> 5; matrix products, arithmetic and copies ran while one was open for 0% -> 0% of each run, Pallas kernels for 26% -> 26%
where the time goes in v6:
time: 79.7 us; the launch traced here: 79.1 us
  Pallas kernels  32.2 us (40%)
  starting transfers between devices  32.1 us (40%)
  waiting for transfers between devices  13.3 us (17%)
  between operations  1.48 us (2%)
    pallas_call x11, Pallas kernels, call(): pl.pallas_call(kernel, out_shape=[jax.ShapeDtypeStruct(shape, dtype) for...  32.2 us
    all_to_all x2, starting transfers between devices, exchanged(): return lax.all_to_all(value, 'dom', split_axis=0, concat_axis=0, tiled=True)  15.2 us
    ppermute x2, starting transfers between devices, traded(): return lax.ppermute(state, 'lam', pairs)  7.95 us
    ppermute x3, starting transfers between devices, neighbours(): above = lax.ppermute(low, 'dom', [(i, (i - 1) % size) for i in range(size)])  7.67 us
    ppermute x2, waiting for transfers between devices, traded(): return lax.ppermute(state, 'lam', pairs)  7.15 us
    all_to_all x2, waiting for transfers between devices, exchanged(): return lax.all_to_all(value, 'dom', split_axis=0, concat_axis=0, tiled=True)  6.07 us
  transfers between devices with their start and end apart: 10, of which 5 were waited for; matrix products, arithmetic and copies ran while one was open for 0% of the time, Pallas kernels for 26%

profile of v6, /device:TPU:32, one launch (start us, length us, event | category | flops | bytes accessed | tf_op | source)
XLA Modules:
  0.0 79.1 jit_solution(9326126376061528189)
XLA Ops:
  1.3 2.8 %shard_map.166 = (f32[384,128]{1,0:T(8,128)}, f32[8,1024]{1,0:T(8,128)}, f32[16,1024]{1,0:T(8,128)}, f32[8,512]{1,0:T(8,128)}, f32[8,512]{1,0:T(8,128)}) custom-call(f32[1]{0:T(128)S(6)} %copy.18.lam_ref, s32[3,1,1024]{2,1,0:T(1,128)} %bitcast.22, f32[3,1,1024]{2,1,0:T(1,128)} %bitcast.23, f32[3,1,1024]{2,1,0:T(1,128)} %bitcast.24, f32[1,1024]{1,0:T(1,128)} %bitcast.25, ...), custom_call_target="tpu_custom_call" | custom-call | bytes 200000 | tf_op jit(solution)/shard_map/pallas_call | solution.py:567
  4.1 0.0 copy-start.5
  4.1 0.0 copy-start.6
  4.1 10.6 %all-to-all-start = ((f32[16,24,128]{2,1,0:T(8,128)}), f32[16,24,128]{2,1,0:T(8,128)S(1)}, u32[]{:S(2)}, u32[]{:S(2)}) async-start(f32[16,24,128]{2,1,0:T(8,128)} %bitcast.21), calls=%async_computation | async-start | bytes 393216 | tf_op jit(solution)/shard_map/all_to_all | solution.py:593
  14.7 0.0 copy-start.7
  14.7 0.0 copy-start.4
  14.7 0.4 collective-permute-start
  15.1 2.6 %collective-permute-start.1 = (f32[8,512]{1,0:T(8,128)S(1)}, f32[8,512]{1,0:T(8,128)S(1)}, u32[]{:S(2)}, u32[]{:S(2)}) collective-permute-start(f32[8,512]{1,0:T(8,128)S(1)} %copy-done.8), channel_id=1, source_target_pairs={{0,15},{1,0},{2,1},{3,2},{4,3},{5,4},{6,5},{7,6},{8,7},{9,8},{10,9... | collective-permute-start | bytes 49160 | tf_op jit(solution)/shard_map/ppermute | solution.py:581
  17.7 0.0 copy-start
  17.7 4.2 %shard_map.167 = (f32[8,1024]{1,0:T(8,128)S(1)}, f32[2,128,128]{2,1,0:T(8,128)S(1)}) custom-call(f32[1]{0:T(128)S(6)} %copy.18.lam_ref, s32[6,1,8]{2,1,0:T(1,128)S(1)} %bitcast.17, f32[17,65]{1,0:T(8,128)S(1)} %copy-done.6, f32[8,1024]{1,0:T(8,128)S(1)} %copy-done.2, f32[128,8]{1,0:T(8,128)S(1)} %copy-done.5, f32[8,128]{1,0:T(8,128)S(1)} %copy-done.7), custom_call_target="tpu_custom_call" | custom-call | flops 2000000000 | bytes 200000 | tf_op jit(solution)/shard_map/pallas_call | solution.py:567
  21.9 0.1 collective-permute-done.below_ref
  22.0 0.0 collective-permute-done.1.above_ref
  22.0 2.6 %all-to-all-done = f32[16,24,128]{2,1,0:T(8,128)S(1)} async-done(((f32[16,24,128]{2,1,0:T(8,128)}), f32[16,24,128]{2,1,0:T(8,128)S(1)}, u32[]{:S(2)}, u32[]{:S(2)}) %all-to-all-start) | async-done | bytes 196640 | tf_op jit(solution)/shard_map/all_to_all | solution.py:593
  24.6 1.5 %shard_map.168 = f32[384,128]{1,0:T(8,128)} custom-call(f32[384,128]{1,0:T(8,128)S(1)} %bitcast.16, f32[2,128,128]{2,1,0:T(8,128)S(1)} %get-tuple-element.29.gain_ref, bf16[512,128]{1,0:T(8,128)(2,1)S(1)} %copy-done, f32[8,512]{1,0:T(8,128)S(1)} %collective-permute-done.below_ref, f32[8,512]{1,0:T(8,128)S(1)} %collective-permute-done.1.above_ref), custom_call_target="tpu_custom_call" | custom-call | bytes 200000 | tf_op jit(solution)/shard_map/pallas_call | solution.py:567
  26.1 4.7 %all-to-all-start.1 = ((f32[16,24,128]{2,1,0:T(8,128)}), f32[16,24,128]{2,1,0:T(8,128)S(1)}, u32[]{:S(2)}, u32[]{:S(2)}) async-start(f32[16,24,128]{2,1,0:T(8,128)} %bitcast.10), calls=%async_computation.1 | async-start | bytes 393216 | tf_op jit(solution)/shard_map/all_to_all | solution.py:593
  30.8 6.5 %shard_map.169 = (f32[8,1024]{1,0:T(8,128)S(1)}, bf16[128,2048]{1,0:T(8,128)(2,1)S(1)}, bf16[128,2048]{1,0:T(8,128)(2,1)S(1)}, f32[64,1024]{1,0:T(8,128)S(1)}, f32[32,1024]{1,0:T(8,128)S(1)}) custom-call(f32[1]{0:T(128)S(6)} %copy.18.lam_ref, s32[6,1,8]{2,1,0:T(1,128)S(1)} %bitcast.18, f32[8,1024]{1,0:T(8,128)S(1)} %copy-done.2, ...), custom_call_target="tpu_custom_call" | custom-call | flops 2000000000 | bytes 200000 | tf_op jit(solution)/shard_map/pallas_call | solution.py:567
  37.3 3.5 %all-to-all-done.1 = f32[16,24,128]{2,1,0:T(8,128)S(1)} async-done(((f32[16,24,128]{2,1,0:T(8,128)}), f32[16,24,128]{2,1,0:T(8,128)S(1)}, u32[]{:S(2)}, u32[]{:S(2)}) %all-to-all-start.1) | async-done | bytes 196640 | tf_op jit(solution)/shard_map/all_to_all | solution.py:593
  40.7 1.5 %shard_map.170 = (f32[8,1024]{1,0:T(8,128)S(1)}, f32[8,1024]{1,0:T(8,128)S(1)}, f32[16,1024]{1,0:T(8,128)S(1)}, f32[8,512]{1,0:T(8,128)S(1)}, f32[8,512]{1,0:T(8,128)S(1)}) custom-call(f32[384,128]{1,0:T(8,128)S(1)} %bitcast.15, f32[8,1024]{1,0:T(8,128)S(1)} %copy-done.2, f32[16,1024]{1,0:T(8,128)S(1)} %copy-done.1, ...), custom_call_target="tpu_custom_call" | custom-call | bytes 200000 | tf_op jit(solution)/shard_map/pallas_call | solution.py:567
  42.2 0.8 collective-permute-start.2
  43.0 2.2 %collective-permute-start.3 = (f32[8,512]{1,0:T(8,128)S(1)}, f32[8,512]{1,0:T(8,128)S(1)}, u32[]{:S(2)}, u32[]{:S(2)}) collective-permute-start(f32[8,512]{1,0:T(8,128)S(1)} %get-tuple-element.41), channel_id=1, source_target_pairs={{0,15},{1,0},{2,1},{3,2},{4,3},{5,4},{6,5},{7,6},{8,7},{9,8},{10,9... | collective-permute-start | bytes 49160 | tf_op jit(solution)/shard_map/ppermute | solution.py:581
  45.2 4.8 %shard_map.171.partial_ref = f32[8,1024]{1,0:T(8,128)S(1)} custom-call(f32[1]{0:T(128)S(6)} %copy.18.lam_ref, s32[6,1,8]{2,1,0:T(1,128)S(1)} %bitcast.19, f32[8,1024]{1,0:T(8,128)S(1)} %get-tuple-element.39.data_ref), custom_call_target="tpu_custom_call" | custom-call | flops 2000000000 | bytes 200000 | tf_op jit(solution)/shard_map/pallas_call | solution.py:567
  50.0 0.0 collective-permute-done.2.below_ref
  50.0 2.8 %shard_map.172 = (f32[8,1024]{1,0:T(8,128)S(1)}, f32[16,1024]{1,0:T(8,128)S(1)}, f32[8,512]{1,0:T(8,128)S(1)}, f32[8,512]{1,0:T(8,128)S(1)}) custom-call(f32[1]{0:T(128)S(6)} %copy.18.lam_ref, f32[8,1024]{1,0:T(8,128)S(1)} %get-tuple-element.39.data_ref, f32[8,512]{1,0:T(8,128)S(1)} %collective-permute-done.2.below_ref, ...), custom_call_target="tpu_custom_call" | custom-call | bytes 200000 | tf_op jit(solution)/shard_map/pallas_call | solution.py:567
  52.8 0.0 collective-permute-start.4
  52.9 2.9 %collective-permute-start.5 = (f32[8,512]{1,0:T(8,128)S(1)}, f32[8,512]{1,0:T(8,128)S(1)}, u32[]{:S(2)}, u32[]{:S(2)}) collective-permute-start(f32[8,512]{1,0:T(8,128)S(1)} %get-tuple-element.46), channel_id=1, source_target_pairs={{0,15},{1,0},{2,1},{3,2},{4,3},{5,4},{6,5},{7,6},{8,7},{9,8},{10,9... | collective-permute-start | bytes 49160 | tf_op jit(solution)/shard_map/ppermute | solution.py:581
  55.8 4.8 %shard_map.173.partial_ref = f32[8,1024]{1,0:T(8,128)S(1)} custom-call(f32[1]{0:T(128)S(6)} %copy.18.lam_ref, s32[6,1,8]{2,1,0:T(1,128)S(1)} %bitcast.20, f32[8,1024]{1,0:T(8,128)S(1)} %get-tuple-element.44.data_ref), custom_call_target="tpu_custom_call" | custom-call | flops 2000000000 | bytes 200000 | tf_op jit(solution)/shard_map/pallas_call | solution.py:567
  60.6 2.7 %shard_map.174.here_ref = f32[10,1,1024]{2,1,0:T(1,128)S(1)} custom-call(f32[1]{0:T(128)S(6)} %copy.18.lam_ref, f32[8,1024]{1,0:T(8,128)S(1)} %get-tuple-element.44.data_ref, f32[8,512]{1,0:T(8,128)S(1)} %collective-permute-done.4.below_ref, f32[8,512]{1,0:T(8,128)S(1)} %collective-permute-done.5.above_ref, f32[8,1024]{1,0:T(8,128)S(1)} %shard_map.173.partial_ref, ...), custom_call_target="tpu_custom_call" | custom-call | bytes 200000 | tf_op jit(solution)/shard_map/pallas_call | solution.py:567
  63.4 3.4 %collective-permute-start.6 = (f32[10,1,1024]{2,1,0:T(1,128)S(1)}, f32[10,1,1024]{2,1,0:T(1,128)S(1)}, u32[]{:S(2)}, u32[]{:S(2)}) collective-permute-start(f32[10,1,1024]{2,1,0:T(1,128)S(1)} %shard_map.174.here_ref), channel_id=1, source_target_pairs={{0,16},{16,0},{32,48},{48,32},{64,80},{80,64},{96,112},{112,96},{1... | collective-permute-start | bytes 122888 | tf_op jit(solution)/shard_map/ppermute | solution.py:589
  66.8 2.5 %collective-permute-done.6.there_ref = f32[10,1,1024]{2,1,0:T(1,128)S(1)} collective-permute-done((f32[10,1,1024]{2,1,0:T(1,128)S(1)}, f32[10,1,1024]{2,1,0:T(1,128)S(1)}, u32[]{:S(2)}, u32[]{:S(2)}) %collective-permute-start.6) | collective-permute-done | bytes 40992 | tf_op jit(solution)/shard_map/ppermute | solution.py:589
  69.3 4.6 %collective-permute-start.7 = (f32[10,1,1024]{2,1,0:T(1,128)S(1)}, f32[10,1,1024]{2,1,0:T(1,128)S(1)}, u32[]{:S(2)}, u32[]{:S(2)}) collective-permute-start(f32[10,1,1024]{2,1,0:T(1,128)S(1)} %shard_map.175.here_ref), channel_id=1, source_target_pairs={{16,32},{32,16},{48,64},{64,48},{80,96},{96,80},{112,128},{128,112... | collective-permute-start | bytes 122888 | tf_op jit(solution)/shard_map/ppermute | solution.py:589
  73.9 4.7 %collective-permute-done.7.there_ref = f32[10,1,1024]{2,1,0:T(1,128)S(1)} collective-permute-done((f32[10,1,1024]{2,1,0:T(1,128)S(1)}, f32[10,1,1024]{2,1,0:T(1,128)S(1)}, u32[]{:S(2)}, u32[]{:S(2)}) %collective-permute-start.7) | collective-permute-done | bytes 40992 | tf_op jit(solution)/shard_map/ppermute | solution.py:589
  78.5 0.6 shard_map.176
  (19 shorter events, 0.1 us)
Async XLA Ops:
  4.1 10.6 %copy-start.9 = (f32[8,512]{1,0:T(8,128)S(1)}, f32[8,512]{1,0:T(8,128)}, u32[]{:S(2)}) copy-start(f32[8,512]{1,0:T(8,128)} %get-tuple-element.30) | copy-start | bytes 49156
  4.1 11.1 %copy-start.8 = (f32[8,512]{1,0:T(8,128)S(1)}, f32[8,512]{1,0:T(8,128)}, u32[]{:S(2)}) copy-start(f32[8,512]{1,0:T(8,128)} %get-tuple-element.31) | copy-start | bytes 49156
  4.1 13.6 %copy-start.2 = (f32[8,1024]{1,0:T(8,128)S(1)}, f32[8,1024]{1,0:T(8,128)}, u32[]{:S(2)}) copy-start(f32[8,1024]{1,0:T(8,128)} %get-tuple-element.28.data_ref) | copy-start | bytes 98308
  4.1 13.6 %copy-start.5 = (f32[128,8]{1,0:T(8,128)S(1)}, f32[128,8]{1,0:T(8,128)}, u32[]{:S(2)}) copy-start(f32[128,8]{1,0:T(8,128)} %constant.12.clone.rows_ref) | copy-start | bytes 12292
  4.1 13.6 %copy-start.6 = (f32[17,65]{1,0:T(8,128)S(1)}, f32[17,65]{1,0:T(8,128)}, u32[]{:S(2)}) copy-start(f32[17,65]{1,0:T(8,128)} %constant.11.clone.weights_ref) | copy-start | bytes 13264
  4.1 20.5 %all-to-all-start = ((f32[16,24,128]{2,1,0:T(8,128)}), f32[16,24,128]{2,1,0:T(8,128)S(1)}, u32[]{:S(2)}, u32[]{:S(2)}) async-start(f32[16,24,128]{2,1,0:T(8,128)} %bitcast.21), calls=%async_computation | async-start | bytes 393216 | tf_op jit(solution)/shard_map/all_to_all | solution.py:593
  14.7 3.0 %copy-start.7 = (f32[8,128]{1,0:T(8,128)S(1)}, f32[8,128]{1,0:T(8,128)}, u32[]{:S(2)}) copy-start(f32[8,128]{1,0:T(8,128)} %constant.13.clone.lanes_ref) | copy-start | bytes 12292
  14.7 3.0 %copy-start.4 = (s32[1,8,6]{1,0,2:T(1,128)S(1)}, s32[1,8,6]{1,0,2:T(1,128)}, u32[]{:S(2)}) copy-start(s32[1,8,6]{1,0,2:T(1,128)} %param.22) | copy-start | bytes 580
  14.7 7.3 %collective-permute-start = (f32[8,512]{1,0:T(8,128)S(1)}, f32[8,512]{1,0:T(8,128)S(1)}, u32[]{:S(2)}, u32[]{:S(2)}) collective-permute-start(f32[8,512]{1,0:T(8,128)S(1)} %copy-done.9), channel_id=1, source_target_pairs={{0,1},{1,2},{2,3},{3,4},{4,5},{5,6},{6,7},{7,8},{8,9},{9,10},{10,1... | collective-permute-start | bytes 49160 | tf_op jit(solution)/shard_map/ppermute | solution.py:580
  15.1 6.9 %collective-permute-start.1 = (f32[8,512]{1,0:T(8,128)S(1)}, f32[8,512]{1,0:T(8,128)S(1)}, u32[]{:S(2)}, u32[]{:S(2)}) collective-permute-start(f32[8,512]{1,0:T(8,128)S(1)} %copy-done.8), channel_id=1, source_target_pairs={{0,15},{1,0},{2,1},{3,2},{4,3},{5,4},{6,5},{7,6},{8,7},{9,8},{10,9... | collective-permute-start | bytes 49160 | tf_op jit(solution)/shard_map/ppermute | solution.py:581
  17.7 6.9 %copy-start = (bf16[512,128]{1,0:T(8,128)(2,1)S(1)}, bf16[512,128]{1,0:T(8,128)(2,1)}, u32[]{:S(2)}) copy-start(bf16[512,128]{1,0:T(8,128)(2,1)} %constant.14.clone.basis_ref) | copy-start | bytes 393220
  26.1 4.7 %copy-start.1 = (f32[16,1024]{1,0:T(8,128)S(1)}, f32[16,1024]{1,0:T(8,128)}, u32[]{:S(2)}) copy-start(f32[16,1024]{1,0:T(8,128)} %get-tuple-element.32.move_ref) | copy-start | bytes 196612
  26.1 4.7 %copy-start.3 = (f32[32,32]{1,0:T(8,128)S(1)}, f32[32,32]{1,0:T(8,128)}, u32[]{:S(2)}) copy-start(f32[32,32]{1,0:T(8,128)} %constant.10.clone.slab_hbm.slab_ref) | copy-start | bytes 12292
  26.1 14.6 %all-to-all-start.1 = ((f32[16,24,128]{2,1,0:T(8,128)}), f32[16,24,128]{2,1,0:T(8,128)S(1)}, u32[]{:S(2)}, u32[]{:S(2)}) async-start(f32[16,24,128]{2,1,0:T(8,128)} %bitcast.10), calls=%async_computation.1 | async-start | bytes 393216 | tf_op jit(solution)/shard_map/all_to_all | solution.py:593
  42.2 7.8 %collective-permute-start.2 = (f32[8,512]{1,0:T(8,128)S(1)}, f32[8,512]{1,0:T(8,128)S(1)}, u32[]{:S(2)}, u32[]{:S(2)}) collective-permute-start(f32[8,512]{1,0:T(8,128)S(1)} %get-tuple-element.40), channel_id=1, source_target_pairs={{0,1},{1,2},{2,3},{3,4},{4,5},{5,6},{6,7},{7,8},{8,9},{9,10},{10,1... | collective-permute-start | bytes 49160 | tf_op jit(solution)/shard_map/ppermute | solution.py:580
  43.0 7.0 %collective-permute-start.3 = (f32[8,512]{1,0:T(8,128)S(1)}, f32[8,512]{1,0:T(8,128)S(1)}, u32[]{:S(2)}, u32[]{:S(2)}) collective-permute-start(f32[8,512]{1,0:T(8,128)S(1)} %get-tuple-element.41), channel_id=1, source_target_pairs={{0,15},{1,0},{2,1},{3,2},{4,3},{5,4},{6,5},{7,6},{8,7},{9,8},{10,9... | collective-permute-start | bytes 49160 | tf_op jit(solution)/shard_map/ppermute | solution.py:581
  52.8 7.8 %collective-permute-start.4 = (f32[8,512]{1,0:T(8,128)S(1)}, f32[8,512]{1,0:T(8,128)S(1)}, u32[]{:S(2)}, u32[]{:S(2)}) collective-permute-start(f32[8,512]{1,0:T(8,128)S(1)} %get-tuple-element.45), channel_id=1, source_target_pairs={{0,1},{1,2},{2,3},{3,4},{4,5},{5,6},{6,7},{7,8},{8,9},{9,10},{10,1... | collective-permute-start | bytes 49160 | tf_op jit(solution)/shard_map/ppermute | solution.py:580
  52.9 7.8 %collective-permute-start.5 = (f32[8,512]{1,0:T(8,128)S(1)}, f32[8,512]{1,0:T(8,128)S(1)}, u32[]{:S(2)}, u32[]{:S(2)}) collective-permute-start(f32[8,512]{1,0:T(8,128)S(1)} %get-tuple-element.46), channel_id=1, source_target_pairs={{0,15},{1,0},{2,1},{3,2},{4,3},{5,4},{6,5},{7,6},{8,7},{9,8},{10,9... | collective-permute-start | bytes 49160 | tf_op jit(solution)/shard_map/ppermute | solution.py:581
  63.4 5.9 %collective-permute-start.6 = (f32[10,1,1024]{2,1,0:T(1,128)S(1)}, f32[10,1,1024]{2,1,0:T(1,128)S(1)}, u32[]{:S(2)}, u32[]{:S(2)}) collective-permute-start(f32[10,1,1024]{2,1,0:T(1,128)S(1)} %shard_map.174.here_ref), channel_id=1, source_target_pairs={{0,16},{16,0},{32,48},{48,32},{64,80},{80,64},{96,112},{112,96},{1... | collective-permute-start | bytes 122888 | tf_op jit(solution)/shard_map/ppermute | solution.py:589
  69.3 9.2 %collective-permute-start.7 = (f32[10,1,1024]{2,1,0:T(1,128)S(1)}, f32[10,1,1024]{2,1,0:T(1,128)S(1)}, u32[]{:S(2)}, u32[]{:S(2)}) collective-permute-start(f32[10,1,1024]{2,1,0:T(1,128)S(1)} %shard_map.175.here_ref), channel_id=1, source_target_pairs={{16,32},{32,16},{48,64},{64,48},{80,96},{96,80},{112,128},{128,112... | collective-permute-start | bytes 122888 | tf_op jit(solution)/shard_map/ppermute | solution.py:589

commit v7 on v6

--- a/solution.py
+++ b/solution.py
@@ -194,28 +194,12 @@
             )
 
 
-def spread_kernel(
-    lam_ref, cells_hbm, off_hbm, vel_hbm, charge_hbm, coup_hbm, mass_hbm, lists_hbm, slab_hbm, flag_hbm,
-    out_ref, data_ref, move_ref, low_ref, high_ref, mixed_high, mixed_low,
-    cells_ref, off_ref, vel_ref, charge_ref, coup_ref, mass_ref, lists_ref, slab_ref, flag_ref, arrived,
+def state_kernel(
+    lam_ref, cells_ref, off_ref, vel_ref, charge_ref, coup_ref, mass_ref, lists_ref, flag_ref, grid_ref,
+    data_ref, move_ref, low_ref, high_ref,
 ):
-    copies = [
-        pltpu.make_async_copy(source, target, arrived.at[i])
-        for i, (source, target) in enumerate(
-            (
-                (cells_hbm, cells_ref), (off_hbm, off_ref), (vel_hbm, vel_ref), (charge_hbm, charge_ref),
-                (coup_hbm, coup_ref), (mass_hbm, mass_ref), (lists_hbm, lists_ref), (slab_hbm, slab_ref),
-                (flag_hbm, flag_ref),
-            )
-        )
-    ]
-    for copy in copies:
-        copy.start()
-    for copy in copies:
-        copy.wait()
+    del grid_ref
     weight = 1.0 - lam_ref[0] * coup_ref[...]
-    charge = charge_ref[...] * weight
-
     for i in range(3):
         cell = cells_ref[i].astype(F32)
         move_ref[i : i + 1, :] = off_ref[i]
@@ -227,13 +211,34 @@
     move_ref[11:12, 0:HALO] = (lists_ref[0, 0:1, :] & (CLUSTER - 1)).astype(F32)
     move_ref[11:12, HALO : 2 * HALO] = (lists_ref[0, 1:2, :] & (CLUSTER - 1)).astype(F32)
     move_ref[12:16, :] = jnp.zeros((4, A_DEV), F32)
-    data_ref[3:4, :] = charge
+    data_ref[3:4, :] = charge_ref[...] * weight
     data_ref[4:5, :] = weight
     data_ref[5:6, :] = mass_ref[...]
     data_ref[6:8, :] = jnp.zeros((2, A_DEV), F32)
     write_halo(data_ref[...], move_ref[11:12, :], low_ref, high_ref)
 
-    off = move_ref[0:3, :]
+
+def spread_kernel(
+    lam_ref, cells_hbm, off_hbm, charge_hbm, coup_hbm, slab_hbm,
+    out_ref, mixed_high, mixed_low, cells_ref, off_ref, charge_ref, coup_ref, slab_ref, rows_ref, arrived,
+):
+    copies = [
+        pltpu.make_async_copy(source, target, arrived.at[i])
+        for i, (source, target) in enumerate(
+            (
+                (cells_hbm, cells_ref), (off_hbm, off_ref), (charge_hbm, charge_ref), (coup_hbm, coup_ref),
+                (slab_hbm, slab_ref),
+            )
+        )
+    ]
+    for copy in copies:
+        copy.start()
+    for copy in copies:
+        copy.wait()
+    charge = charge_ref[...] * (1.0 - lam_ref[0] * coup_ref[...])
+    for i in range(3):
+        rows_ref[i : i + 1, :] = off_ref[i]
+    off = rows_ref[0:3, :]
     cells = [cells_ref[i] for i in range(3)]
     weights, _ = spline_set(off)
     row = iota_rows(16, A_DEV)
@@ -368,12 +373,12 @@
             for i in range(3):
                 near[i, rows, :] = near[i, rows, :] + (listed(tiles_ref, a, b) * total[i] if j else total[i])
 
-    def two_clusters(k, carry):
-        for side in range(2):
-            one_cluster(2 * k + side, side)
+    def four_clusters(k, carry):
+        for side in range(4):
+            one_cluster(4 * k + side, side)
         return carry
 
-    lax.fori_loop(first // 2, last // 2, two_clusters, 0)
+    lax.fori_loop(first // 4, last // 4, four_clusters, 0)
     force_ref[...] = jnp.zeros_like(force_ref)
     ones = jnp.ones((8, CLUSTER), BF16)
     for c in range(CLUSTERS):
@@ -427,7 +432,12 @@
                 )
         return carry
 
-    lax.fori_loop(0, HALO // CLUSTER, one_pair, 0)
+    def two_pairs(k, carry):
+        for side in range(2):
+            one_pair(2 * k + side, carry)
+        return carry
+
+    lax.fori_loop(0, HALO // CLUSTER // 2, two_pairs, 0)
 
 
 def rest_kernel(
@@ -602,7 +612,7 @@
     turns = pltpu.VMEM((3, A_DEV), F32)
     pair_scratch = [
         turns, pltpu.VMEM((3, CLUSTERS * 8, CLUSTER), F32), pltpu.VMEM((6, A_DEV, CLUSTER), F32),
-        pltpu.VMEM((A_DEV, 8), F32), pltpu.VMEM((6, CLUSTER, CLUSTER), jnp.int32), pltpu.VMEM((4, CLUSTER, CLUSTER), F32),
+        pltpu.VMEM((A_DEV, 8), F32), pltpu.VMEM((12, CLUSTER, CLUSTER), jnp.int32), pltpu.VMEM((8, CLUSTER, CLUSTER), F32),
     ]
     spare = pltpu.VMEM((8, A_DEV), F32)
     tiles = jnp.transpose(tile_lists, (2, 0, 1))
@@ -619,22 +629,28 @@
         return jnp.transpose(x, (1, 0, 2))
 
 
-    grid, data, move, low, high = call(
+    rows = [by_row(x) for x in (cells, offsets, velocities)]
+    whole, some = (3, 1, A_DEV), (1, A_DEV)
+    (grid,) = call(
         spread_kernel,
         [
-            ("s", lambdas), ("a", by_row(cells)), ("a", by_row(offsets)), ("a", by_row(velocities)),
-            ("a", charges[None]), ("a", coupling[None]), ("a", inverse_mass[None]), ("a", halo_lists), ("a", slab),
-            ("a", accept_flags.T),
+            ("s", lambdas), ("a", rows[0]), ("a", rows[1]), ("a", charges[None]), ("a", coupling[None]), ("a", slab),
         ],
-        [((ROWS, K), F32), wide, moving, border, border],
+        [((ROWS, K), F32)],
         [
-            pltpu.VMEM((ROWS, A_DEV), BF16), pltpu.VMEM((ROWS, A_DEV), BF16),
-            pltpu.VMEM((3, 1, A_DEV), jnp.int32), pltpu.VMEM((3, 1, A_DEV), F32), pltpu.VMEM((3, 1, A_DEV), F32),
-            pltpu.VMEM((1, A_DEV), F32), pltpu.VMEM((1, A_DEV), F32), pltpu.VMEM((1, A_DEV), F32),
-            pltpu.VMEM((1, 2, HALO), jnp.int32), pltpu.VMEM((MODES, MODES), F32), pltpu.VMEM((1, 2), jnp.int32),
-            pltpu.SemaphoreType.DMA((9,)),
+            pltpu.VMEM((ROWS, A_DEV), BF16), pltpu.VMEM((ROWS, A_DEV), BF16), pltpu.VMEM(whole, jnp.int32),
+            pltpu.VMEM(whole, F32), pltpu.VMEM(some, F32), pltpu.VMEM(some, F32), pltpu.VMEM((MODES, MODES), F32),
+            pltpu.VMEM((8, A_DEV), F32), pltpu.SemaphoreType.DMA((5,)),
         ],
         limit=60,
+    )
+    data, move, low, high = call(
+        state_kernel,
+        [
+            ("s", lambdas), *(("v", x) for x in rows), ("v", charges[None]), ("v", coupling[None]),
+            ("v", inverse_mass[None]), ("v", halo_lists), ("v", accept_flags.T), ("a", grid),
+        ],
+        [wide, moving, border, border],
     )
     grid = exchanged(grid)
     below, above = neighbours(low, high)

time: 79.7 us -> 79.4 us (level)
  Pallas kernels: 32.2 us -> 30.6 us
    pallas_call x11 -> x12, Pallas kernels: 32.2 us -> 30.6 us  [call(): pl.pallas_call(kernel, out_shape=[jax.ShapeDtypeStruct(shape, dtype) for...]
  transfers between devices with their start and end apart: 10 -> 10, of which waited for: 5 -> 4; matrix products, arithmetic and copies ran while one was open for 0% -> 0% of each run, Pallas kernels for 26% -> 25%
where the time goes in v7:
time: 79.4 us; the launch traced here: 78.8 us
  starting transfers between devices  32.8 us (41%)
  Pallas kernels  30.6 us (39%)
  waiting for transfers between devices  13.2 us (17%)
  between operations  1.58 us (2%)
    pallas_call x12, Pallas kernels, call(): pl.pallas_call(kernel, out_shape=[jax.ShapeDtypeStruct(shape, dtype) for...  30.6 us
    all_to_all x2, starting transfers between devices, exchanged(): return lax.all_to_all(value, 'dom', split_axis=0, concat_axis=0, tiled=True)  15.9 us
    ppermute x2, starting transfers between devices, traded(): return lax.ppermute(state, 'lam', pairs)  7.96 us
    ppermute x3, starting transfers between devices, neighbours(): above = lax.ppermute(low, 'dom', [(i, (i - 1) % size) for i in range(size)])  7.66 us
    ppermute x2, waiting for transfers between devices, traded(): return lax.ppermute(state, 'lam', pairs)  7.14 us
    all_to_all x2, waiting for transfers between devices, exchanged(): return lax.all_to_all(value, 'dom', split_axis=0, concat_axis=0, tiled=True)  6.06 us
  transfers between devices with their start and end apart: 10, of which 4 were waited for; matrix products, arithmetic and copies ran while one was open for 0% of the time, Pallas kernels for 25%

profile of v7, /device:TPU:32, one launch (start us, length us, event | category | flops | bytes accessed | tf_op | source)
XLA Modules:
  0.0 78.8 jit_solution(814871979948466100)
XLA Ops:
  1.3 2.7 %shard_map.166.grid_ref = f32[384,128]{1,0:T(8,128)} custom-call(f32[1]{0:T(128)S(6)} %copy.18.lam_ref, s32[3,1,1024]{2,1,0:T(1,128)} %bitcast.18, f32[3,1,1024]{2,1,0:T(1,128)} %bitcast.20, f32[1,1024]{1,0:T(1,128)} %bitcast.22, f32[1,1024]{1,0:T(1,128)} %bitcast.24, f32[32,32]{1,0:T(8,128)} %constant.10.clone.slab_hbm.slab_ref), custom_call_target="tpu_custom_call" | custom-call | bytes 200000 | tf_op jit(solution)/shard_map/pallas_call | solution.py:577
  4.0 0.0 copy-start.5
  4.0 0.0 copy-start.7
  4.0 10.6 %all-to-all-start = ((f32[16,24,128]{2,1,0:T(8,128)}), f32[16,24,128]{2,1,0:T(8,128)S(1)}, u32[]{:S(2)}, u32[]{:S(2)}) async-start(f32[16,24,128]{2,1,0:T(8,128)} %bitcast.15), calls=%async_computation | async-start | bytes 393216 | tf_op jit(solution)/shard_map/all_to_all | solution.py:603
  14.6 0.0 copy-start.4
  14.7 0.6 copy-done.4
  15.3 0.1 shard_map.167
  15.4 0.0 copy-start.14
  15.5 0.4 collective-permute-start
  15.9 2.5 %collective-permute-start.1 = (f32[8,512]{1,0:T(8,128)S(1)}, f32[8,512]{1,0:T(8,128)S(1)}, u32[]{:S(2)}, u32[]{:S(2)}) collective-permute-start(f32[8,512]{1,0:T(8,128)S(1)} %get-tuple-element.29), channel_id=1, source_target_pairs={{0,15},{1,0},{2,1},{3,2},{4,3},{5,4},{6,5},{7,6},{8,7},{9,8},{10,9... | collective-permute-start | bytes 49160 | tf_op jit(solution)/shard_map/ppermute | solution.py:591
  18.4 0.0 copy-start.1
  18.4 4.1 %shard_map.168 = (f32[8,1024]{1,0:T(8,128)S(1)}, f32[2,128,128]{2,1,0:T(8,128)S(1)}) custom-call(f32[1]{0:T(128)S(6)} %copy.18.lam_ref, s32[6,1,8]{2,1,0:T(1,128)S(1)} %bitcast.29, f32[17,65]{1,0:T(8,128)S(1)} %copy-done.13, f32[8,1024]{1,0:T(8,128)S(1)} %get-tuple-element.26.data_ref, f32[128,8]{1,0:T(8,128)S(1)} %copy-done.12, f32[8,128]{1,0:T(8,128)S(1)} %copy-done.14), custom_call_target="tpu_custom_call" | custom-call | flops 2000000000 | bytes 200000 | tf_op jit(solution)/shard_map/pallas_call | solution.py:577
  22.5 0.0 collective-permute-done.below_ref
  22.5 2.0 %all-to-all-done = f32[16,24,128]{2,1,0:T(8,128)S(1)} async-done(((f32[16,24,128]{2,1,0:T(8,128)}), f32[16,24,128]{2,1,0:T(8,128)S(1)}, u32[]{:S(2)}, u32[]{:S(2)}) %all-to-all-start) | async-done | bytes 196640 | tf_op jit(solution)/shard_map/all_to_all | solution.py:603
  24.6 1.5 %shard_map.169 = f32[384,128]{1,0:T(8,128)} custom-call(f32[384,128]{1,0:T(8,128)S(1)} %bitcast.17, f32[2,128,128]{2,1,0:T(8,128)S(1)} %get-tuple-element.27.gain_ref, bf16[512,128]{1,0:T(8,128)(2,1)S(1)} %copy-done.1, f32[8,512]{1,0:T(8,128)S(1)} %collective-permute-done.below_ref, f32[8,512]{1,0:T(8,128)S(1)} %collective-permute-done.1.above_ref), custom_call_target="tpu_custom_call" | custom-call | bytes 200000 | tf_op jit(solution)/shard_map/pallas_call | solution.py:577
  26.0 5.4 %all-to-all-start.1 = ((f32[16,24,128]{2,1,0:T(8,128)}), f32[16,24,128]{2,1,0:T(8,128)S(1)}, u32[]{:S(2)}, u32[]{:S(2)}) async-start(f32[16,24,128]{2,1,0:T(8,128)} %bitcast.10), calls=%async_computation.1 | async-start | bytes 393216 | tf_op jit(solution)/shard_map/all_to_all | solution.py:603
  31.4 5.9 %shard_map.170 = (f32[8,1024]{1,0:T(8,128)S(1)}, bf16[128,2048]{1,0:T(8,128)(2,1)S(1)}, bf16[128,2048]{1,0:T(8,128)(2,1)S(1)}, f32[64,1024]{1,0:T(8,128)S(1)}, f32[32,1024]{1,0:T(8,128)S(1)}) custom-call(f32[1]{0:T(128)S(6)} %copy.18.lam_ref, s32[6,1,8]{2,1,0:T(1,128)S(1)} %bitcast.30, f32[8,1024]{1,0:T(8,128)S(1)} %get-tuple-element.26.data_ref, ...), custom_call_target="tpu_custom_call" | custom-call | flops 2000000000 | bytes 200000 | tf_op jit(solution)/shard_map/pallas_call | solution.py:577
  37.3 4.0 %all-to-all-done.1 = f32[16,24,128]{2,1,0:T(8,128)S(1)} async-done(((f32[16,24,128]{2,1,0:T(8,128)}), f32[16,24,128]{2,1,0:T(8,128)S(1)}, u32[]{:S(2)}, u32[]{:S(2)}) %all-to-all-start.1) | async-done | bytes 196640 | tf_op jit(solution)/shard_map/all_to_all | solution.py:603
  41.3 1.5 %shard_map.171 = (f32[8,1024]{1,0:T(8,128)S(1)}, f32[8,1024]{1,0:T(8,128)S(1)}, f32[16,1024]{1,0:T(8,128)S(1)}, f32[8,512]{1,0:T(8,128)S(1)}, f32[8,512]{1,0:T(8,128)S(1)}) custom-call(f32[384,128]{1,0:T(8,128)S(1)} %bitcast.16, f32[8,1024]{1,0:T(8,128)S(1)} %get-tuple-element.26.data_ref, f32[16,1024]{1,0:T(8,128)S(1)} %get-tuple-element.30.move_ref, ...), custom_call_target="tpu_custom_call" | custom-call | bytes 200000 | tf_op jit(solution)/shard_map/pallas_call | solution.py:577
  42.8 0.8 %collective-permute-start.2 = (f32[8,512]{1,0:T(8,128)S(1)}, f32[8,512]{1,0:T(8,128)S(1)}, u32[]{:S(2)}, u32[]{:S(2)}) collective-permute-start(f32[8,512]{1,0:T(8,128)S(1)} %get-tuple-element.38), channel_id=1, source_target_pairs={{0,1},{1,2},{2,3},{3,4},{4,5},{5,6},{6,7},{7,8},{8,9},{9,10},{10,1... | collective-permute-start | bytes 49160 | tf_op jit(solution)/shard_map/ppermute | solution.py:590
  43.6 2.2 %collective-permute-start.3 = (f32[8,512]{1,0:T(8,128)S(1)}, f32[8,512]{1,0:T(8,128)S(1)}, u32[]{:S(2)}, u32[]{:S(2)}) collective-permute-start(f32[8,512]{1,0:T(8,128)S(1)} %get-tuple-element.39), channel_id=1, source_target_pairs={{0,15},{1,0},{2,1},{3,2},{4,3},{5,4},{6,5},{7,6},{8,7},{9,8},{10,9... | collective-permute-start | bytes 49160 | tf_op jit(solution)/shard_map/ppermute | solution.py:591
  45.8 4.6 %shard_map.172.partial_ref = f32[8,1024]{1,0:T(8,128)S(1)} custom-call(f32[1]{0:T(128)S(6)} %copy.18.lam_ref, s32[6,1,8]{2,1,0:T(1,128)S(1)} %bitcast.31, f32[8,1024]{1,0:T(8,128)S(1)} %get-tuple-element.37.data_ref), custom_call_target="tpu_custom_call" | custom-call | flops 2000000000 | bytes 200000 | tf_op jit(solution)/shard_map/pallas_call | solution.py:577
  50.4 2.5 %shard_map.173 = (f32[8,1024]{1,0:T(8,128)S(1)}, f32[16,1024]{1,0:T(8,128)S(1)}, f32[8,512]{1,0:T(8,128)S(1)}, f32[8,512]{1,0:T(8,128)S(1)}) custom-call(f32[1]{0:T(128)S(6)} %copy.18.lam_ref, f32[8,1024]{1,0:T(8,128)S(1)} %get-tuple-element.37.data_ref, f32[8,512]{1,0:T(8,128)S(1)} %collective-permute-done.2.below_ref, ...), custom_call_target="tpu_custom_call" | custom-call | bytes 200000 | tf_op jit(solution)/shard_map/pallas_call | solution.py:577
  53.0 0.0 collective-permute-start.4
  53.0 2.9 %collective-permute-start.5 = (f32[8,512]{1,0:T(8,128)S(1)}, f32[8,512]{1,0:T(8,128)S(1)}, u32[]{:S(2)}, u32[]{:S(2)}) collective-permute-start(f32[8,512]{1,0:T(8,128)S(1)} %get-tuple-element.44), channel_id=1, source_target_pairs={{0,15},{1,0},{2,1},{3,2},{4,3},{5,4},{6,5},{7,6},{8,7},{9,8},{10,9... | collective-permute-start | bytes 49160 | tf_op jit(solution)/shard_map/ppermute | solution.py:591
  56.0 4.6 %shard_map.174.partial_ref = f32[8,1024]{1,0:T(8,128)S(1)} custom-call(f32[1]{0:T(128)S(6)} %copy.18.lam_ref, s32[6,1,8]{2,1,0:T(1,128)S(1)} %bitcast.32, f32[8,1024]{1,0:T(8,128)S(1)} %get-tuple-element.42.data_ref), custom_call_target="tpu_custom_call" | custom-call | flops 2000000000 | bytes 200000 | tf_op jit(solution)/shard_map/pallas_call | solution.py:577
  60.6 2.4 %shard_map.175.here_ref = f32[10,1,1024]{2,1,0:T(1,128)S(1)} custom-call(f32[1]{0:T(128)S(6)} %copy.18.lam_ref, f32[8,1024]{1,0:T(8,128)S(1)} %get-tuple-element.42.data_ref, f32[8,512]{1,0:T(8,128)S(1)} %collective-permute-done.4.below_ref, f32[8,512]{1,0:T(8,128)S(1)} %collective-permute-done.5.above_ref, f32[8,1024]{1,0:T(8,128)S(1)} %shard_map.174.partial_ref, ...), custom_call_target="tpu_custom_call" | custom-call | bytes 200000 | tf_op jit(solution)/shard_map/pallas_call | solution.py:577
  63.1 3.4 %collective-permute-start.6 = (f32[10,1,1024]{2,1,0:T(1,128)S(1)}, f32[10,1,1024]{2,1,0:T(1,128)S(1)}, u32[]{:S(2)}, u32[]{:S(2)}) collective-permute-start(f32[10,1,1024]{2,1,0:T(1,128)S(1)} %shard_map.175.here_ref), channel_id=1, source_target_pairs={{0,16},{16,0},{32,48},{48,32},{64,80},{80,64},{96,112},{112,96},{1... | collective-permute-start | bytes 122888 | tf_op jit(solution)/shard_map/ppermute | solution.py:599
  66.5 2.5 %collective-permute-done.6.there_ref = f32[10,1,1024]{2,1,0:T(1,128)S(1)} collective-permute-done((f32[10,1,1024]{2,1,0:T(1,128)S(1)}, f32[10,1,1024]{2,1,0:T(1,128)S(1)}, u32[]{:S(2)}, u32[]{:S(2)}) %collective-permute-start.6) | collective-permute-done | bytes 40992 | tf_op jit(solution)/shard_map/ppermute | solution.py:599
  69.0 4.6 %collective-permute-start.7 = (f32[10,1,1024]{2,1,0:T(1,128)S(1)}, f32[10,1,1024]{2,1,0:T(1,128)S(1)}, u32[]{:S(2)}, u32[]{:S(2)}) collective-permute-start(f32[10,1,1024]{2,1,0:T(1,128)S(1)} %shard_map.176.here_ref), channel_id=1, source_target_pairs={{16,32},{32,16},{48,64},{64,48},{80,96},{96,80},{112,128},{128,112... | collective-permute-start | bytes 122888 | tf_op jit(solution)/shard_map/ppermute | solution.py:599
  73.5 4.7 %collective-permute-done.7.there_ref = f32[10,1,1024]{2,1,0:T(1,128)S(1)} collective-permute-done((f32[10,1,1024]{2,1,0:T(1,128)S(1)}, f32[10,1,1024]{2,1,0:T(1,128)S(1)}, u32[]{:S(2)}, u32[]{:S(2)}) %collective-permute-start.7) | collective-permute-done | bytes 40992 | tf_op jit(solution)/shard_map/ppermute | solution.py:599
  78.2 0.6 shard_map.177
  (30 shorter events, 0.1 us)
Async XLA Ops:
  4.0 10.7 %copy-start = (f32[384,128]{1,0:T(8,128)S(1)}, f32[384,128]{1,0:T(8,128)}, u32[]{:S(2)}) copy-start(f32[384,128]{1,0:T(8,128)} %shard_map.166.grid_ref) | copy-start | bytes 589828
  4.0 10.7 %copy-start.2 = (s32[1,3,1024]{2,0,1:T(1,128)S(1)}, s32[1,3,1024]{2,0,1:T(1,128)}, u32[]{:S(2)}) copy-start(s32[1,3,1024]{2,0,1:T(1,128)} %param.15) | copy-start | bytes 36868
  4.0 10.7 %copy-start.3 = (f32[1,3,1024]{2,0,1:T(1,128)S(1)}, f32[1,3,1024]{2,0,1:T(1,128)}, u32[]{:S(2)}) copy-start(f32[1,3,1024]{2,0,1:T(1,128)} %param.16) | copy-start | bytes 36868
  4.0 10.7 %copy-start.5 = (f32[1024]{0:T(1024)S(1)}, f32[1024]{0:T(1024)}, u32[]{:S(2)}) copy-start(f32[1024]{0:T(1024)} %param.19) | copy-start | bytes 12292
  4.0 10.7 %copy-start.7 = (f32[1,3,1024]{2,0,1:T(1,128)S(1)}, f32[1,3,1024]{2,0,1:T(1,128)}, u32[]{:S(2)}) copy-start(f32[1,3,1024]{2,0,1:T(1,128)} %param.17) | copy-start | bytes 36868
  4.0 10.7 %copy-start.8 = (f32[1024]{0:T(1024)S(1)}, f32[1024]{0:T(1024)}, u32[]{:S(2)}) copy-start(f32[1024]{0:T(1024)} %param.20) | copy-start | bytes 12292
  4.0 10.7 %copy-start.9 = (s32[1,2,512]{2,1,0:T(2,128)S(1)}, s32[1,2,512]{2,1,0:T(2,128)}, u32[]{:S(2)}) copy-start(s32[1,2,512]{2,1,0:T(2,128)} %lists_ref.1) | copy-start | bytes 12292
  4.0 20.5 %all-to-all-start = ((f32[16,24,128]{2,1,0:T(8,128)}), f32[16,24,128]{2,1,0:T(8,128)S(1)}, u32[]{:S(2)}, u32[]{:S(2)}) async-start(f32[16,24,128]{2,1,0:T(8,128)} %bitcast.15), calls=%async_computation | async-start | bytes 393216 | tf_op jit(solution)/shard_map/all_to_all | solution.py:603
  14.6 0.7 copy-start.4
  14.6 0.7 copy-start.10
  15.3 3.1 %copy-start.12 = (f32[128,8]{1,0:T(8,128)S(1)}, f32[128,8]{1,0:T(8,128)}, u32[]{:S(2)}) copy-start(f32[128,8]{1,0:T(8,128)} %constant.12.clone.rows_ref) | copy-start | bytes 12292
  15.3 3.1 %copy-start.13 = (f32[17,65]{1,0:T(8,128)S(1)}, f32[17,65]{1,0:T(8,128)}, u32[]{:S(2)}) copy-start(f32[17,65]{1,0:T(8,128)} %constant.11.clone.weights_ref) | copy-start | bytes 13264
  15.4 3.0 %copy-start.14 = (f32[8,128]{1,0:T(8,128)S(1)}, f32[8,128]{1,0:T(8,128)}, u32[]{:S(2)}) copy-start(f32[8,128]{1,0:T(8,128)} %constant.13.clone.lanes_ref) | copy-start | bytes 12292
  15.4 3.0 %copy-start.11 = (s32[1,8,6]{1,0,2:T(1,128)S(1)}, s32[1,8,6]{1,0,2:T(1,128)}, u32[]{:S(2)}) copy-start(s32[1,8,6]{1,0,2:T(1,128)} %param.22) | copy-start | bytes 580
  15.5 7.1 %collective-permute-start = (f32[8,512]{1,0:T(8,128)S(1)}, f32[8,512]{1,0:T(8,128)S(1)}, u32[]{:S(2)}, u32[]{:S(2)}) collective-permute-start(f32[8,512]{1,0:T(8,128)S(1)} %get-tuple-element.28), channel_id=1, source_target_pairs={{0,1},{1,2},{2,3},{3,4},{4,5},{5,6},{6,7},{7,8},{8,9},{9,10},{10,1... | collective-permute-start | bytes 49160 | tf_op jit(solution)/shard_map/ppermute | solution.py:590
  15.9 6.7 %collective-permute-start.1 = (f32[8,512]{1,0:T(8,128)S(1)}, f32[8,512]{1,0:T(8,128)S(1)}, u32[]{:S(2)}, u32[]{:S(2)}) collective-permute-start(f32[8,512]{1,0:T(8,128)S(1)} %get-tuple-element.29), channel_id=1, source_target_pairs={{0,15},{1,0},{2,1},{3,2},{4,3},{5,4},{6,5},{7,6},{8,7},{9,8},{10,9... | collective-permute-start | bytes 49160 | tf_op jit(solution)/shard_map/ppermute | solution.py:591
  18.4 6.1 %copy-start.1 = (bf16[512,128]{1,0:T(8,128)(2,1)S(1)}, bf16[512,128]{1,0:T(8,128)(2,1)}, u32[]{:S(2)}) copy-start(bf16[512,128]{1,0:T(8,128)(2,1)} %constant.14.clone.basis_ref) | copy-start | bytes 393220
  26.0 5.4 %copy-start.6 = (f32[32,32]{1,0:T(8,128)S(1)}, f32[32,32]{1,0:T(8,128)}, u32[]{:S(2)}) copy-start(f32[32,32]{1,0:T(8,128)} %constant.10.clone.slab_hbm.slab_ref) | copy-start | bytes 12292
  26.0 15.3 %all-to-all-start.1 = ((f32[16,24,128]{2,1,0:T(8,128)}), f32[16,24,128]{2,1,0:T(8,128)S(1)}, u32[]{:S(2)}, u32[]{:S(2)}) async-start(f32[16,24,128]{2,1,0:T(8,128)} %bitcast.10), calls=%async_computation.1 | async-start | bytes 393216 | tf_op jit(solution)/shard_map/all_to_all | solution.py:603
  42.8 7.6 %collective-permute-start.2 = (f32[8,512]{1,0:T(8,128)S(1)}, f32[8,512]{1,0:T(8,128)S(1)}, u32[]{:S(2)}, u32[]{:S(2)}) collective-permute-start(f32[8,512]{1,0:T(8,128)S(1)} %get-tuple-element.38), channel_id=1, source_target_pairs={{0,1},{1,2},{2,3},{3,4},{4,5},{5,6},{6,7},{7,8},{8,9},{9,10},{10,1... | collective-permute-start | bytes 49160 | tf_op jit(solution)/shard_map/ppermute | solution.py:590
  43.6 6.8 %collective-permute-start.3 = (f32[8,512]{1,0:T(8,128)S(1)}, f32[8,512]{1,0:T(8,128)S(1)}, u32[]{:S(2)}, u32[]{:S(2)}) collective-permute-start(f32[8,512]{1,0:T(8,128)S(1)} %get-tuple-element.39), channel_id=1, source_target_pairs={{0,15},{1,0},{2,1},{3,2},{4,3},{5,4},{6,5},{7,6},{8,7},{9,8},{10,9... | collective-permute-start | bytes 49160 | tf_op jit(solution)/shard_map/ppermute | solution.py:591
  53.0 7.6 %collective-permute-start.4 = (f32[8,512]{1,0:T(8,128)S(1)}, f32[8,512]{1,0:T(8,128)S(1)}, u32[]{:S(2)}, u32[]{:S(2)}) collective-permute-start(f32[8,512]{1,0:T(8,128)S(1)} %get-tuple-element.43), channel_id=1, source_target_pairs={{0,1},{1,2},{2,3},{3,4},{4,5},{5,6},{6,7},{7,8},{8,9},{9,10},{10,1... | collective-permute-start | bytes 49160 | tf_op jit(solution)/shard_map/ppermute | solution.py:590
  53.0 7.6 %collective-permute-start.5 = (f32[8,512]{1,0:T(8,128)S(1)}, f32[8,512]{1,0:T(8,128)S(1)}, u32[]{:S(2)}, u32[]{:S(2)}) collective-permute-start(f32[8,512]{1,0:T(8,128)S(1)} %get-tuple-element.44), channel_id=1, source_target_pairs={{0,15},{1,0},{2,1},{3,2},{4,3},{5,4},{6,5},{7,6},{8,7},{9,8},{10,9... | collective-permute-start | bytes 49160 | tf_op jit(solution)/shard_map/ppermute | solution.py:591
  63.1 5.9 %collective-permute-start.6 = (f32[10,1,1024]{2,1,0:T(1,128)S(1)}, f32[10,1,1024]{2,1,0:T(1,128)S(1)}, u32[]{:S(2)}, u32[]{:S(2)}) collective-permute-start(f32[10,1,1024]{2,1,0:T(1,128)S(1)} %shard_map.175.here_ref), channel_id=1, source_target_pairs={{0,16},{16,0},{32,48},{48,32},{64,80},{80,64},{96,112},{112,96},{1... | collective-permute-start | bytes 122888 | tf_op jit(solution)/shard_map/ppermute | solution.py:599
  69.0 9.2 %collective-permute-start.7 = (f32[10,1,1024]{2,1,0:T(1,128)S(1)}, f32[10,1,1024]{2,1,0:T(1,128)S(1)}, u32[]{:S(2)}, u32[]{:S(2)}) collective-permute-start(f32[10,1,1024]{2,1,0:T(1,128)S(1)} %shard_map.176.here_ref), channel_id=1, source_target_pairs={{16,32},{32,16},{48,64},{64,48},{80,96},{96,80},{112,128},{128,112... | collective-permute-start | bytes 122888 | tf_op jit(solution)/shard_map/ppermute | solution.py:599

commit v8 on v7

--- a/solution.py
+++ b/solution.py
@@ -408,7 +408,7 @@
     turns[...] = fixed_turns(data_ref[0:3, :])
     floor_value = SOFT_FLOOR + SOFT_SCALE * lam_ref[0]
 
-    def one_pair(k, carry):
+    def one_pair(k):
         start = pl.multiple_of(k * CLUSTER, CLUSTER)
         starts = [pl.multiple_of(k * (2 * CLUSTER), CLUSTER), pl.multiple_of(k * (2 * CLUSTER) + CLUSTER, CLUSTER)]
         owns = [own_rows(data_ref, turns, s) for s in starts]
@@ -430,14 +430,9 @@
                 force_ref[i : i + 1, lanes] = partial_ref[i : i + 1, lanes] + SPAN * jnp.sum(
                     totals[j][i], axis=0, keepdims=True
                 )
-        return carry
-
-    def two_pairs(k, carry):
-        for side in range(2):
-            one_pair(2 * k + side, carry)
-        return carry
-
-    lax.fori_loop(0, HALO // CLUSTER // 2, two_pairs, 0)
+
+    for k in range(HALO // CLUSTER):
+        one_pair(k)
 
 
 def rest_kernel(

time: 79.4 us -> 79.5 us (level)
  transfers between devices with their start and end apart: 10 -> 10, of which waited for: 4 -> 4; matrix products, arithmetic and copies ran while one was open for 0% -> 0% of each run, Pallas kernels for 25% -> 24%
where the time goes in v8:
time: 79.5 us; the launch traced here: 78.9 us
  starting transfers between devices  32.8 us (41%)
  Pallas kernels  30.4 us (38%)
  waiting for transfers between devices  13.5 us (17%)
  between operations  1.57 us (2%)
    pallas_call x12, Pallas kernels, call(): pl.pallas_call(kernel, out_shape=[jax.ShapeDtypeStruct(shape, dtype) for...  30.4 us
    all_to_all x2, starting transfers between devices, exchanged(): return lax.all_to_all(value, 'dom', split_axis=0, concat_axis=0, tiled=True)  15.9 us
    ppermute x2, starting transfers between devices, traded(): return lax.ppermute(state, 'lam', pairs)  7.96 us
    ppermute x3, starting transfers between devices, neighbours(): above = lax.ppermute(low, 'dom', [(i, (i - 1) % size) for i in range(size)])  7.67 us
    ppermute x2, waiting for transfers between devices, traded(): return lax.ppermute(state, 'lam', pairs)  7.14 us
    all_to_all x2, waiting for transfers between devices, exchanged(): return lax.all_to_all(value, 'dom', split_axis=0, concat_axis=0, tiled=True)  6.39 us
  transfers between devices with their start and end apart: 10, of which 4 were waited for; matrix products, arithmetic and copies ran while one was open for 0% of the time, Pallas kernels for 24%

profile of v8, /device:TPU:32, one launch (start us, length us, event | category | flops | bytes accessed | tf_op | source)
XLA Modules:
  0.0 78.9 jit_solution(3779727049725378937)
XLA Ops:
  1.3 2.7 %shard_map.166.grid_ref = f32[384,128]{1,0:T(8,128)} custom-call(f32[1]{0:T(128)S(6)} %copy.18.lam_ref, s32[3,1,1024]{2,1,0:T(1,128)} %bitcast.18, f32[3,1,1024]{2,1,0:T(1,128)} %bitcast.20, f32[1,1024]{1,0:T(1,128)} %bitcast.22, f32[1,1024]{1,0:T(1,128)} %bitcast.24, f32[32,32]{1,0:T(8,128)} %constant.10.clone.slab_hbm.slab_ref), custom_call_target="tpu_custom_call" | custom-call | bytes 200000 | tf_op jit(solution)/shard_map/pallas_call | solution.py:572
  4.0 0.0 copy-start.5
  4.0 0.0 copy-start.7
  4.0 10.6 %all-to-all-start = ((f32[16,24,128]{2,1,0:T(8,128)}), f32[16,24,128]{2,1,0:T(8,128)S(1)}, u32[]{:S(2)}, u32[]{:S(2)}) async-start(f32[16,24,128]{2,1,0:T(8,128)} %bitcast.15), calls=%async_computation | async-start | bytes 393216 | tf_op jit(solution)/shard_map/all_to_all | solution.py:598
  14.6 0.0 copy-start.4
  14.7 0.6 copy-done.4
  15.3 0.1 shard_map.167
  15.4 0.0 copy-start.14
  15.5 0.4 collective-permute-start
  15.9 2.5 %collective-permute-start.1 = (f32[8,512]{1,0:T(8,128)S(1)}, f32[8,512]{1,0:T(8,128)S(1)}, u32[]{:S(2)}, u32[]{:S(2)}) collective-permute-start(f32[8,512]{1,0:T(8,128)S(1)} %get-tuple-element.29), channel_id=1, source_target_pairs={{0,15},{1,0},{2,1},{3,2},{4,3},{5,4},{6,5},{7,6},{8,7},{9,8},{10,9... | collective-permute-start | bytes 49160 | tf_op jit(solution)/shard_map/ppermute | solution.py:586
  18.4 0.0 copy-start.1
  18.4 4.1 %shard_map.168 = (f32[8,1024]{1,0:T(8,128)S(1)}, f32[2,128,128]{2,1,0:T(8,128)S(1)}) custom-call(f32[1]{0:T(128)S(6)} %copy.18.lam_ref, s32[6,1,8]{2,1,0:T(1,128)S(1)} %bitcast.29, f32[17,65]{1,0:T(8,128)S(1)} %copy-done.13, f32[8,1024]{1,0:T(8,128)S(1)} %get-tuple-element.26.data_ref, f32[128,8]{1,0:T(8,128)S(1)} %copy-done.12, f32[8,128]{1,0:T(8,128)S(1)} %copy-done.14), custom_call_target="tpu_custom_call" | custom-call | flops 2000000000 | bytes 200000 | tf_op jit(solution)/shard_map/pallas_call | solution.py:572
  22.5 0.0 collective-permute-done.below_ref
  22.5 2.0 %all-to-all-done = f32[16,24,128]{2,1,0:T(8,128)S(1)} async-done(((f32[16,24,128]{2,1,0:T(8,128)}), f32[16,24,128]{2,1,0:T(8,128)S(1)}, u32[]{:S(2)}, u32[]{:S(2)}) %all-to-all-start) | async-done | bytes 196640 | tf_op jit(solution)/shard_map/all_to_all | solution.py:598
  24.6 1.5 %shard_map.169 = f32[384,128]{1,0:T(8,128)} custom-call(f32[384,128]{1,0:T(8,128)S(1)} %bitcast.17, f32[2,128,128]{2,1,0:T(8,128)S(1)} %get-tuple-element.27.gain_ref, bf16[512,128]{1,0:T(8,128)(2,1)S(1)} %copy-done.1, f32[8,512]{1,0:T(8,128)S(1)} %collective-permute-done.below_ref, f32[8,512]{1,0:T(8,128)S(1)} %collective-permute-done.1.above_ref), custom_call_target="tpu_custom_call" | custom-call | bytes 200000 | tf_op jit(solution)/shard_map/pallas_call | solution.py:572
  26.0 5.4 %all-to-all-start.1 = ((f32[16,24,128]{2,1,0:T(8,128)}), f32[16,24,128]{2,1,0:T(8,128)S(1)}, u32[]{:S(2)}, u32[]{:S(2)}) async-start(f32[16,24,128]{2,1,0:T(8,128)} %bitcast.10), calls=%async_computation.1 | async-start | bytes 393216 | tf_op jit(solution)/shard_map/all_to_all | solution.py:598
  31.4 5.6 %shard_map.170 = (f32[8,1024]{1,0:T(8,128)S(1)}, bf16[128,2048]{1,0:T(8,128)(2,1)S(1)}, bf16[128,2048]{1,0:T(8,128)(2,1)S(1)}, f32[64,1024]{1,0:T(8,128)S(1)}, f32[32,1024]{1,0:T(8,128)S(1)}) custom-call(f32[1]{0:T(128)S(6)} %copy.18.lam_ref, s32[6,1,8]{2,1,0:T(1,128)S(1)} %bitcast.30, f32[8,1024]{1,0:T(8,128)S(1)} %get-tuple-element.26.data_ref, ...), custom_call_target="tpu_custom_call" | custom-call | flops 2000000000 | bytes 200000 | tf_op jit(solution)/shard_map/pallas_call | solution.py:572
  37.0 4.4 %all-to-all-done.1 = f32[16,24,128]{2,1,0:T(8,128)S(1)} async-done(((f32[16,24,128]{2,1,0:T(8,128)}), f32[16,24,128]{2,1,0:T(8,128)S(1)}, u32[]{:S(2)}, u32[]{:S(2)}) %all-to-all-start.1) | async-done | bytes 196640 | tf_op jit(solution)/shard_map/all_to_all | solution.py:598
  41.3 1.5 %shard_map.171 = (f32[8,1024]{1,0:T(8,128)S(1)}, f32[8,1024]{1,0:T(8,128)S(1)}, f32[16,1024]{1,0:T(8,128)S(1)}, f32[8,512]{1,0:T(8,128)S(1)}, f32[8,512]{1,0:T(8,128)S(1)}) custom-call(f32[384,128]{1,0:T(8,128)S(1)} %bitcast.16, f32[8,1024]{1,0:T(8,128)S(1)} %get-tuple-element.26.data_ref, f32[16,1024]{1,0:T(8,128)S(1)} %get-tuple-element.30.move_ref, ...), custom_call_target="tpu_custom_call" | custom-call | bytes 200000 | tf_op jit(solution)/shard_map/pallas_call | solution.py:572
  42.8 0.8 %collective-permute-start.2 = (f32[8,512]{1,0:T(8,128)S(1)}, f32[8,512]{1,0:T(8,128)S(1)}, u32[]{:S(2)}, u32[]{:S(2)}) collective-permute-start(f32[8,512]{1,0:T(8,128)S(1)} %get-tuple-element.38), channel_id=1, source_target_pairs={{0,1},{1,2},{2,3},{3,4},{4,5},{5,6},{6,7},{7,8},{8,9},{9,10},{10,1... | collective-permute-start | bytes 49160 | tf_op jit(solution)/shard_map/ppermute | solution.py:585
  43.6 2.2 %collective-permute-start.3 = (f32[8,512]{1,0:T(8,128)S(1)}, f32[8,512]{1,0:T(8,128)S(1)}, u32[]{:S(2)}, u32[]{:S(2)}) collective-permute-start(f32[8,512]{1,0:T(8,128)S(1)} %get-tuple-element.39), channel_id=1, source_target_pairs={{0,15},{1,0},{2,1},{3,2},{4,3},{5,4},{6,5},{7,6},{8,7},{9,8},{10,9... | collective-permute-start | bytes 49160 | tf_op jit(solution)/shard_map/ppermute | solution.py:586
  45.8 4.6 %shard_map.172.partial_ref = f32[8,1024]{1,0:T(8,128)S(1)} custom-call(f32[1]{0:T(128)S(6)} %copy.18.lam_ref, s32[6,1,8]{2,1,0:T(1,128)S(1)} %bitcast.31, f32[8,1024]{1,0:T(8,128)S(1)} %get-tuple-element.37.data_ref), custom_call_target="tpu_custom_call" | custom-call | flops 2000000000 | bytes 200000 | tf_op jit(solution)/shard_map/pallas_call | solution.py:572
  50.4 2.5 %shard_map.173 = (f32[8,1024]{1,0:T(8,128)S(1)}, f32[16,1024]{1,0:T(8,128)S(1)}, f32[8,512]{1,0:T(8,128)S(1)}, f32[8,512]{1,0:T(8,128)S(1)}) custom-call(f32[1]{0:T(128)S(6)} %copy.18.lam_ref, f32[8,1024]{1,0:T(8,128)S(1)} %get-tuple-element.37.data_ref, f32[8,512]{1,0:T(8,128)S(1)} %collective-permute-done.2.below_ref, ...), custom_call_target="tpu_custom_call" | custom-call | bytes 200000 | tf_op jit(solution)/shard_map/pallas_call | solution.py:572
  52.9 0.0 collective-permute-start.4
  53.0 2.9 %collective-permute-start.5 = (f32[8,512]{1,0:T(8,128)S(1)}, f32[8,512]{1,0:T(8,128)S(1)}, u32[]{:S(2)}, u32[]{:S(2)}) collective-permute-start(f32[8,512]{1,0:T(8,128)S(1)} %get-tuple-element.44), channel_id=1, source_target_pairs={{0,15},{1,0},{2,1},{3,2},{4,3},{5,4},{6,5},{7,6},{8,7},{9,8},{10,9... | collective-permute-start | bytes 49160 | tf_op jit(solution)/shard_map/ppermute | solution.py:586
  55.9 4.9 %shard_map.174.partial_ref = f32[8,1024]{1,0:T(8,128)S(1)} custom-call(f32[1]{0:T(128)S(6)} %copy.18.lam_ref, s32[6,1,8]{2,1,0:T(1,128)S(1)} %bitcast.32, f32[8,1024]{1,0:T(8,128)S(1)} %get-tuple-element.42.data_ref), custom_call_target="tpu_custom_call" | custom-call | flops 2000000000 | bytes 200000 | tf_op jit(solution)/shard_map/pallas_call | solution.py:572
  60.8 2.4 %shard_map.175.here_ref = f32[10,1,1024]{2,1,0:T(1,128)S(1)} custom-call(f32[1]{0:T(128)S(6)} %copy.18.lam_ref, f32[8,1024]{1,0:T(8,128)S(1)} %get-tuple-element.42.data_ref, f32[8,512]{1,0:T(8,128)S(1)} %collective-permute-done.4.below_ref, f32[8,512]{1,0:T(8,128)S(1)} %collective-permute-done.5.above_ref, f32[8,1024]{1,0:T(8,128)S(1)} %shard_map.174.partial_ref, ...), custom_call_target="tpu_custom_call" | custom-call | bytes 200000 | tf_op jit(solution)/shard_map/pallas_call | solution.py:572
  63.2 3.4 %collective-permute-start.6 = (f32[10,1,1024]{2,1,0:T(1,128)S(1)}, f32[10,1,1024]{2,1,0:T(1,128)S(1)}, u32[]{:S(2)}, u32[]{:S(2)}) collective-permute-start(f32[10,1,1024]{2,1,0:T(1,128)S(1)} %shard_map.175.here_ref), channel_id=1, source_target_pairs={{0,16},{16,0},{32,48},{48,32},{64,80},{80,64},{96,112},{112,96},{1... | collective-permute-start | bytes 122888 | tf_op jit(solution)/shard_map/ppermute | solution.py:594
  66.6 2.5 %collective-permute-done.6.there_ref = f32[10,1,1024]{2,1,0:T(1,128)S(1)} collective-permute-done((f32[10,1,1024]{2,1,0:T(1,128)S(1)}, f32[10,1,1024]{2,1,0:T(1,128)S(1)}, u32[]{:S(2)}, u32[]{:S(2)}) %collective-permute-start.6) | collective-permute-done | bytes 40992 | tf_op jit(solution)/shard_map/ppermute | solution.py:594
  69.1 4.6 %collective-permute-start.7 = (f32[10,1,1024]{2,1,0:T(1,128)S(1)}, f32[10,1,1024]{2,1,0:T(1,128)S(1)}, u32[]{:S(2)}, u32[]{:S(2)}) collective-permute-start(f32[10,1,1024]{2,1,0:T(1,128)S(1)} %shard_map.176.here_ref), channel_id=1, source_target_pairs={{16,32},{32,16},{48,64},{64,48},{80,96},{96,80},{112,128},{128,112... | collective-permute-start | bytes 122888 | tf_op jit(solution)/shard_map/ppermute | solution.py:594
  73.6 4.7 %collective-permute-done.7.there_ref = f32[10,1,1024]{2,1,0:T(1,128)S(1)} collective-permute-done((f32[10,1,1024]{2,1,0:T(1,128)S(1)}, f32[10,1,1024]{2,1,0:T(1,128)S(1)}, u32[]{:S(2)}, u32[]{:S(2)}) %collective-permute-start.7) | collective-permute-done | bytes 40992 | tf_op jit(solution)/shard_map/ppermute | solution.py:594
  78.3 0.6 shard_map.177
  (30 shorter events, 0.1 us)
Async XLA Ops:
  4.0 10.7 %copy-start = (f32[384,128]{1,0:T(8,128)S(1)}, f32[384,128]{1,0:T(8,128)}, u32[]{:S(2)}) copy-start(f32[384,128]{1,0:T(8,128)} %shard_map.166.grid_ref) | copy-start | bytes 589828
  4.0 10.7 %copy-start.2 = (s32[1,3,1024]{2,0,1:T(1,128)S(1)}, s32[1,3,1024]{2,0,1:T(1,128)}, u32[]{:S(2)}) copy-start(s32[1,3,1024]{2,0,1:T(1,128)} %param.15) | copy-start | bytes 36868
  4.0 10.7 %copy-start.3 = (f32[1,3,1024]{2,0,1:T(1,128)S(1)}, f32[1,3,1024]{2,0,1:T(1,128)}, u32[]{:S(2)}) copy-start(f32[1,3,1024]{2,0,1:T(1,128)} %param.16) | copy-start | bytes 36868
  4.0 10.7 %copy-start.5 = (f32[1024]{0:T(1024)S(1)}, f32[1024]{0:T(1024)}, u32[]{:S(2)}) copy-start(f32[1024]{0:T(1024)} %param.19) | copy-start | bytes 12292
  4.0 10.7 %copy-start.7 = (f32[1,3,1024]{2,0,1:T(1,128)S(1)}, f32[1,3,1024]{2,0,1:T(1,128)}, u32[]{:S(2)}) copy-start(f32[1,3,1024]{2,0,1:T(1,128)} %param.17) | copy-start | bytes 36868
  4.0 10.7 %copy-start.8 = (f32[1024]{0:T(1024)S(1)}, f32[1024]{0:T(1024)}, u32[]{:S(2)}) copy-start(f32[1024]{0:T(1024)} %param.20) | copy-start | bytes 12292
  4.0 10.7 %copy-start.9 = (s32[1,2,512]{2,1,0:T(2,128)S(1)}, s32[1,2,512]{2,1,0:T(2,128)}, u32[]{:S(2)}) copy-start(s32[1,2,512]{2,1,0:T(2,128)} %lists_ref.1) | copy-start | bytes 12292
  4.0 20.5 %all-to-all-start = ((f32[16,24,128]{2,1,0:T(8,128)}), f32[16,24,128]{2,1,0:T(8,128)S(1)}, u32[]{:S(2)}, u32[]{:S(2)}) async-start(f32[16,24,128]{2,1,0:T(8,128)} %bitcast.15), calls=%async_computation | async-start | bytes 393216 | tf_op jit(solution)/shard_map/all_to_all | solution.py:598
  14.6 0.7 copy-start.4
  14.6 0.7 copy-start.10
  15.3 3.1 %copy-start.12 = (f32[128,8]{1,0:T(8,128)S(1)}, f32[128,8]{1,0:T(8,128)}, u32[]{:S(2)}) copy-start(f32[128,8]{1,0:T(8,128)} %constant.12.clone.rows_ref) | copy-start | bytes 12292
  15.3 3.1 %copy-start.13 = (f32[17,65]{1,0:T(8,128)S(1)}, f32[17,65]{1,0:T(8,128)}, u32[]{:S(2)}) copy-start(f32[17,65]{1,0:T(8,128)} %constant.11.clone.weights_ref) | copy-start | bytes 13264
  15.4 3.0 %copy-start.14 = (f32[8,128]{1,0:T(8,128)S(1)}, f32[8,128]{1,0:T(8,128)}, u32[]{:S(2)}) copy-start(f32[8,128]{1,0:T(8,128)} %constant.13.clone.lanes_ref) | copy-start | bytes 12292
  15.4 3.0 %copy-start.11 = (s32[1,8,6]{1,0,2:T(1,128)S(1)}, s32[1,8,6]{1,0,2:T(1,128)}, u32[]{:S(2)}) copy-start(s32[1,8,6]{1,0,2:T(1,128)} %param.22) | copy-start | bytes 580
  15.5 7.1 %collective-permute-start = (f32[8,512]{1,0:T(8,128)S(1)}, f32[8,512]{1,0:T(8,128)S(1)}, u32[]{:S(2)}, u32[]{:S(2)}) collective-permute-start(f32[8,512]{1,0:T(8,128)S(1)} %get-tuple-element.28), channel_id=1, source_target_pairs={{0,1},{1,2},{2,3},{3,4},{4,5},{5,6},{6,7},{7,8},{8,9},{9,10},{10,1... | collective-permute-start | bytes 49160 | tf_op jit(solution)/shard_map/ppermute | solution.py:585
  15.9 6.7 %collective-permute-start.1 = (f32[8,512]{1,0:T(8,128)S(1)}, f32[8,512]{1,0:T(8,128)S(1)}, u32[]{:S(2)}, u32[]{:S(2)}) collective-permute-start(f32[8,512]{1,0:T(8,128)S(1)} %get-tuple-element.29), channel_id=1, source_target_pairs={{0,15},{1,0},{2,1},{3,2},{4,3},{5,4},{6,5},{7,6},{8,7},{9,8},{10,9... | collective-permute-start | bytes 49160 | tf_op jit(solution)/shard_map/ppermute | solution.py:586
  18.4 6.1 %copy-start.1 = (bf16[512,128]{1,0:T(8,128)(2,1)S(1)}, bf16[512,128]{1,0:T(8,128)(2,1)}, u32[]{:S(2)}) copy-start(bf16[512,128]{1,0:T(8,128)(2,1)} %constant.14.clone.basis_ref) | copy-start | bytes 393220
  26.0 5.4 %copy-start.6 = (f32[32,32]{1,0:T(8,128)S(1)}, f32[32,32]{1,0:T(8,128)}, u32[]{:S(2)}) copy-start(f32[32,32]{1,0:T(8,128)} %constant.10.clone.slab_hbm.slab_ref) | copy-start | bytes 12292
  26.0 15.3 %all-to-all-start.1 = ((f32[16,24,128]{2,1,0:T(8,128)}), f32[16,24,128]{2,1,0:T(8,128)S(1)}, u32[]{:S(2)}, u32[]{:S(2)}) async-start(f32[16,24,128]{2,1,0:T(8,128)} %bitcast.10), calls=%async_computation.1 | async-start | bytes 393216 | tf_op jit(solution)/shard_map/all_to_all | solution.py:598
  42.8 7.6 %collective-permute-start.2 = (f32[8,512]{1,0:T(8,128)S(1)}, f32[8,512]{1,0:T(8,128)S(1)}, u32[]{:S(2)}, u32[]{:S(2)}) collective-permute-start(f32[8,512]{1,0:T(8,128)S(1)} %get-tuple-element.38), channel_id=1, source_target_pairs={{0,1},{1,2},{2,3},{3,4},{4,5},{5,6},{6,7},{7,8},{8,9},{9,10},{10,1... | collective-permute-start | bytes 49160 | tf_op jit(solution)/shard_map/ppermute | solution.py:585
  43.6 6.8 %collective-permute-start.3 = (f32[8,512]{1,0:T(8,128)S(1)}, f32[8,512]{1,0:T(8,128)S(1)}, u32[]{:S(2)}, u32[]{:S(2)}) collective-permute-start(f32[8,512]{1,0:T(8,128)S(1)} %get-tuple-element.39), channel_id=1, source_target_pairs={{0,15},{1,0},{2,1},{3,2},{4,3},{5,4},{6,5},{7,6},{8,7},{9,8},{10,9... | collective-permute-start | bytes 49160 | tf_op jit(solution)/shard_map/ppermute | solution.py:586
  52.9 7.8 %collective-permute-start.4 = (f32[8,512]{1,0:T(8,128)S(1)}, f32[8,512]{1,0:T(8,128)S(1)}, u32[]{:S(2)}, u32[]{:S(2)}) collective-permute-start(f32[8,512]{1,0:T(8,128)S(1)} %get-tuple-element.43), channel_id=1, source_target_pairs={{0,1},{1,2},{2,3},{3,4},{4,5},{5,6},{6,7},{7,8},{8,9},{9,10},{10,1... | collective-permute-start | bytes 49160 | tf_op jit(solution)/shard_map/ppermute | solution.py:585
  53.0 7.8 %collective-permute-start.5 = (f32[8,512]{1,0:T(8,128)S(1)}, f32[8,512]{1,0:T(8,128)S(1)}, u32[]{:S(2)}, u32[]{:S(2)}) collective-permute-start(f32[8,512]{1,0:T(8,128)S(1)} %get-tuple-element.44), channel_id=1, source_target_pairs={{0,15},{1,0},{2,1},{3,2},{4,3},{5,4},{6,5},{7,6},{8,7},{9,8},{10,9... | collective-permute-start | bytes 49160 | tf_op jit(solution)/shard_map/ppermute | solution.py:586
  63.2 5.9 %collective-permute-start.6 = (f32[10,1,1024]{2,1,0:T(1,128)S(1)}, f32[10,1,1024]{2,1,0:T(1,128)S(1)}, u32[]{:S(2)}, u32[]{:S(2)}) collective-permute-start(f32[10,1,1024]{2,1,0:T(1,128)S(1)} %shard_map.175.here_ref), channel_id=1, source_target_pairs={{0,16},{16,0},{32,48},{48,32},{64,80},{80,64},{96,112},{112,96},{1... | collective-permute-start | bytes 122888 | tf_op jit(solution)/shard_map/ppermute | solution.py:594
  69.1 9.2 %collective-permute-start.7 = (f32[10,1,1024]{2,1,0:T(1,128)S(1)}, f32[10,1,1024]{2,1,0:T(1,128)S(1)}, u32[]{:S(2)}, u32[]{:S(2)}) collective-permute-start(f32[10,1,1024]{2,1,0:T(1,128)S(1)} %shard_map.176.here_ref), channel_id=1, source_target_pairs={{16,32},{32,16},{48,64},{64,48},{80,96},{96,80},{112,128},{128,112... | collective-permute-start | bytes 122888 | tf_op jit(solution)/shard_map/ppermute | solution.py:594
